TPU v7x, 32 devices: a whole 2x2x4 slice. The times are simulated.
32 devices in a mesh: batch: 4 (over y, core), blk: 8 (over z, x).
Axes of the slice: x: 2, y: 2, z: 4, core: 2. Of those that a mesh axis runs over, the one named last changes fastest.
Arguments:
- tokens: bfloat16 [32, 1024, 1024], P('batch', 'blk'), may hold values from -6 to 6
- cotangent: bfloat16 [32, 1024, 1024], P('batch', 'blk'), may hold values from -6 to 6
- w_query: bfloat16 [1024, 1024], replicated, may hold values from -0.1875 to 0.1875
- w_key: bfloat16 [1024, 1024], replicated, may hold values from -0.1875 to 0.1875
- w_value: bfloat16 [1024, 1024], replicated, may hold values from -0.1875 to 0.1875
- w_gate: bfloat16 [1024, 1024], replicated, may hold values from -0.1875 to 0.1875
- w_out: bfloat16 [1024, 1024], replicated, may hold values from -0.375 to 0.375
- out_gain: float32 [1024], replicated, may hold values from 0.1 to 1.9
- w_first: bfloat16 [1024, 2816], replicated, may hold values from -0.1875 to 0.1875
- w_second: bfloat16 [1024, 2816], replicated, may hold values from -0.1875 to 0.1875
- w_third: bfloat16 [2816, 1024], replicated, may hold values from -0.109375 to 0.109375
Outputs:
- output: bfloat16 [32, 1024, 1024], P('batch', 'blk')
- grad_tokens: float32 [32, 1024, 1024], P('batch', 'blk')
- grad_query: float32 [1024, 1024], P('blk')
- grad_key: float32 [1024, 1024], P('blk')
- grad_value: float32 [1024, 1024], P('blk')
- grad_gate: float32 [1024, 1024], P('blk')
- grad_out: float32 [1024, 1024], P('blk')
- grad_gain: float32 [1024], P('blk')
- grad_first: float32 [1024, 2816], P('blk')
- grad_second: float32 [1024, 2816], P('blk')
- grad_third: float32 [2816, 1024], P('blk')
All inputs are finite; a program needn't handle non-finite values.
Results may differ from a plain program's by a relative error of at most 0.014.
Values sent between devices are 32-bit elements; how exact they have to be, the bound alone decides.
A program may use at most 384 MiB of HBM per device.

v0:
```python
import jax
import jax.numpy as jnp
from jax import lax
from jax.sharding import PartitionSpec as P

HEADS = 16
HEAD = 64


EPS = 1e-06


def entering(x, axis, combine, identity, reverse):
    peers, here = (lax.axis_size(axis), lax.axis_index(axis))
    everything = lax.all_gather(x, axis)
    start = jnp.broadcast_to(jnp.asarray(identity, x.dtype), x.shape)

    def step(k, before):
        at = peers - 1 - k if reverse else k
        reached = at > here if reverse else at < here
        new = combine(before, everything[at])
        return jnp.where(reached, new, before)

    return lax.fori_loop(0, peers, step, start)


def silu_parts(pre):
    sig = jax.nn.sigmoid(pre)
    return (pre * sig, sig * (1.0 + pre * (1.0 - sig)))


def norm_back(grad, value, scale):
    inner = jnp.mean(grad * value, axis=-1, keepdims=True)
    return scale * grad - value * (scale * scale * scale) * inner


def project(left, weight):
    return jnp.dot(left, weight, preferred_element_type=jnp.float32)


def weight_grad(left, right):
    return jnp.einsum("td,tf->df", left, right, preferred_element_type=jnp.float32)


def back_project(grad, weight):
    return jnp.einsum("tf,df->td", grad, weight, preferred_element_type=jnp.float32)


def add_terms(earlier, later):
    return earlier + later


def body(
    tokens, cotangent, w_query, w_key, w_value, w_gate, w_out, out_gain, w_first, w_second, w_third
):
    seqs, span, width = tokens.shape
    rows = seqs * span
    xf = tokens.reshape(rows, width).astype(jnp.float32)
    rone = lax.rsqrt(jnp.mean(xf * xf, axis=-1, keepdims=True) + EPS)
    normed = (xf * rone).astype(jnp.bfloat16)
    query = project(normed, w_query)
    key = project(normed, w_key)
    value = project(normed, w_value)
    gate = project(normed, w_gate)
    fquery, query_der = silu_parts(query)
    fkey, key_der = silu_parts(key)
    shape4 = (seqs, span, HEADS, HEAD)
    qfour = fquery.astype(jnp.bfloat16).reshape(shape4)
    kfour = fkey.astype(jnp.bfloat16).reshape(shape4)
    vfour = value.astype(jnp.bfloat16).reshape(shape4)
    causal = (jnp.arange(span)[:, None] >= jnp.arange(span)[None, :]).astype(jnp.float32)
    scores = (
        jnp.einsum("sthe,suhe->shtu", qfour, kfour, preferred_element_type=jnp.float32) * causal
    )
    scores_low = scores.astype(jnp.bfloat16)
    intra = jnp.einsum("shtu,suhf->sthf", scores_low, vfour, preferred_element_type=jnp.float32)
    local_state = jnp.einsum("sthe,sthf->shef", kfour, vfour, preferred_element_type=jnp.float32)
    empty = jnp.zeros_like(local_state)
    prefix = entering(local_state, "blk", add_terms, empty, False)
    prefix_low = prefix.astype(jnp.bfloat16)
    inter = jnp.einsum("sthe,shef->sthf", qfour, prefix_low, preferred_element_type=jnp.float32)
    attn = (intra + inter).reshape(rows, width)
    rattn = lax.rsqrt(jnp.mean(attn * attn, axis=-1, keepdims=True) + EPS)
    unit_attn = attn * rattn
    scaled = unit_attn * out_gain
    gate_act, gate_der = silu_parts(gate)
    mixed = (scaled * gate_act).astype(jnp.bfloat16)
    resid = xf + project(mixed, w_out)
    rtwo = lax.rsqrt(jnp.mean(resid * resid, axis=-1, keepdims=True) + EPS)
    normed2 = (resid * rtwo).astype(jnp.bfloat16)
    first = project(normed2, w_first)
    second = project(normed2, w_second)
    inner = (first * second).astype(jnp.bfloat16)
    output = (resid + project(inner, w_third)).astype(jnp.bfloat16)
    grad_top = cotangent.reshape(rows, width)
    grad_w3 = weight_grad(inner, grad_top)
    grad_inner = back_project(grad_top, w_third)
    grad_one = (grad_inner * second).astype(jnp.bfloat16)
    grad_two = (grad_inner * first).astype(jnp.bfloat16)
    grad_w1 = weight_grad(normed2, grad_one)
    grad_w2 = weight_grad(normed2, grad_two)
    grad_normed2 = back_project(grad_one, w_first) + back_project(grad_two, w_second)
    grad_resid = grad_top.astype(jnp.float32) + norm_back(grad_normed2, resid, rtwo)
    grad_resid_low = grad_resid.astype(jnp.bfloat16)
    grad_wo = weight_grad(mixed, grad_resid_low)
    grad_mixed = back_project(grad_resid_low, w_out)
    grad_scaled = grad_mixed * gate_act
    grad_gate_low = (grad_mixed * scaled * gate_der).astype(jnp.bfloat16)
    grad_gain_local = jnp.sum(grad_scaled * unit_attn, axis=0)
    grad_attn = norm_back(grad_scaled * out_gain, attn, rattn)
    gafour = grad_attn.astype(jnp.bfloat16).reshape(shape4)
    grad_scores = (
        jnp.einsum("sthf,suhf->shtu", gafour, vfour, preferred_element_type=jnp.float32) * causal
    ).astype(jnp.bfloat16)
    grad_prefix_local = jnp.einsum(
        "sthe,sthf->shef", qfour, gafour, preferred_element_type=jnp.float32
    )
    grad_state = entering(grad_prefix_local, "blk", add_terms, empty, True)
    grad_state_low = grad_state.astype(jnp.bfloat16)
    grad_fq = jnp.einsum("shtu,suhe->sthe", grad_scores, kfour, preferred_element_type=jnp.float32)
    grad_fq = grad_fq + jnp.einsum(
        "sthf,shef->sthe", gafour, prefix_low, preferred_element_type=jnp.float32
    )
    grad_fk = jnp.einsum("shtu,sthe->suhe", grad_scores, qfour, preferred_element_type=jnp.float32)
    grad_fk = grad_fk + jnp.einsum(
        "sthf,shef->sthe", vfour, grad_state_low, preferred_element_type=jnp.float32
    )
    grad_vv = jnp.einsum("shtu,sthf->suhf", scores_low, gafour, preferred_element_type=jnp.float32)
    grad_vv = grad_vv + jnp.einsum(
        "sthe,shef->sthf", kfour, grad_state_low, preferred_element_type=jnp.float32
    )
    grad_query_low = (grad_fq.reshape(rows, width) * query_der).astype(jnp.bfloat16)
    grad_key_low = (grad_fk.reshape(rows, width) * key_der).astype(jnp.bfloat16)
    grad_value_low = grad_vv.reshape(rows, width).astype(jnp.bfloat16)
    grad_wq = weight_grad(normed, grad_query_low)
    grad_wk = weight_grad(normed, grad_key_low)
    grad_wv = weight_grad(normed, grad_value_low)
    grad_wg = weight_grad(normed, grad_gate_low)
    grad_normed = back_project(grad_query_low, w_query) + back_project(grad_key_low, w_key)
    grad_normed = (
        grad_normed + back_project(grad_value_low, w_value) + back_project(grad_gate_low, w_gate)
    )
    grad_input = grad_resid + norm_back(grad_normed, xf, rone)
    sq, sk, sv, sg, so, sgain, sthree, sone, stwo = (
        lax.psum_scatter(grad_wq, "blk", scatter_dimension=0, tiled=True),
        lax.psum_scatter(grad_wk, "blk", scatter_dimension=0, tiled=True),
        lax.psum_scatter(grad_wv, "blk", scatter_dimension=0, tiled=True),
        lax.psum_scatter(grad_wg, "blk", scatter_dimension=0, tiled=True),
        lax.psum_scatter(grad_wo, "blk", scatter_dimension=0, tiled=True),
        lax.psum_scatter(grad_gain_local, "blk", scatter_dimension=0, tiled=True),
        lax.psum_scatter(grad_w3, "blk", scatter_dimension=0, tiled=True),
        lax.psum_scatter(grad_w1, "blk", scatter_dimension=0, tiled=True),
        lax.psum_scatter(grad_w2, "blk", scatter_dimension=0, tiled=True),
    )
    sq, sk, sv, sg, so, sgain, sthree, sone, stwo = lax.psum(
        (sq, sk, sv, sg, so, sgain, sthree, sone, stwo), "batch"
    )
    grad_tokens = grad_input.reshape(seqs, span, width)
    return (
        output.reshape(seqs, span, width),
        grad_tokens,
        sq,
        sk,
        sv,
        sg,
        so,
        sgain,
        sone,
        stwo,
        sthree,
    )


def solution(mesh):
    placed = (
        P("batch", "blk", None),
        P("batch", "blk", None),
        P(),
        P(),
        P(),
        P(),
        P(),
        P(),
        P(),
        P(),
        P(),
    )
    return jax.shard_map(
        body,
        mesh=mesh,
        in_specs=placed,
        out_specs=(
            P("batch", "blk", None),
            P("batch", "blk", None),
            P("blk", None),
            P("blk", None),
            P("blk", None),
            P("blk", None),
            P("blk", None),
            P("blk"),
            P("blk", None),
            P("blk", None),
            P("blk", None),
        ),
        check_vma=False,
    )
```

profile of v0, /device:TPU:0, one launch (start us, length us, event | category | flops | bytes accessed | tf_op | source)
XLA Modules:
  0.0 2704.3 jit_solution(13242400342458577844)
XLA Ops:
  86.5 609.2 %all-gather.5.cloned.1.call-done = f32[64,16,64,64]{3,2,1,0:T(8,128)} async-done(((f32[8,16,64,64]{3,2,1,0:T(8,128)}), f32[64,16,64,64]{3,2,1,0:T(8,128)}) %all-gather.5.cloned.1.call-update) | async-done | bytes 16777232 | tf_op jit(solution)/shard_map/all_gather | solution.py:15
  695.6 54.9 %while.30 = (s32[]{:T(128)}, f32[8,16,64,64]{3,2,1,0:T(8,128)}, s32[]{:T(128)}, f32[8,8,16,64,64]{4,3,2,1,0:T(8,128)}, s32[]{:T(128)}, /*index=5*/s32[]{:T(128)}) while((s32[]{:T(128)}, f32[8,16,64,64]{3,2,1,0:T(8,128)}, s32[]{:T(128)}, f32[8,8,16,64,64]{4,3,2,1,0:T(8,128)}, s32[]{:T(128)}, /*index=5*/s32[]{:T(128)}) %tuple.116), condition=%wide.region_2.3_spmd.clone, body=%wide.region_1.2_spmd.clone.sunk | while | flops 1572868 | bytes 6291557 | solution.py:24
  764.9 7.8 reshape.173
  772.7 8.4 multiply_convert_fusion.9
  786.0 8.8 fusion.29
  794.9 8.8 fusion.28
  803.7 18.1 multiply_convert_fusion
  821.7 10.2 fusion.30
  832.0 8.5 multiply_reduce_fusion.2
  917.6 11.8 fusion.41
  929.5 11.9 fusion.40
  941.4 12.0 fusion.42
  960.9 544.2 %all-gather.7.cloned.1.call-done = f32[64,16,64,64]{3,2,1,0:T(8,128)} async-done(((f32[8,16,64,64]{3,2,1,0:T(8,128)}), f32[64,16,64,64]{3,2,1,0:T(8,128)}) %all-gather.7.cloned.1.call-update) | async-done | bytes 16777232 | tf_op jit(solution)/shard_map/all_gather | solution.py:15
  1505.1 55.0 %while.31 = (s32[]{:T(128)}, f32[8,16,64,64]{3,2,1,0:T(8,128)}, s32[]{:T(128)}, f32[8,8,16,64,64]{4,3,2,1,0:T(8,128)}, s32[]{:T(128)}, /*index=5*/s32[]{:T(128)}, s32[]{:T(128)}, s32[]{:T(128)}) while((s32[]{:T(128)}, f32[8,16,64,64]{3,2,1,0:T(8,128)}, s32[]{:T(128)}, f32[8,8,16,64,64]{4,3,2,1,0:T(8,128)}, s32[]{:T(128)}, ...), condition=%wide.region_8.9_spmd.clone, body=%wide.region_7.8_spmd.clone.sunk | while | flops 1572872 | bytes 6291619 | solution.py:24
  1607.2 20.7 all-reduce
  1634.8 11.5 add_convert_fusion.1
  1646.3 42.4 %reduce-scatter.9.cloned.1.call-done = f32[128,1024]{1,0:T(8,128)} async-done(((f32[1024,1024]{1,0:T(8,128)}), f32[128,1024]{1,0:T(8,128)}) %reduce-scatter.9.cloned.1.call-update) | async-done | bytes 524304 | tf_op jit(solution)/shard_map/reduce_scatter | solution.py:145
  1688.8 91.2 %reduce-scatter.15.cloned.1.call-done = f32[128,1024]{1,0:T(8,128)} async-done(((f32[1024,1024]{1,0:T(8,128)}), f32[128,1024]{1,0:T(8,128)}) %reduce-scatter.15.cloned.1.call-update) | async-done | bytes 524304 | tf_op jit(solution)/shard_map/reduce_scatter | solution.py:148
  1779.9 196.3 %reduce-scatter.21.cloned.1.call-done = f32[128,2816]{1,0:T(8,128)} async-done(((f32[1024,2816]{1,0:T(8,128)}), f32[128,2816]{1,0:T(8,128)}) %reduce-scatter.21.cloned.1.call-update) | async-done | bytes 1441808 | tf_op jit(solution)/shard_map/reduce_scatter | solution.py:153
  1976.3 195.8 %reduce-scatter.19.cloned.1.call-done = f32[128,2816]{1,0:T(8,128)} async-done(((f32[1024,2816]{1,0:T(8,128)}), f32[128,2816]{1,0:T(8,128)}) %reduce-scatter.19.cloned.1.call-update) | async-done | bytes 1441808 | tf_op jit(solution)/shard_map/reduce_scatter | solution.py:152
  2172.1 195.8 %reduce-scatter.23.cloned.1.call-done = f32[352,1024]{1,0:T(8,128)} async-done(((f32[2816,1024]{1,0:T(8,128)}), f32[352,1024]{1,0:T(8,128)}) %reduce-scatter.23.cloned.1.call-update) | async-done | bytes 1441808 | tf_op jit(solution)/shard_map/reduce_scatter | solution.py:151
  2367.9 91.1 %reduce-scatter.13.cloned.1.call-done = f32[128,1024]{1,0:T(8,128)} async-done(((f32[1024,1024]{1,0:T(8,128)}), f32[128,1024]{1,0:T(8,128)}) %reduce-scatter.13.cloned.1.call-update) | async-done | bytes 524304 | tf_op jit(solution)/shard_map/reduce_scatter | solution.py:147
  2459.0 91.9 %reduce-scatter.11.cloned.1.call-done = f32[128,1024]{1,0:T(8,128)} async-done(((f32[1024,1024]{1,0:T(8,128)}), f32[128,1024]{1,0:T(8,128)}) %reduce-scatter.11.cloned.1.call-update) | async-done | bytes 524304 | tf_op jit(solution)/shard_map/reduce_scatter | solution.py:146
  2567.3 118.1 %all-reduce.4.cloned.1.call-done = (f32[128,1024]{1,0:T(8,128)}, f32[128,1024]{1,0:T(8,128)}, f32[128,1024]{1,0:T(8,128)}, f32[128,1024]{1,0:T(8,128)}, f32[128,...) async-done(((f32[128,1024]{1,0:T(8,128)}, f32[128,1024]{1,0:T(8,128)}, f32[128,1024]{1,0:T(8,128)}, f32[128,1024]{1,0:T(8,128)}, ...) | async-done | bytes 6946832 | tf_op jit(solution)/shard_map/psum | solution.py:155
  (220 shorter events, 374.1 us)
Async XLA Ops:
  7.2 774.0 %copy-start = (bf16[1024,1024]{1,0:T(8,128)(2,1)S(1)}, bf16[1024,1024]{1,0:T(8,128)(2,1)}, u32[]{:S(2)}) copy-start(bf16[1024,1024]{1,0:T(8,128)(2,1)} %param.21) | copy-start | bytes 6291460
  7.2 688.4 %all-gather.5.cloned.1.call-start = ((), (), s32[]{:S(2)}) async-start(), calls=%async_computation.16 | async-start | bytes 37748736 | tf_op jit(solution)/shard_map/all_gather | solution.py:15
  55.1 1450.1 %all-gather.7.cloned.1.call-start = ((), (), s32[]{:S(2)}) async-start(), calls=%async_computation.17 | async-start | bytes 37748736 | tf_op jit(solution)/shard_map/all_gather | solution.py:15
  772.7 8.5 copy-start.5
  785.7 9.2 slice-start
  786.0 8.9 copy-start.34
  786.0 8.9 slice-start.1
  821.7 10.2 copy-start.16
  821.7 10.3 copy-start.20
  832.0 8.5 copy-start.19
  842.1 9.4 copy-start.17
  867.3 779.1 %reduce-scatter.17.cloned.1.call-start = ((), (), s32[]{:S(2)}) async-start(), calls=%async_computation.12 | async-start | bytes 4718592 | tf_op jit(solution)/shard_map/reduce_scatter | solution.py:149
  874.5 814.3 %reduce-scatter.9.cloned.1.call-start = ((), (), s32[]{:S(2)}) async-start(), calls=%async_computation.8 | async-start | bytes 4718592 | tf_op jit(solution)/shard_map/reduce_scatter | solution.py:145
  910.7 869.2 %reduce-scatter.15.cloned.1.call-start = ((), (), s32[]{:S(2)}) async-start(), calls=%async_computation.11 | async-start | bytes 4718592 | tf_op jit(solution)/shard_map/reduce_scatter | solution.py:148
  917.4 1058.9 %reduce-scatter.21.cloned.1.call-start = ((), (), s32[]{:S(2)}) async-start(), calls=%async_computation.14 | async-start | bytes 12976128 | tf_op jit(solution)/shard_map/reduce_scatter | solution.py:153
  929.4 1242.7 %reduce-scatter.19.cloned.1.call-start = ((), (), s32[]{:S(2)}) async-start(), calls=%async_computation.13 | async-start | bytes 12976128 | tf_op jit(solution)/shard_map/reduce_scatter | solution.py:152
  941.4 1426.6 %reduce-scatter.23.cloned.1.call-start = ((), (), s32[]{:S(2)}) async-start(), calls=%async_computation.15 | async-start | bytes 12976128 | tf_op jit(solution)/shard_map/reduce_scatter | solution.py:151
  953.4 1505.6 %reduce-scatter.13.cloned.1.call-start = ((), (), s32[]{:S(2)}) async-start(), calls=%async_computation.10 | async-start | bytes 4718592 | tf_op jit(solution)/shard_map/reduce_scatter | solution.py:147
  1505.1 55.0 %copy-start.10 = (bf16[8,128,16,64]{1,3,2,0:T(8,128)(2,1)S(1)}, bf16[8,128,16,64]{1,3,2,0:T(8,128)(2,1)}, u32[]{:S(2)}) copy-start(bf16[8,128,16,64]{1,3,2,0:T(8,128)(2,1)} %copy.78) | copy-start | bytes 6291460
  1572.1 978.8 %reduce-scatter.11.cloned.1.call-start = ((), (), s32[]{:S(2)}) async-start(), calls=%async_computation.9 | async-start | bytes 4718592 | tf_op jit(solution)/shard_map/reduce_scatter | solution.py:146
  1605.4 1080.0 %all-reduce.4.cloned.1.call-start = ((), (), s32[]{:S(2)}) async-start(), calls=%async_computation.18 | async-start | bytes 13893632 | tf_op jit(solution)/shard_map/psum | solution.py:155
  1646.3 904.6 %copy-start.25 = (bf16[1024,1024]{1,0:T(8,128)(2,1)S(1)}, bf16[1024,1024]{1,0:T(8,128)(2,1)}, u32[]{:S(2)}) copy-start(bf16[1024,1024]{1,0:T(8,128)(2,1)} %copy-done.24) | copy-start | bytes 6291460
  2685.4 8.6 copy-start.37
  2685.4 9.7 copy-start.36
  (41 other events, 141.8 us)
Sparse Core Ops, SparseCore 0:
  55.2 640.4 all-gather.4
  867.4 637.6 all-gather.6
  1508.8 88.0 reduce-scatter.16
  1600.7 87.9 reduce-scatter.8
  1692.3 87.6 reduce-scatter.14
  1783.8 192.4 reduce-scatter.20
  1980.3 191.7 reduce-scatter.18
  2176.1 191.7 reduce-scatter.22
  2372.0 86.9 reduce-scatter.12
  2463.1 87.8 reduce-scatter.10
  2554.1 131.2 all-reduce.3
where the time goes:
time: 2710 us; the launch traced here: 2700 us
  waiting for transfers between devices  2180 us (80%)
  matrix products  226 us (8%)
  other arithmetic  135 us (5%)
  local copies, waits for them, and re-layouts  122 us (5%)
  blocking collectives  27.5 us (1%)
    all_gather x2, waiting for transfers between devices, entering(): everything = lax.all_gather(x, axis)  1150 us
    reduce_scatter x1, waiting for transfers between devices, body(): lax.psum_scatter(grad_w2, 'blk', scatter_dimension=0, tiled=True)  196 us
    reduce_scatter x1, waiting for transfers between devices, body(): lax.psum_scatter(grad_w1, 'blk', scatter_dimension=0, tiled=True)  196 us
    reduce_scatter x1, waiting for transfers between devices, body(): lax.psum_scatter(grad_w3, 'blk', scatter_dimension=0, tiled=True)  196 us
    psum x1, waiting for transfers between devices, body(): lax.psum((sq, sk, sv, sg, so, sgain, sthree, sone, stwo), 'batch')  118 us
    select_n x16, other arithmetic, step(): return jnp.where(reached, new, before)  110 us
    reduce_scatter x1, waiting for transfers between devices, body(): lax.psum_scatter(grad_wk, 'blk', scatter_dimension=0, tiled=True)  91.9 us
    reduce_scatter x1, waiting for transfers between devices, body(): lax.psum_scatter(grad_wg, 'blk', scatter_dimension=0, tiled=True)  91.2 us
  transfers between devices with their start and end apart: 11, of which 10 were waited for; matrix products, arithmetic and copies ran while one was open for 9% of the time, Pallas kernels for 0%

commit v1 on v0

v1 whole, which is shorter than its diff:
```python
import functools

import jax
import jax.numpy as jnp
from jax import lax
from jax.experimental import pallas as pl
from jax.experimental.pallas import tpu as pltpu
from jax.sharding import PartitionSpec as P

HEAD = 64
EPS = 1e-06
MESH = pl.DeviceIdType.MESH
F32 = jnp.float32
BF16 = jnp.bfloat16
MIB = 2**20


def silu_parts(pre):
    sig = jax.nn.sigmoid(pre)
    return (pre * sig, sig * (1.0 + pre * (1.0 - sig)))


def norm_back(grad, value, scale):
    inner = jnp.mean(grad * value, axis=-1, keepdims=True)
    return scale * grad - value * (scale * scale * scale) * inner


def project(left, weight):
    return jnp.dot(left, weight, preferred_element_type=F32)


def weight_grad(left, right):
    return jnp.einsum("td,tf->df", left, right, preferred_element_type=F32)


def back_project(grad, weight):
    return jnp.einsum("tf,df->td", grad, weight, preferred_element_type=F32)


def dot(a, b, ca, cb):
    return lax.dot_general(a, b, (((ca,), (cb,)), ((), ())), preferred_element_type=F32)


def low_lanes(shape):
    return lax.broadcasted_iota(jnp.int32, shape, len(shape) - 1) < HEAD


def two_heads(x):
    low = low_lanes(x.shape)
    zero = jnp.zeros_like(x)
    return jnp.concatenate([jnp.where(low, x, zero), jnp.where(low, zero, x)], axis=0)


def pick_heads(x):
    half = x.shape[0] // 2
    return jnp.where(low_lanes((half, x.shape[1])), x[:half], x[half:])


def causal_pair(span):
    t = lax.broadcasted_iota(jnp.int32, (span, 2 * span), 0)
    u = lax.broadcasted_iota(jnp.int32, (span, 2 * span), 1)
    return t >= u % span


def pair_of(ref, p):
    return ref[:, pl.ds(p * 2 * HEAD, 2 * HEAD)]


def state_kernel(left_ref, right_ref, out_ref):
    for p in range(out_ref.shape[1]):
        out_ref[0, p] = pick_heads(dot(pair_of(left_ref, p), pair_of(right_ref, p), 0, 0))


def attn_kernel(q_ref, k_ref, v_ref, prefix_ref, out_ref):
    span = q_ref.shape[0]
    causal = causal_pair(span)
    for p in range(prefix_ref.shape[1]):
        q, k2, v2 = pair_of(q_ref, p), two_heads(pair_of(k_ref, p)), two_heads(pair_of(v_ref, p))
        scores = jnp.where(causal, dot(q, k2, 1, 1), 0.0).astype(BF16)
        prefix = two_heads(prefix_ref[0, p])
        out_ref[:, pl.ds(p * 2 * HEAD, 2 * HEAD)] = dot(scores, v2, 1, 0) + dot(q, prefix, 1, 0)


def attn_back_kernel(q_ref, k_ref, v_ref, g_ref, prefix_ref, dstate_ref, dq_ref, dk_ref, dv_ref):
    span = q_ref.shape[0]
    causal = causal_pair(span)
    for p in range(prefix_ref.shape[1]):
        q, k, v, g = (pair_of(r, p) for r in (q_ref, k_ref, v_ref, g_ref))
        k2, v2 = two_heads(k), two_heads(v)
        prefix, dstate = two_heads(prefix_ref[0, p]), two_heads(dstate_ref[0, p])
        scores = jnp.where(causal, dot(q, k2, 1, 1), 0.0).astype(BF16)
        dscores = jnp.where(causal, dot(g, v2, 1, 1), 0.0).astype(BF16)
        lanes = pl.ds(p * 2 * HEAD, 2 * HEAD)
        dq_ref[:, lanes] = dot(dscores, k2, 1, 0) + dot(g, prefix, 1, 1)
        dk_ref[:, lanes] = pick_heads(dot(dscores, q, 0, 0)) + dot(v, dstate, 1, 1)
        dv_ref[:, lanes] = pick_heads(dot(scores, g, 0, 0)) + dot(k, dstate, 1, 0)


def rows_spec(span, width):
    return pl.BlockSpec((span, width), lambda s: (s, 0))


def state_spec(pairs):
    return pl.BlockSpec((1, pairs, HEAD, 2 * HEAD), lambda s: (s, 0, 0, 0))


def local_states(left, right, seqs):
    rows, width = left.shape
    span, pairs = rows // seqs, width // (2 * HEAD)
    return pl.pallas_call(
        state_kernel,
        grid=(seqs,),
        in_specs=[rows_spec(span, width)] * 2,
        out_specs=state_spec(pairs),
        out_shape=jax.ShapeDtypeStruct((seqs, pairs, HEAD, 2 * HEAD), F32),
    )(left, right)


def attention(q, k, v, prefix, seqs):
    rows, width = q.shape
    span, pairs = rows // seqs, width // (2 * HEAD)
    return pl.pallas_call(
        attn_kernel,
        grid=(seqs,),
        in_specs=[rows_spec(span, width)] * 3 + [state_spec(pairs)],
        out_specs=rows_spec(span, width),
        out_shape=jax.ShapeDtypeStruct((rows, width), F32),
    )(q, k, v, prefix)


def attention_back(q, k, v, g, prefix, dstate, seqs):
    rows, width = q.shape
    span, pairs = rows // seqs, width // (2 * HEAD)
    return pl.pallas_call(
        attn_back_kernel,
        grid=(seqs,),
        in_specs=[rows_spec(span, width)] * 4 + [state_spec(pairs)] * 2,
        out_specs=[rows_spec(span, width)] * 3,
        out_shape=[jax.ShapeDtypeStruct((rows, width), F32)] * 3,
    )(q, k, v, g, prefix, dstate)


def scan_kernel(outer, reverse, s_ref, out_ref, held, summed, other, zs, zr, xs, xr):
    chunks = s_ref.shape[0]
    k = lax.axis_index("blk")
    z, x = k // 2, k % 2
    if reverse:
        zz, xx = outer - 1 - z, 1 - x
        after, before = jnp.maximum(z - 1, 0), jnp.minimum(z + 1, outer - 1)
    else:
        zz, xx = z, x
        after, before = jnp.minimum(z + 1, outer - 1), jnp.maximum(z - 1, 0)
    nxt, prv, side = {"blk": after * 2 + x}, {"blk": before * 2 + x}, {"blk": z * 2 + 1 - x}
    first, last = zz == 0, zz == outer - 1

    bar = pltpu.get_barrier_semaphore()
    pl.semaphore_signal(bar, inc=1, device_id=side, device_id_type=MESH)
    pl.when(~last)(lambda: pl.semaphore_signal(bar, inc=1, device_id=nxt, device_id_type=MESH))
    pl.when(~first)(lambda: pl.semaphore_signal(bar, inc=1, device_id=prv, device_id_type=MESH))
    pl.semaphore_wait(bar, 1 + jnp.where(last, 0, 1) + jnp.where(first, 0, 1))

    def along(i):
        return pltpu.make_async_remote_copy(
            src_ref=summed.at[i], dst_ref=held.at[i], send_sem=zs.at[i], recv_sem=zr.at[i],
            device_id=nxt, device_id_type=MESH)

    def across(i, src):
        return pltpu.make_async_remote_copy(
            src_ref=src.at[i], dst_ref=other.at[i], send_sem=xs.at[i], recv_sem=xr.at[i],
            device_id=side, device_id_type=MESH)

    def pass_on(i):
        pl.when(~first)(lambda: along(i).wait_recv())

        @pl.when(first)
        def _():
            held[i] = jnp.zeros_like(held[i])

        summed[i] = held[i] + s_ref[i]
        pl.when(~last)(lambda: along(i).start())
        pl.when(xx == 0)(lambda: across(i, summed).start())
        pl.when(xx == 1)(lambda: across(i, held).start())

    def finish(i):
        across(i, held).wait_recv()
        out_ref[i] = (held[i] + other[i]).astype(out_ref.dtype)

    def step(i, carry):
        pl.when(i < chunks)(lambda: pass_on(i))
        pl.when(i > 0)(lambda: finish(i - 1))
        return carry

    lax.fori_loop(0, chunks + 1, step, 0)

    def drain(i, carry):
        pl.when(~last)(lambda: along(i).wait_send())
        across(i, held).wait_send()
        return carry

    lax.fori_loop(0, chunks, drain, 0)


def entering(states, blk, reverse):
    seqs, pairs, head, lanes = states.shape
    per = max(1, pairs // 2)
    shape = (seqs * pairs // per, per, head, lanes)
    vmem = pl.BlockSpec(memory_space=pltpu.VMEM)
    sems = [pltpu.SemaphoreType.DMA((shape[0],))] * 4
    out = pl.pallas_call(
        functools.partial(scan_kernel, blk // 2, reverse),
        out_shape=jax.ShapeDtypeStruct(shape, BF16),
        in_specs=[vmem],
        out_specs=vmem,
        scratch_shapes=[pltpu.VMEM(shape, F32)] * 3 + sems,
        compiler_params=pltpu.CompilerParams(
            collective_id=2 if reverse else 1, has_side_effects=True, vmem_limit_bytes=24 * MIB),
    )(states.reshape(shape))
    return out.reshape(states.shape)


LAND, FIN, ACC = 4, 8, 10
CORE, XA, YA, YB, XB, XC, YC = range(7)


def reduce_kernel(outer, theirs, mine, out, core_rx, acc, xa, ya, yb, xb, xc, yc, zab, zc, fin,
                  ssem, rsem, zss, zrs, lsem, osem, cgs, cgr, ygs, ygr):
    chunks = theirs.shape[0]
    b, k = lax.axis_index("batch"), lax.axis_index("blk")
    y, c = b // 2, b % 2
    z, x = k // 2, k % 2
    ox, oy = 1 - x, 1 - y
    top = outer - 1
    zr = top - z
    to_core, to_y, to_x = {"batch": y * 2 + 1 - c}, {"batch": oy * 2 + c}, {"blk": z * 2 + ox}
    to_up = {"blk": jnp.minimum(z + 1, top) * 2 + x}
    to_down = {"blk": jnp.maximum(z - 1, 0) * 2 + x}

    bar = pltpu.get_barrier_semaphore()
    for d in (to_core, to_y, to_x):
        pl.semaphore_signal(bar, inc=1, device_id=d, device_id_type=MESH)
    pl.when(z < top)(lambda: pl.semaphore_signal(bar, inc=1, device_id=to_up, device_id_type=MESH))
    pl.when(z > 0)(lambda: pl.semaphore_signal(bar, inc=1, device_id=to_down, device_id_type=MESH))
    pl.semaphore_wait(bar, 3 + jnp.where(z < top, 1, 0) + jnp.where(z > 0, 1, 0))

    def remote(src, dst, s, r, dev):
        return pltpu.make_async_remote_copy(
            src_ref=src, dst_ref=dst, send_sem=s, recv_sem=r, device_id=dev, device_id_type=MESH)

    def link(kind, i, src, dst, dev):
        return remote(src, dst.at[i % LAND], ssem.at[kind, i % LAND], rsem.at[kind, i % LAND], dev)

    def at(i, *where):
        return acc.at[(i % ACC,) + where]

    A, B, C = pl.ds(0, 32), pl.ds(32, 16), pl.ds(48, 16)
    every = slice(None)

    def core_copy(i):
        return link(CORE, i, theirs.at[i], core_rx, to_core)

    def mine_copy(i):
        return pltpu.make_async_copy(mine.at[i], at(i), lsem.at[i % LAND])

    def xa_copy(i):
        return link(XA, i, at(i, every, ox, every, A), xa, to_x)

    def ya_copy(i):
        return link(YA, i, at(i, every, x, oy, A), ya, to_y)

    def yb_copy(i):
        return link(YB, i, at(i, every, every, oy, B), yb, to_y)

    def xb_copy(i):
        return link(XB, i, at(i, every, ox, y, B), xb, to_x)

    def xc_copy(i):
        return link(XC, i, at(i, z, ox, every, C), xc, to_x)

    def yc_copy(i):
        return link(YC, i, at(i, z, x, oy, C), yc, to_y)

    def y_share(i):
        f = i % FIN
        return remote(fin.at[f, y], fin.at[f, y], ygs.at[f], ygr.at[f], to_y)

    def core_share(i):
        f = i % FIN
        return remote(fin.at[f], out.at[i, c], cgs.at[f], cgr.at[f], to_core)

    def store(i):
        return pltpu.make_async_copy(fin.at[i % FIN], out.at[i, c], osem.at[i % FIN])

    def part_ab(i, s):
        return at(i, s, x, y, pl.ds(0, 48))

    def part_c(i, s):
        return at(i, s, every, every, C)

    AB, CC = (0, part_ab, zab), (1, part_c, zc)

    def hop(group, i, r, up, s):
        g, part, land = group
        d = 0 if up else 1
        sem = (g, d, r - 1, i % LAND)
        return remote(part(i, s), land.at[i % LAND, d, r - 1], zss.at[sem], zrs.at[sem],
                      to_up if up else to_down)

    def z_each(group, i, r, act):
        up = hop(group, i, r, True, jnp.minimum(outer - r + z, top))
        down = hop(group, i, r, False, jnp.maximum(r - 1 - zr, 0))
        pl.when((z <= r - 1) & (z < top))(lambda: act(up))
        pl.when((zr <= r - 1) & (z > 0))(lambda: act(down))

    def z_send(group, i, r):
        z_each(group, i, r, lambda copy: copy.start())

    def z_sent(group, i, r):
        z_each(group, i, r, lambda copy: copy.wait_send())

    def z_take(group, i, r):
        g, part, land = group

        def take(up, s):
            hop(group, i, r, up, s).wait_recv()
            ref = part(i, s)
            ref[...] = ref[...] + land[i % LAND, 0 if up else 1, r - 1]

        pl.when((z > 0) & (z <= r))(lambda: take(True, jnp.clip(outer - r + z - 1, 0, top)))
        pl.when((z < top) & (zr <= r))(lambda: take(False, jnp.clip(r - zr, 0, top)))

    def add(ref, landed):
        ref[...] = ref[...] + landed

    def begin(i):
        mine_copy(i).start()
        core_copy(i).start()

    def cores(i):
        mine_copy(i).wait()
        core_copy(i).wait_recv()
        core_copy(i).wait_send()
        add(at(i), core_rx[i % LAND])
        xa_copy(i).start()
        yb_copy(i).start()
        z_send(CC, i, 1)

    def second(i):
        yb_copy(i).wait_recv()
        add(at(i, every, every, y, B), yb[i % LAND])
        xb_copy(i).start()
        xa_copy(i).wait_recv()
        add(at(i, every, x, every, A), xa[i % LAND])
        ya_copy(i).start()
        z_take(CC, i, 1)
        z_send(CC, i, 2)
        xa_copy(i).wait_send()
        yb_copy(i).wait_send()
        z_sent(CC, i, 1)

    def third(i):
        xb_copy(i).wait_recv()
        add(at(i, every, x, y, B), xb[i % LAND])
        ya_copy(i).wait_recv()
        add(at(i, every, x, y, A), ya[i % LAND])
        z_send(AB, i, 1)
        z_take(CC, i, 2)
        z_send(CC, i, 3)
        xb_copy(i).wait_send()
        ya_copy(i).wait_send()
        z_sent(CC, i, 2)

    def fourth(i):
        z_take(AB, i, 1)
        z_send(AB, i, 2)
        z_take(CC, i, 3)
        xc_copy(i).start()
        z_sent(AB, i, 1)
        z_sent(CC, i, 3)

    def fifth(i):
        z_take(AB, i, 2)
        z_send(AB, i, 3)
        xc_copy(i).wait_recv()
        add(at(i, z, x, every, C), xc[i % LAND])
        yc_copy(i).start()
        z_sent(AB, i, 2)
        xc_copy(i).wait_send()

    def sixth(i):
        yc_copy(i).wait_recv()
        z_take(AB, i, 3)
        fin[i % FIN, y, pl.ds(0, 48)] = acc[i % ACC, z, x, y, pl.ds(0, 48)]
        fin[i % FIN, y, C] = acc[i % ACC, z, x, y, C] + yc[i % LAND]
        y_share(i).start()
        z_sent(AB, i, 3)
        yc_copy(i).wait_send()

    def seventh(i):
        y_share(i).wait_recv()
        y_share(i).wait_send()
        core_share(i).start()
        store(i).start()

    def last(i):
        core_share(i).wait_send()
        store(i).wait()
        core_share(i).wait_recv()

    stages = (begin, cores, second, third, fourth, fifth, sixth, seventh, last)

    def step(t, carry):
        for n, stage in enumerate(stages):
            i = t - n
            pl.when((i >= 0) & (i < chunks))(functools.partial(stage, i))
        return carry

    lax.fori_loop(0, chunks + len(stages) - 1, step, 0)


def reduce_chunks(theirs, mine):
    chunks = theirs.shape[0]
    anywhere = pl.BlockSpec(memory_space=pl.ANY)

    def v(*shape):
        return pltpu.VMEM(shape, F32)

    def sem(*shape):
        return pltpu.SemaphoreType.DMA(shape)

    return pl.pallas_call(
        functools.partial(reduce_kernel, 4),
        out_shape=jax.ShapeDtypeStruct((chunks, 2, 2, 64, 128), F32),
        in_specs=[anywhere, anywhere],
        out_specs=anywhere,
        scratch_shapes=[
            v(LAND, 4, 2, 2, 64, 128), v(ACC, 4, 2, 2, 64, 128), v(LAND, 4, 2, 32, 128),
            v(LAND, 4, 32, 128), v(LAND, 4, 2, 16, 128), v(LAND, 4, 16, 128), v(LAND, 2, 16, 128),
            v(LAND, 16, 128), v(LAND, 2, 3, 48, 128), v(LAND, 2, 3, 2, 2, 16, 128), v(FIN, 2, 64, 128),
            sem(7, LAND), sem(7, LAND), sem(2, 2, 3, LAND), sem(2, 2, 3, LAND),
            sem(LAND), sem(FIN), sem(FIN), sem(FIN), sem(FIN), sem(FIN),
        ],
        compiler_params=pltpu.CompilerParams(
            collective_id=3, has_side_effects=True, vmem_limit_bytes=32 * MIB),
    )(theirs, mine)


def square_chunks(g):
    g = g.reshape(4, 2, 2, 64, 2, 2, 2, 128)
    g = g.transpose(4, 2, 5, 0, 1, 6, 3, 7)
    return g.reshape(2, 4, 4, 2, 2, 64, 128)


def square_back(out):
    out = out.reshape(2, 2, 2, 2, 64, 128)
    return out.transpose(0, 4, 2, 1, 3, 5).reshape(128, 1024)


def wide_chunks(g1, g2):
    n = g1.shape[1] // 256
    g = jnp.stack([g1, g2])
    g = g.reshape(2, 4, 2, 2, 64, 2, n, 128)
    g = g.transpose(5, 3, 6, 1, 2, 0, 4, 7)
    return g.reshape(2, 2 * n, 4, 2, 2, 64, 128)


def wide_back(out):
    n = out.shape[0] // 2
    out = out.reshape(2, n, 2, 2, 64, 128)
    out = out.transpose(3, 0, 4, 2, 1, 5).reshape(2, 128, 2 * n * 128)
    return out[0], out[1]


def tall_chunks(g):
    n = g.shape[0] // 256
    g = g.reshape(4, 2, n, 32, 2, 2, 2, 128)
    g = g.transpose(4, 2, 0, 1, 5, 6, 3, 7)
    return g.reshape(2, n, 4, 2, 2, 64, 128)


def tall_back(out):
    n = out.shape[0]
    out = out.reshape(n, 2, 2, 2, 32, 128)
    return out.transpose(0, 4, 1, 2, 3, 5).reshape(n * 32, 1024)


def reduce_weights(grads):
    gq, gk, gv, gg, go, g1, g2, g3 = grads
    parts = [tall_chunks(g3), wide_chunks(g1, g2)]
    parts += [square_chunks(g) for g in (go, gg, gq, gk, gv)]
    every = jnp.concatenate(parts, axis=1)
    c = lax.axis_index("batch") % 2
    theirs = lax.dynamic_index_in_dim(every, 1 - c, 0, False)
    mine = lax.dynamic_index_in_dim(every, c, 0, False)
    out = reduce_chunks(theirs, mine)
    n3, n12 = parts[0].shape[1], parts[1].shape[1]
    s3 = tall_back(out[:n3])
    s1, s2 = wide_back(out[n3:n3 + n12])
    at = n3 + n12
    so, sg, sq, sk, sv = (square_back(out[at + 4 * i:at + 4 * i + 4]) for i in range(5))
    return sq, sk, sv, sg, so, s1, s2, s3


def reduce_plain(grads):
    return tuple(
        lax.psum(lax.psum_scatter(g, "blk", scatter_dimension=0, tiled=True), "batch") for g in grads)


def body(
    sizes, tokens, cotangent, w_query, w_key, w_value, w_gate, w_out, out_gain, w_first, w_second, w_third
):
    batch, blk = sizes
    seqs, span, width = tokens.shape
    rows = seqs * span
    xf = tokens.reshape(rows, width).astype(F32)
    rone = lax.rsqrt(jnp.mean(xf * xf, axis=-1, keepdims=True) + EPS)
    normed = (xf * rone).astype(BF16)
    key = project(normed, w_key)
    value = project(normed, w_value)
    fkey, key_der = silu_parts(key)
    k, v = fkey.astype(BF16), value.astype(BF16)
    prefix = entering(local_states(k, v, seqs), blk, False)
    query = project(normed, w_query)
    gate = project(normed, w_gate)
    fquery, query_der = silu_parts(query)
    q = fquery.astype(BF16)
    attn = attention(q, k, v, prefix, seqs)
    rattn = lax.rsqrt(jnp.mean(attn * attn, axis=-1, keepdims=True) + EPS)
    unit_attn = attn * rattn
    scaled = unit_attn * out_gain
    gate_act, gate_der = silu_parts(gate)
    mixed = (scaled * gate_act).astype(BF16)
    resid = xf + project(mixed, w_out)
    rtwo = lax.rsqrt(jnp.mean(resid * resid, axis=-1, keepdims=True) + EPS)
    normed2 = (resid * rtwo).astype(BF16)
    first = project(normed2, w_first)
    second = project(normed2, w_second)
    inner = (first * second).astype(BF16)
    output = (resid + project(inner, w_third)).astype(BF16)
    grad_top = cotangent.reshape(rows, width)
    grad_w3 = weight_grad(inner, grad_top)
    grad_inner = back_project(grad_top, w_third)
    grad_one = (grad_inner * second).astype(BF16)
    grad_two = (grad_inner * first).astype(BF16)
    grad_w1 = weight_grad(normed2, grad_one)
    grad_w2 = weight_grad(normed2, grad_two)
    grad_normed2 = back_project(grad_one, w_first) + back_project(grad_two, w_second)
    grad_resid = grad_top.astype(F32) + norm_back(grad_normed2, resid, rtwo)
    grad_resid_low = grad_resid.astype(BF16)
    grad_wo = weight_grad(mixed, grad_resid_low)
    grad_mixed = back_project(grad_resid_low, w_out)
    grad_scaled = grad_mixed * gate_act
    grad_gate_low = (grad_mixed * scaled * gate_der).astype(BF16)
    grad_gain_local = jnp.sum(grad_scaled * unit_attn, axis=0)
    grad_attn = norm_back(grad_scaled * out_gain, attn, rattn).astype(BF16)
    dstate = entering(local_states(q, grad_attn, seqs), blk, True)
    grad_fq, grad_fk, grad_vv = attention_back(q, k, v, grad_attn, prefix, dstate, seqs)
    grad_query_low = (grad_fq * query_der).astype(BF16)
    grad_key_low = (grad_fk * key_der).astype(BF16)
    grad_value_low = grad_vv.astype(BF16)
    grad_wq = weight_grad(normed, grad_query_low)
    grad_wk = weight_grad(normed, grad_key_low)
    grad_wv = weight_grad(normed, grad_value_low)
    grad_wg = weight_grad(normed, grad_gate_low)
    grad_normed = back_project(grad_query_low, w_query) + back_project(grad_key_low, w_key)
    grad_normed = (
        grad_normed + back_project(grad_value_low, w_value) + back_project(grad_gate_low, w_gate)
    )
    grad_input = grad_resid + norm_back(grad_normed, xf, rone)
    grads = (grad_wq, grad_wk, grad_wv, grad_wg, grad_wo, grad_w1, grad_w2, grad_w3)
    fits = (batch, blk) == (4, 8) and width == 1024 and w_first.shape[1] % 256 == 0
    sq, sk, sv, sg, so, s1, s2, s3 = (reduce_weights if fits else reduce_plain)(grads)
    sgain = lax.psum(
        lax.psum_scatter(grad_gain_local, "blk", scatter_dimension=0, tiled=True), "batch")
    return (
        output.reshape(seqs, span, width),
        grad_input.reshape(seqs, span, width),
        sq, sk, sv, sg, so, sgain, s1, s2, s3,
    )


def solution(mesh):
    rows = P("batch", "blk", None)
    cut = P("blk", None)
    return jax.shard_map(
        functools.partial(body, (mesh.shape["batch"], mesh.shape["blk"])),
        mesh=mesh,
        in_specs=(rows, rows) + (P(),) * 9,
        out_specs=(rows, rows) + (cut,) * 5 + (P("blk"),) + (cut,) * 3,
        check_vma=False,
    )
```

time: 2710 us -> 846 us (0.31)
  waiting for transfers between devices: 2180 us -> 0 us
  Pallas kernels: 0 us -> 395 us
  other arithmetic: 135 us -> 31.3 us
  local copies, waits for them, and re-layouts: 122 us -> 216 us
  matrix products: 226 us -> 168 us
    all_gather x2 -> x0, waiting for transfers between devices: 1150 us -> none  [entering(): everything = lax.all_gather(x, axis)]
    reduce_scatter x8 -> x0, waiting for transfers between devices: 905 us -> none  [the longest x1 196 us: body(): lax.psum_scatter(grad_w2, 'blk', scatter_dimension=0, tiled=True)]
    pallas_call x0 -> x7, Pallas kernels: none -> 395 us  [the longest x1 225 us: reduce_chunks(): pl.pallas_call(functools.partial(reduce_kernel, 4), out_shape=jax.ShapeDt...]
    psum x1 -> x0, waiting for transfers between devices: 118 us -> none  [body(): lax.psum((sq, sk, sv, sg, so, sgain, sthree, sone, stwo), 'batch')]
    select_n x16 -> x0, other arithmetic: 110 us -> none  [step(): return jnp.where(reached, new, before)]
    reshape x14 -> x8, local copies, waits for them, and re-layouts: 90.2 us -> 17.7 us  [the longest x1 6.76 us: square_chunks(): g = g.reshape(4, 2, 2, 64, 2, 2, 2, 128)]
    dot_general x36 -> x24, matrix products: 226 us -> 168 us  [the longest x8 57.7 us: weight_grad(): return jnp.einsum('td,tf->df', left, right, preferred_element_type=F32)]
    squeeze x0 -> x3, local copies, waits for them, and re-layouts: none -> 40 us  [the longest x1 35.9 us: reduce_weights(): mine = lax.dynamic_index_in_dim(every, c, 0, False)]
  transfers between devices with their start and end apart: 11 -> 0, of which waited for: 10 -> 0; matrix products, arithmetic and copies ran while one was open for 9% -> 0% of each run, Pallas kernels for 0% -> 0%
where the time goes in v1:
time: 846 us; the launch traced here: 839 us
  Pallas kernels  395 us (47%)
  local copies, waits for them, and re-layouts  216 us (26%)
  matrix products  168 us (20%)
  other arithmetic  31.3 us (4%)
  blocking collectives  26 us (3%)
    pallas_call x1, Pallas kernels, reduce_chunks(): pl.pallas_call(functools.partial(reduce_kernel, 4), out_shape=jax.ShapeDt...  225 us
    pallas_call x2, Pallas kernels, entering(): pl.pallas_call(functools.partial(scan_kernel, blk // 2, reverse), out_sha...  126 us
    unnamed x118, local copies, waits for them, and re-layouts  58.7 us
    dot_general x8, matrix products, weight_grad(): return jnp.einsum('td,tf->df', left, right, preferred_element_type=F32)  57.7 us
    dot_general x8, matrix products, back_project(): return jnp.einsum('tf,df->td', grad, weight, preferred_element_type=F32)  56.4 us
    dot_general x8, matrix products, project(): return jnp.dot(left, weight, preferred_element_type=F32)  53.5 us
    squeeze x1, local copies, waits for them, and re-layouts, reduce_weights(): mine = lax.dynamic_index_in_dim(every, c, 0, False)  35.9 us
    another operation x2, local copies, waits for them, and re-layouts, wide_chunks(): g = jnp.stack([g1, g2])  30.3 us

profile of v1, /device:TPU:0, one launch (start us, length us, event | category | flops | bytes accessed | tf_op | source)
XLA Modules:
  0.0 838.6 jit_solution(4889428522904686739)
XLA Ops:
  28.6 50.6 %shard_map.195 = bf16[16,4,64,128]{3,2,1,0:T(8,128)(2,1)S(1)} custom-call(f32[16,4,64,128]{3,2,1,0:T(8,128)S(1)} %bitcast.166), custom_call_target="tpu_custom_call" | custom-call | tf_op jit(solution)/shard_map/pallas_call | solution.py:209
  80.1 11.0 %shard_map.196 = f32[1024,1024]{1,0:T(8,128)} custom-call(bf16[1024,1024]{1,0:T(8,128)(2,1)} %get-tuple-element.36.q_ref.left_ref, bf16[1024,1024]{1,0:T(8,128)(2,1)} %get-tuple-element.38.left_ref.k_ref, bf16[1024,1024]{1,0:T(8,128)(2,1)} %convolution_convert_fusion.right_ref.v_ref, bf16[8,8,64,128]{3,2,1,0:T(8,128)(2,1)} %bitcast.164), custom_call_target="tpu_custom_call" | custom-call | tf_op jit(solution)/shard_map/pallas_call | solution.py:122
  94.6 7.2 multiply_convert_fusion.7
  106.8 8.8 %fusion.16 = f32[1024,2816]{1,0:T(8,128)} fusion(bf16[1024,1024]{1,0:T(8,128)(2,1)S(1)} %multiply_convert_fusion.6, bf16[1024,2816]{1,0:T(8,128)(2,1)S(1)} %bitcast.203), kind=kOutput, calls=%fused_computation.70 | convolution fusion | flops 5905580032 | bytes 19398656 | tf_op jit(solution)/shard_map/dot_general | solution.py:29
  115.6 8.9 %fusion.17 = f32[1024,2816]{1,0:T(8,128)} fusion(bf16[1024,1024]{1,0:T(8,128)(2,1)S(1)} %multiply_convert_fusion.6, bf16[1024,2816]{1,0:T(8,128)(2,1)S(1)} %bitcast.205), kind=kOutput, calls=%fused_computation.71 | convolution fusion | flops 5905580032 | bytes 19398656 | tf_op jit(solution)/shard_map/dot_general | solution.py:29
  124.5 18.3 %multiply_convert_fusion = (bf16[1024,2816]{1,0:T(8,128)(2,1)}, bf16[1024,2816]{1,0:T(8,128)(2,1)}, bf16[1024,2816]{1,0:T(8,128)(2,1)}) fusion(f32[1024,2816]{1,0:T(8,128)} %fusion.16, f32[1024,2816]{1,0:T(8,128)} %fusion.17, bf16[1024,1024]{1,0:T(8,128)(2,1)} %bitcast.171, bf16[2816,1024]{1,0:T(8,128)(2,1)} %param.21), kind=kOutput, calls=%fused_computation.4 | convolution fusion | flops 5922881536 | bytes 48234496 | tf_op jit(solution)/shard_map/tf,df->td/dot_general | solution.py:37
  142.8 11.6 %add_convert_fusion = bf16[1024,1024]{1,0:T(8,128)(2,1)} fusion(f32[1024,1024]{1,0:T(8,128)} %copy-done.13, bf16[1024,2816]{1,0:T(8,128)(2,1)} %get-tuple-element.23, bf16[2816,1024]{1,0:T(8,128)(2,1)} %param.21), kind=kOutput, calls=%fused_computation.28 | convolution fusion | flops 5907677184 | bytes 17825792 | tf_op jit(solution)/shard_map/dot_general | solution.py:29
  154.4 9.7 %fusion.18 = f32[1024,1024]{1,0:T(8,128)} fusion(bf16[1024,2816]{1,0:T(8,128)(2,1)S(1)} %copy-done.18, bf16[1024,2816]{1,0:T(8,128)(2,1)} %param.19), kind=kOutput, calls=%fused_computation.72 | convolution fusion | flops 5905580032 | bytes 15728640 | tf_op jit(solution)/shard_map/tf,df->td/dot_general | solution.py:37
  164.1 9.3 %multiply_reduce_fusion.2 = (f32[1024]{0:T(1024)S(1)}, f32[1024,1024]{1,0:T(8,128)S(1)}) fusion(f32[1024,1024]{1,0:T(8,128)S(1)} %copy-done.14, f32[1024,1024]{1,0:T(8,128)} %fusion.18, bf16[1024,2816]{1,0:T(8,128)(2,1)S(1)} %copy-done.19, bf16[1024,2816]{1,0:T(8,128)(2,1)} %param.20), kind=kOutput, calls=%fused_computation.27 | convolution fusion | flops 5908724736 | bytes 24121344 | tf_op jit(solution)/shard_map/tf,df->td/dot_general | solution.py:37
  196.5 75.4 %shard_map.198 = bf16[16,4,64,128]{3,2,1,0:T(8,128)(2,1)S(1)} custom-call(f32[16,4,64,128]{3,2,1,0:T(8,128)S(1)} %bitcast.167), custom_call_target="tpu_custom_call" | custom-call | tf_op jit(solution)/shard_map/pallas_call | solution.py:209
  272.9 19.1 %shard_map.199 = (f32[1024,1024]{1,0:T(8,128)}, f32[1024,1024]{1,0:T(8,128)}, f32[1024,1024]{1,0:T(8,128)}) custom-call(bf16[1024,1024]{1,0:T(8,128)(2,1)} %get-tuple-element.36.q_ref.left_ref, bf16[1024,1024]{1,0:T(8,128)(2,1)} %get-tuple-element.38.left_ref.k_ref, bf16[1024,1024]{1,0:T(8,128)(2,1)} %convolution_convert_fusion.right_ref.v_ref, ...), custom_call_target="tpu_custom_call" | custom-call | tf_op jit(solution)/shard_map/pallas_call | solution.py:134
  314.1 8.5 %copy.128 = bf16[2816,1024]{1,0:T(8,128)(2,1)} copy(bf16[2816,1024]{0,1:T(8,128)(2,1)} %bitcast.170) | data formatting | bytes 11534336 | tf_op jit(solution)/shard_map/convert_element_type | solution.py:537
  325.3 11.4 %fusion.21 = f32[4,2,11,32,2,2,2,128]{7,3,6,5,4,2,1,0:T(8,128)} fusion(bf16[4,2,11,32,1024,1,1,1]{4,3,7,6,5,2,1,0:T(8,128)(2,1)} %bitcast.186, bf16[2,2,2,128,1024,1,1,1]{4,3,2,1,0,7,6,5:T(8,128)(2,1)} %bitcast.198), kind=kOutput, calls=%fused_computation.75 | convolution fusion | flops 5905580032 | bytes 19398656 | tf_op jit(solution)/shard_map/td,tf->df/dot_general | solution.py:33
  336.6 11.1 %copy_dynamic-update-slice_fusion = f32[2,53,4,2,2,64,128]{6,5,4,3,2,1,0:T(8,128)} fusion(f32[2,11,4,2,2,64,128]{6,5,4,0,1,3,2:T(8,128)} %bitcast.181), kind=kLoop, calls=%fused_computation.3 | loop fusion | bytes 23068672
  347.8 11.6 %fusion.23 = f32[1024,2816]{1,0:T(8,128)} fusion(bf16[1024,1024]{1,0:T(8,128)(2,1)S(1)} %copy-done.35, bf16[1024,2816]{1,0:T(8,128)(2,1)} %get-tuple-element.22), kind=kOutput, calls=%fused_computation.77 | convolution fusion | flops 5905580032 | bytes 19398656 | tf_op jit(solution)/shard_map/td,tf->df/dot_general | solution.py:33
  359.4 15.1 %stack.10 = f32[1,4,2,2,64,2,11,128]{7,6,5,4,3,2,1,0:T(8,128)} reshape(f32[1024,2816]{1,0:T(8,128)} %fusion.23) | data formatting | bytes 23068672 | tf_op jit(solution)/shard_map/stack | solution.py:460
  374.5 12.0 %fusion.22 = f32[1024,2816]{1,0:T(8,128)} fusion(bf16[1024,1024]{1,0:T(8,128)(2,1)S(1)} %copy-done.35, bf16[1024,2816]{1,0:T(8,128)(2,1)} %get-tuple-element.24), kind=kOutput, calls=%fused_computation.76 | convolution fusion | flops 5905580032 | bytes 19398656 | tf_op jit(solution)/shard_map/td,tf->df/dot_general | solution.py:33
  386.6 15.1 %stack.9 = f32[1,4,2,2,64,2,11,128]{7,6,5,4,3,2,1,0:T(8,128)} reshape(f32[1024,2816]{1,0:T(8,128)} %fusion.22) | data formatting | bytes 23068672 | tf_op jit(solution)/shard_map/stack | solution.py:460
  401.7 13.3 %maximum_bitcast_fusion = f32[2,2,11,4,2,2,64,128]{7,2,0,6,1,4,3,5:T(8,128)S(1)} fusion(f32[1,4,2,2,64,2,11,128]{7,6,5,4,3,2,1,0:T(8,128)} %stack.10, f32[1,4,2,2,64,2,11,128]{7,6,5,4,3,2,1,0:T(8,128)} %stack.9), kind=kLoop, calls=%fused_computation | loop fusion | flops 5767168 | bytes 46137344 | tf_op jit(solution)/shard_map/transpose | solution.py:462
  415.0 27.7 %copy.130 = f32[2,2,11,4,2,2,64,128]{7,6,5,4,3,2,1,0:T(8,128)} copy(f32[2,2,11,4,2,2,64,128]{7,2,0,6,1,4,3,5:T(8,128)S(1)} %maximum_bitcast_fusion) | data formatting | bytes 46137344 | tf_op jit(solution)/shard_map/transpose | solution.py:462
  442.7 18.0 %constant_dynamic-update-slice_fusion.5 = f32[2,53,4,2,2,64,128]{6,5,4,3,2,1,0:T(8,128)} fusion(f32[2,53,4,2,2,64,128]{6,5,4,3,2,1,0:T(8,128)} %copy_dynamic-update-slice_fusion, f32[2,22,4,2,2,64,128]{6,5,4,3,2,1,0:T(8,128)} %bitcast.169), kind=kLoop, calls=%fused_computation.58 | loop fusion | bytes 46137344
  523.3 35.9 %dynamic-slice_bitcast_fusion = (f32[53,4,2,2,64,128]{5,4,3,2,1,0:T(8,128)}, f32[53,4,2,2,64,128]{5,4,3,2,1,0:T(8,128)}) fusion(f32[2,53,4,2,2,64,128]{6,5,4,3,2,1,0:T(8,128)} %constant_dynamic-update-slice_fusion, s32[]{:T(128)S(6)} %select_n.16, s32[]{:T(128)S(6)} %select_n.15), kind=kLoop, calls=%fused_computation.1 | loop fusion | bytes 111149064 | tf_op jit(solution)/shard_map/jit(dynamic_index_in_dim)/squeeze | solution.py:493
  559.2 225.4 %shard_map.200 = f32[53,2,2,64,128]{4,3,2,1,0:T(8,128)S(1)} custom-call(f32[53,4,2,2,64,128]{5,4,3,2,1,0:T(8,128)} %get-tuple-element.20.theirs, f32[53,4,2,2,64,128]{5,4,3,2,1,0:T(8,128)} %get-tuple-element.19.mine), custom_call_target="tpu_custom_call" | custom-call | tf_op jit(solution)/shard_map/pallas_call | solution.py:430
  795.9 19.9 %all-reduce = f32[1024]{0:T(1024)S(1)} all-reduce(f32[1024]{0:T(1024)S(1)} %copy-done.41), channel_id=2, replica_groups=mesh['batch'=4,'blk'=8] {'blk'}, use_global_device_ids=true, to_apply=%region_7.8.clone | all-reduce | flops 1024 | bytes 8192
  (184 shorter events, 181.3 us)
Async XLA Ops:
  0.6 101.2 %copy-start = (bf16[1024,1024]{1,0:T(8,128)(2,1)S(1)}, bf16[1024,1024]{1,0:T(8,128)(2,1)}, u32[]{:S(2)}) copy-start(bf16[1024,1024]{1,0:T(8,128)(2,1)} %param.17) | copy-start | bytes 6291460
  3.5 7.5 copy-start.38
  5.5 10.8 %copy-start.26 = (bf16[1024,1024]{1,0:T(8,128)(2,1)}, bf16[1024,1024]{1,0:T(8,128)(2,1)S(1)}, u32[]{:S(2)}) copy-start(bf16[1024,1024]{1,0:T(8,128)(2,1)S(1)} %fusion.1) | copy-start | bytes 6291460
  5.5 5.4 copy-start.46
  11.0 5.4 copy-start.42
  94.6 7.2 copy-start.9
  106.4 9.2 %slice-start.3 = ((s8[5767168]{0:T(1024)(128)(4,1)}), s8[4194304]{0:T(1024)(128)(4,1)S(1)}, s32[]{:S(2)}) async-start(s8[5767168]{0:T(1024)(128)(4,1)} %bitcast.204), calls=%async_computation.3 | async-start | bytes 8388608
  106.8 8.9 %copy-start.34 = (bf16[1024,1024]{1,0:T(8,128)(2,1)}, bf16[1024,1024]{1,0:T(8,128)(2,1)S(1)}, u32[]{:S(2)}) copy-start(bf16[1024,1024]{1,0:T(8,128)(2,1)S(1)} %multiply_convert_fusion.6) | copy-start | bytes 6291460
  106.8 8.9 %slice-start.4 = ((s8[5767168]{0:T(1024)(128)(4,1)}), s8[1572864]{0:T(1024)(128)(4,1)S(1)}, s32[]{:S(2)}) async-start(s8[5767168]{0:T(1024)(128)(4,1)} %bitcast.204), calls=%async_computation.4 | async-start | bytes 3145728
  142.8 11.6 %copy-start.18 = (bf16[1024,2816]{1,0:T(8,128)(2,1)S(1)}, bf16[1024,2816]{1,0:T(8,128)(2,1)}, u32[]{:S(2)}) copy-start(bf16[1024,2816]{1,0:T(8,128)(2,1)} %get-tuple-element.24) | copy-start | bytes 17301508
  154.4 9.7 %copy-start.14 = (f32[1024,1024]{1,0:T(8,128)S(1)}, f32[1024,1024]{1,0:T(8,128)}, u32[]{:S(2)}) copy-start(f32[1024,1024]{1,0:T(8,128)} %copy-done.13) | copy-start | bytes 12582916
  154.4 9.7 %copy-start.19 = (bf16[1024,2816]{1,0:T(8,128)(2,1)S(1)}, bf16[1024,2816]{1,0:T(8,128)(2,1)}, u32[]{:S(2)}) copy-start(bf16[1024,2816]{1,0:T(8,128)(2,1)} %get-tuple-element.22) | copy-start | bytes 17301508
  164.1 9.3 %copy-start.11 = (bf16[8,128,1024]{2,1,0:T(8,128)(2,1)S(1)}, bf16[8,128,1024]{2,1,0:T(8,128)(2,1)}, u32[]{:S(2)}) copy-start(bf16[8,128,1024]{2,1,0:T(8,128)(2,1)} %param.12) | copy-start | bytes 6291460
  175.0 10.0 %copy-start.15 = (f32[1024,1024]{1,0:T(8,128)}, f32[1024,1024]{1,0:T(8,128)S(1)}, u32[]{:S(2)}) copy-start(f32[1024,1024]{1,0:T(8,128)S(1)} %subtract_add_fusion) | copy-start | bytes 12582916
  272.9 19.1 %copy-start.43 = (bf16[1024,1024]{1,0:T(8,128)(2,1)S(1)}, bf16[1024,1024]{1,0:T(8,128)(2,1)}, u32[]{:S(2)}) copy-start(bf16[1024,1024]{1,0:T(8,128)(2,1)} %param.15) | copy-start | bytes 6291460
  292.0 5.9 copy-start.29
  292.1 7.1 copy-start.30
  314.1 8.5 %copy-start.12 = (bf16[8,128,1024]{2,1,0:T(8,128)(2,1)S(1)}, bf16[8,128,1024]{2,1,0:T(8,128)(2,1)}, u32[]{:S(2)}) copy-start(bf16[8,128,1024]{2,1,0:T(8,128)(2,1)} %param.12) | copy-start | bytes 6291460
  336.6 11.1 %copy-start.35 = (bf16[1024,1024]{1,0:T(8,128)(2,1)S(1)}, bf16[1024,1024]{1,0:T(8,128)(2,1)}, u32[]{:S(2)}) copy-start(bf16[1024,1024]{1,0:T(8,128)(2,1)} %copy-done.34) | copy-start | bytes 6291460
  442.7 18.0 %copy-start.17 = (f32[1024,1024]{1,0:T(8,128)S(1)}, f32[1024,1024]{1,0:T(8,128)}, u32[]{:S(2)}) copy-start(f32[1024,1024]{1,0:T(8,128)} %copy-done.15) | copy-start | bytes 12582916
  442.7 18.0 %copy-start.50 = (bf16[1024,1024]{1,0:T(8,128)(2,1)S(1)}, bf16[1024,1024]{1,0:T(8,128)(2,1)}, u32[]{:S(2)}) copy-start(bf16[1024,1024]{1,0:T(8,128)(2,1)} %copy-done.49) | copy-start | bytes 6291460
  789.4 6.5 copy-start.41
  789.4 26.4 %copy-start.48 = (u32[32]{0:T(128)S(1)}, u32[32]{0:T(128)}, u32[]{:S(2)}) copy-start(u32[32]{0:T(128)} %constant.43) | copy-start | bytes 388
  830.2 8.2 copy-start.1
  (32 other events, 95.7 us)

commit v2 on v1

v2 whole, which is shorter than its diff:
```python
import functools

import jax
import jax.numpy as jnp
from jax import lax
from jax.experimental import pallas as pl
from jax.experimental.pallas import tpu as pltpu
from jax.sharding import PartitionSpec as P

HEAD = 64
EPS = 1e-06
MESH = pl.DeviceIdType.MESH
F32 = jnp.float32
BF16 = jnp.bfloat16
MIB = 2**20


def silu_parts(pre):
    sig = jax.nn.sigmoid(pre)
    return (pre * sig, sig * (1.0 + pre * (1.0 - sig)))


def norm_back(grad, value, scale):
    inner = jnp.mean(grad * value, axis=-1, keepdims=True)
    return scale * grad - value * (scale * scale * scale) * inner


def project(left, weight):
    return jnp.dot(left, weight, preferred_element_type=F32)


def weight_grad(left, right):
    return jnp.einsum("td,tf->df", left, right, preferred_element_type=F32)


def back_project(grad, weight):
    return jnp.einsum("tf,df->td", grad, weight, preferred_element_type=F32)


def dot(a, b, ca, cb):
    return lax.dot_general(a, b, (((ca,), (cb,)), ((), ())), preferred_element_type=F32)


def low_lanes(shape):
    return lax.broadcasted_iota(jnp.int32, shape, len(shape) - 1) < HEAD


def two_heads(x):
    low = low_lanes(x.shape)
    zero = jnp.zeros_like(x)
    return jnp.concatenate([jnp.where(low, x, zero), jnp.where(low, zero, x)], axis=0)


def pick_heads(x):
    half = x.shape[0] // 2
    return jnp.where(low_lanes((half, x.shape[1])), x[:half], x[half:])


def causal_pair(span):
    t = lax.broadcasted_iota(jnp.int32, (span, 2 * span), 0)
    u = lax.broadcasted_iota(jnp.int32, (span, 2 * span), 1)
    return t >= u % span


def pair_of(ref, p):
    return ref[:, pl.ds(p * 2 * HEAD, 2 * HEAD)]


def state_kernel(left_ref, right_ref, out_ref):
    for p in range(out_ref.shape[1]):
        out_ref[0, p] = pick_heads(dot(pair_of(left_ref, p), pair_of(right_ref, p), 0, 0))


def attn_kernel(q_ref, k_ref, v_ref, prefix_ref, out_ref):
    span = q_ref.shape[0]
    causal = causal_pair(span)
    for p in range(prefix_ref.shape[1]):
        q, k2, v2 = pair_of(q_ref, p), two_heads(pair_of(k_ref, p)), two_heads(pair_of(v_ref, p))
        scores = jnp.where(causal, dot(q, k2, 1, 1), 0.0).astype(BF16)
        prefix = two_heads(prefix_ref[0, p])
        out_ref[:, pl.ds(p * 2 * HEAD, 2 * HEAD)] = dot(scores, v2, 1, 0) + dot(q, prefix, 1, 0)


def attn_back_kernel(q_ref, k_ref, v_ref, g_ref, prefix_ref, dstate_ref, dq_ref, dk_ref, dv_ref):
    span = q_ref.shape[0]
    causal = causal_pair(span)
    for p in range(prefix_ref.shape[1]):
        q, k, v, g = (pair_of(r, p) for r in (q_ref, k_ref, v_ref, g_ref))
        k2, v2 = two_heads(k), two_heads(v)
        prefix, dstate = two_heads(prefix_ref[0, p]), two_heads(dstate_ref[0, p])
        scores = jnp.where(causal, dot(q, k2, 1, 1), 0.0).astype(BF16)
        dscores = jnp.where(causal, dot(g, v2, 1, 1), 0.0).astype(BF16)
        lanes = pl.ds(p * 2 * HEAD, 2 * HEAD)
        dq_ref[:, lanes] = dot(dscores, k2, 1, 0) + dot(g, prefix, 1, 1)
        dk_ref[:, lanes] = pick_heads(dot(dscores, q, 0, 0)) + dot(v, dstate, 1, 1)
        dv_ref[:, lanes] = pick_heads(dot(scores, g, 0, 0)) + dot(k, dstate, 1, 0)


def rows_spec(span, width):
    return pl.BlockSpec((span, width), lambda s: (s, 0))


def state_spec(pairs):
    return pl.BlockSpec((1, pairs, HEAD, 2 * HEAD), lambda s: (s, 0, 0, 0))


def local_states(left, right, seqs):
    rows, width = left.shape
    span, pairs = rows // seqs, width // (2 * HEAD)
    return pl.pallas_call(
        state_kernel,
        grid=(seqs,),
        in_specs=[rows_spec(span, width)] * 2,
        out_specs=state_spec(pairs),
        out_shape=jax.ShapeDtypeStruct((seqs, pairs, HEAD, 2 * HEAD), F32),
    )(left, right)


def attention(q, k, v, prefix, seqs):
    rows, width = q.shape
    span, pairs = rows // seqs, width // (2 * HEAD)
    return pl.pallas_call(
        attn_kernel,
        grid=(seqs,),
        in_specs=[rows_spec(span, width)] * 3 + [state_spec(pairs)],
        out_specs=rows_spec(span, width),
        out_shape=jax.ShapeDtypeStruct((rows, width), F32),
    )(q, k, v, prefix)


def attention_back(q, k, v, g, prefix, dstate, seqs):
    rows, width = q.shape
    span, pairs = rows // seqs, width // (2 * HEAD)
    return pl.pallas_call(
        attn_back_kernel,
        grid=(seqs,),
        in_specs=[rows_spec(span, width)] * 4 + [state_spec(pairs)] * 2,
        out_specs=[rows_spec(span, width)] * 3,
        out_shape=[jax.ShapeDtypeStruct((rows, width), F32)] * 3,
    )(q, k, v, g, prefix, dstate)


def scan_kernel(outer, reverse, s_ref, out_ref, held, summed, other, zs, zr, xs, xr):
    chunks = s_ref.shape[0]
    k = lax.axis_index("blk")
    z, x = k // 2, k % 2
    if reverse:
        zz, xx = outer - 1 - z, 1 - x
        after, before = jnp.maximum(z - 1, 0), jnp.minimum(z + 1, outer - 1)
    else:
        zz, xx = z, x
        after, before = jnp.minimum(z + 1, outer - 1), jnp.maximum(z - 1, 0)
    nxt, prv, side = {"blk": after * 2 + x}, {"blk": before * 2 + x}, {"blk": z * 2 + 1 - x}
    first, last = zz == 0, zz == outer - 1

    bar = pltpu.get_barrier_semaphore()
    pl.semaphore_signal(bar, inc=1, device_id=side, device_id_type=MESH)
    pl.when(~last)(lambda: pl.semaphore_signal(bar, inc=1, device_id=nxt, device_id_type=MESH))
    pl.when(~first)(lambda: pl.semaphore_signal(bar, inc=1, device_id=prv, device_id_type=MESH))
    pl.semaphore_wait(bar, 1 + jnp.where(last, 0, 1) + jnp.where(first, 0, 1))

    def along(i):
        return pltpu.make_async_remote_copy(
            src_ref=summed.at[i], dst_ref=held.at[i], send_sem=zs.at[i], recv_sem=zr.at[i],
            device_id=nxt, device_id_type=MESH)

    def across(i, src):
        return pltpu.make_async_remote_copy(
            src_ref=src.at[i], dst_ref=other.at[i], send_sem=xs.at[i], recv_sem=xr.at[i],
            device_id=side, device_id_type=MESH)

    def pass_on(i):
        pl.when(~first)(lambda: along(i).wait_recv())

        @pl.when(first)
        def _():
            held[i] = jnp.zeros_like(held[i])

        summed[i] = held[i] + s_ref[i]
        pl.when(~last)(lambda: along(i).start())
        pl.when(xx == 0)(lambda: across(i, summed).start())
        pl.when(xx == 1)(lambda: across(i, held).start())

    def finish(i):
        across(i, held).wait_recv()
        out_ref[i] = (held[i] + other[i]).astype(out_ref.dtype)

    def step(i, carry):
        pl.when(i < chunks)(lambda: pass_on(i))
        pl.when(i > 0)(lambda: finish(i - 1))
        return carry

    lax.fori_loop(0, chunks + 1, step, 0)

    def drain(i, carry):
        pl.when(~last)(lambda: along(i).wait_send())
        across(i, held).wait_send()
        return carry

    lax.fori_loop(0, chunks, drain, 0)


def entering(states, blk, reverse):
    seqs, pairs, head, lanes = states.shape
    per = max(1, pairs // 2)
    shape = (seqs * pairs // per, per, head, lanes)
    vmem = pl.BlockSpec(memory_space=pltpu.VMEM)
    sems = [pltpu.SemaphoreType.DMA((shape[0],))] * 4
    out = pl.pallas_call(
        functools.partial(scan_kernel, blk // 2, reverse),
        out_shape=jax.ShapeDtypeStruct(shape, BF16),
        in_specs=[vmem],
        out_specs=vmem,
        scratch_shapes=[pltpu.VMEM(shape, F32)] * 3 + sems,
        compiler_params=pltpu.CompilerParams(
            collective_id=2 if reverse else 1, has_side_effects=True, vmem_limit_bytes=24 * MIB),
    )(states.reshape(shape))
    return out.reshape(states.shape)


LAND, FIN, ACC = 4, 8, 10
CORE, XA, YA, YB, XB, XC, YC = range(7)
TILE = 256


class Named:
    def __init__(self, names, refs):
        self.__dict__.update(zip(names, refs))


class Stream:
    def __init__(self, block, buf, sem):
        self.block, self.buf, self.sem = block, buf, sem

    def copy(self, j):
        return pltpu.make_async_copy(self.block(j), self.buf.at[j % 2], self.sem.at[j % 2])

    def start(self, j):
        self.copy(j).start()

    def get(self, j, count):
        self.copy(j).wait()
        pl.when(j + 1 < count)(lambda: self.start(j + 1))
        return self.buf.at[j % 2]


BACK_IN = (
    "tokens", "dy", "innert", "inner", "first", "second", "resid", "gate", "attn", "q", "k", "v",
    "query", "key", "prefix", "normt", "norm2t", "mixedt", "gain", "w_query", "w_key", "w_value",
    "w_gate", "w_out", "w_first", "w_second", "w_third",
)
BACK_OUT = (
    "output", "dtokens", "tall", "wide", "square", "dgain",
)
BACK_SCRATCH = (
    "tbuf", "core_rx", "acc", "xa", "ya", "yb", "xb", "xc", "yc", "zab", "zc", "fin", "ssem",
    "rsem", "zss", "zrs", "osem", "csem", "crem", "ygs", "ygr", "dyv", "dfs", "dn2", "dlow",
    "dgate", "dattn", "at0", "at1", "held", "sums", "other", "dstate", "sz", "rz", "sx", "rx",
    "gacc", "gbuf", "gland", "gs", "gr", "lsem",
)


def back_kernel(outer, seqs, *refs):
    r = Named(BACK_IN + BACK_OUT + BACK_SCRATCH, refs)
    rows, width = r.tokens.shape
    ff = r.first.shape[1]
    span, pairs = rows // seqs, width // (2 * HEAD)
    n_tall, n_wide, n_square = ff // 256, ff // 128, 20
    chunks = n_tall + n_wide + n_square
    at_wide, at_square = n_tall, n_tall + n_wide
    blocks = rows // TILE

    b, k = lax.axis_index("batch"), lax.axis_index("blk")
    y, c = b // 2, b % 2
    z, x = k // 2, k % 2
    ox, oy = 1 - x, 1 - y
    top = outer - 1
    zr = top - z
    to_core, to_y, to_x = {"batch": y * 2 + 1 - c}, {"batch": oy * 2 + c}, {"blk": z * 2 + ox}
    to_up = {"blk": jnp.minimum(z + 1, top) * 2 + x}
    to_down = {"blk": jnp.maximum(z - 1, 0) * 2 + x}
    to_z = [{"blk": (z + d) % outer * 2 + x} for d in range(1, outer)]

    peers = [to_core, to_y, to_x] + to_z
    bar = pltpu.get_barrier_semaphore()
    for d in peers:
        pl.semaphore_signal(bar, inc=1, device_id=d, device_id_type=MESH)
    pl.semaphore_wait(bar, len(peers))

    def remote(src, dst, s, t, dev):
        return pltpu.make_async_remote_copy(
            src_ref=src, dst_ref=dst, send_sem=s, recv_sem=t, device_id=dev, device_id_type=MESH)

    def link(kind, i, src, dst, dev):
        return remote(src, dst.at[i % LAND], r.ssem.at[kind, i % LAND], r.rsem.at[kind, i % LAND], dev)

    def at(i, *where):
        return r.acc.at[(i % ACC,) + where]

    A, B, C = pl.ds(0, 32), pl.ds(32, 16), pl.ds(48, 16)
    every = slice(None)

    def core_copy(i):
        return link(CORE, i, r.tbuf.at[i % 2], r.core_rx, to_core)

    def xa_copy(i):
        return link(XA, i, at(i, every, ox, every, A), r.xa, to_x)

    def ya_copy(i):
        return link(YA, i, at(i, every, x, oy, A), r.ya, to_y)

    def yb_copy(i):
        return link(YB, i, at(i, every, every, oy, B), r.yb, to_y)

    def xb_copy(i):
        return link(XB, i, at(i, every, ox, y, B), r.xb, to_x)

    def xc_copy(i):
        return link(XC, i, at(i, z, ox, every, C), r.xc, to_x)

    def yc_copy(i):
        return link(YC, i, at(i, z, x, oy, C), r.yc, to_y)

    def y_share(i):
        f = i % FIN
        return remote(r.fin.at[f, y], r.fin.at[f, y], r.ygs.at[f], r.ygr.at[f], to_y)

    def part_ab(i, s):
        return at(i, s, x, y, pl.ds(0, 48))

    def part_c(i, s):
        return at(i, s, every, every, C)

    AB, CC = (0, part_ab, r.zab), (1, part_c, r.zc)

    def hop(group, i, n, up, s):
        g, part, land = group
        d = 0 if up else 1
        sem = (g, d, n - 1, i % LAND)
        return remote(part(i, s), land.at[i % LAND, d, n - 1], r.zss.at[sem], r.zrs.at[sem],
                      to_up if up else to_down)

    def z_each(group, i, n, act):
        up = hop(group, i, n, True, jnp.minimum(outer - n + z, top))
        down = hop(group, i, n, False, jnp.maximum(n - 1 - zr, 0))
        pl.when((z <= n - 1) & (z < top))(lambda: act(up))
        pl.when((zr <= n - 1) & (z > 0))(lambda: act(down))

    def z_send(group, i, n):
        z_each(group, i, n, lambda copy: copy.start())

    def z_sent(group, i, n):
        z_each(group, i, n, lambda copy: copy.wait_send())

    def add(ref, landed):
        ref[...] = ref[...] + landed

    def z_take(group, i, n):
        g, part, land = group

        def take(up, s):
            hop(group, i, n, up, s).wait_recv()
            add(part(i, s), land[i % LAND, 0 if up else 1, n - 1])

        pl.when((z > 0) & (z <= n))(lambda: take(True, jnp.clip(outer - n + z - 1, 0, top)))
        pl.when((z < top) & (zr <= n))(lambda: take(False, jnp.clip(n - zr, 0, top)))

    def places(i, act):
        f = r.fin.at[i % FIN]

        @pl.when(i < at_wide)
        def _():
            for yy in range(2):
                for blk in range(2):
                    col = pl.multiple_of(c * (width // 2) + (yy * 2 + blk) * 128, 128)
                    act(f.at[yy, pl.ds(blk * 32, 32)], r.tall.at[pl.ds(i * 32, 32), pl.ds(col, 128)])

        @pl.when((i >= at_wide) & (i < at_square))
        def _():
            j, h = (i - at_wide) // 2, (i - at_wide) % 2
            col = pl.multiple_of(c * (ff // 2) + j * 128, 128)
            for yy in range(2):
                act(f.at[yy], r.wide.at[yy, pl.ds(h * 64, 64), pl.ds(col, 128)])

        @pl.when(i >= at_square)
        def _():
            j = i - at_square
            m, u, h = j // 4, j // 2 % 2, j % 2
            for yy in range(2):
                col = pl.multiple_of(c * (width // 2) + u * 256 + yy * 128, 128)
                act(f.at[yy], r.square.at[m, pl.ds(h * 64, 64), pl.ds(col, 128)])

    def cores(i):
        core_copy(i).wait_recv()
        core_copy(i).wait_send()
        add(at(i), r.core_rx[i % LAND])
        xa_copy(i).start()
        yb_copy(i).start()
        z_send(CC, i, 1)

    def second(i):
        yb_copy(i).wait_recv()
        add(at(i, every, every, y, B), r.yb[i % LAND])
        xb_copy(i).start()
        xa_copy(i).wait_recv()
        add(at(i, every, x, every, A), r.xa[i % LAND])
        ya_copy(i).start()
        z_take(CC, i, 1)
        z_send(CC, i, 2)
        xa_copy(i).wait_send()
        yb_copy(i).wait_send()
        z_sent(CC, i, 1)

    def third(i):
        xb_copy(i).wait_recv()
        add(at(i, every, x, y, B), r.xb[i % LAND])
        ya_copy(i).wait_recv()
        add(at(i, every, x, y, A), r.ya[i % LAND])
        z_send(AB, i, 1)
        z_take(CC, i, 2)
        z_send(CC, i, 3)
        xb_copy(i).wait_send()
        ya_copy(i).wait_send()
        z_sent(CC, i, 2)

    def fourth(i):
        z_take(AB, i, 1)
        z_send(AB, i, 2)
        z_take(CC, i, 3)
        xc_copy(i).start()
        z_sent(AB, i, 1)
        z_sent(CC, i, 3)

    def fifth(i):
        z_take(AB, i, 2)
        z_send(AB, i, 3)
        xc_copy(i).wait_recv()
        add(at(i, z, x, every, C), r.xc[i % LAND])
        yc_copy(i).start()
        z_sent(AB, i, 2)
        xc_copy(i).wait_send()

    def sixth(i):
        yc_copy(i).wait_recv()
        z_take(AB, i, 3)
        f = i % FIN
        r.fin[f, y, pl.ds(0, 48)] = r.acc[i % ACC, z, x, y, pl.ds(0, 48)]
        r.fin[f, y, C] = r.acc[i % ACC, z, x, y, C] + r.yc[i % LAND]
        y_share(i).start()
        z_sent(AB, i, 3)
        yc_copy(i).wait_send()

    def seventh(i):
        y_share(i).wait_recv()
        y_share(i).wait_send()
        f = i % FIN

        def go(src, dst):
            remote(src, dst, r.csem.at[f], r.crem.at[f], to_core).start()
            pltpu.make_async_copy(src, dst, r.osem.at[f]).start()

        places(i, go)

    def last(i):
        f = i % FIN
        whole = r.fin.at[f]
        copy = remote(whole, whole, r.csem.at[f], r.crem.at[f], to_core)
        copy.wait_send()
        copy.wait_recv()
        pltpu.make_async_copy(whole, whole, r.osem.at[f]).wait()

    stages = (None, cores, second, third, fourth, fifth, sixth, seventh, last)

    def move(t):
        for n, stage in enumerate(stages):
            if stage is not None:
                i = t - n
                pl.when((i >= 0) & (i < chunks))(functools.partial(stage, i))

    def make(t, fill):
        fill(1 - c, r.tbuf.at[t % 2])
        core_copy(t).start()
        fill(c, r.acc.at[t % ACC])

    def fill_tall(lhs):
        def fill(half, dst):
            for yy in range(2):
                col = pl.multiple_of(half * (width // 2) + yy * 256, 256)
                res = dot(lhs, r.dyv[:, pl.ds(col, 256)], 1, 0).reshape(4, 2, 32, 256)
                for blk in range(2):
                    dst[:, :, yy, pl.ds(blk * 32, 32), :] = res[..., blk * 128:(blk + 1) * 128]
        return fill

    def left_rows(ref, h):
        return ref[:, h].reshape(8 * 64, rows)

    def fill_two(left, h, take):
        def fill(half, dst):
            res = dot(left_rows(left, h), take(half), 1, 0).reshape(4, 2, 64, 256)
            dst[:, :, 0] = res[..., :128]
            dst[:, :, 1] = res[..., 128:]
        return fill

    def make_wide(t):
        i = t - at_wide
        j, h = i // 2, i % 2

        def take(half):
            col = pl.ds(pl.multiple_of(half * (ff // 2) + j * 128, 128), 128)
            return jnp.concatenate([r.dfs[0, :, col], r.dfs[1, :, col]], axis=1)

        make(t, fill_two(r.at0, h, take))

    def make_square(t, base, left, right):
        i = t - base
        u, h = i // 2, i % 2

        def take(half):
            return right(pl.ds(pl.multiple_of(half * (width // 2) + u * 256, 256), 256))

        make(t, fill_two(left, h, take))

    zz, xx = zr, ox
    n_scan = r.sums.shape[0]
    halves = n_scan // seqs
    scan_at = at_wide + 1

    def along(i):
        return remote(r.sums.at[i], r.held.at[i], r.sz.at[i], r.rz.at[i], to_down)

    def across(i, src):
        return remote(src.at[i], r.other.at[i], r.sx.at[i], r.rx.at[i], to_x)

    def pass_on(i):
        pl.when(zz > 0)(lambda: along(i).wait_recv())

        @pl.when(zz == 0)
        def _():
            r.held[i] = jnp.zeros_like(r.held[i])

        r.sums[i] = r.held[i] + r.sums[i]
        pl.when(zz < top)(lambda: along(i).start())
        pl.when(xx == 0)(lambda: across(i, r.sums).start())
        pl.when(xx == 1)(lambda: across(i, r.held).start())

    def finish(i):
        across(i, r.held).wait_recv()
        r.dstate[i] = (r.held[i] + r.other[i]).astype(BF16)
        pl.when(zz < top)(lambda: along(i).wait_send())
        across(i, r.held).wait_send()

    def scan(t):
        i = t - scan_at - zz
        pl.when((i >= 0) & (i < n_scan))(lambda: pass_on(i))
        pl.when((i >= 2) & (i < n_scan + 2))(lambda: finish(i - 2))

    def tok(j, n=TILE):
        return pl.ds(pl.multiple_of(j * n, n), n)

    def tile_inner(j, w3, w1, w2, first, second):
        def block(m, carry):
            at_rows = tok(m, 512)
            din = dot(r.dyv[at_rows, :], w3[...], 1, 1)
            one = (din * second[at_rows, :].astype(F32)).astype(BF16)
            two = (din * first[at_rows, :].astype(F32)).astype(BF16)
            cols = pl.ds(pl.multiple_of(j * 256, 256), 256)
            r.dfs[0, at_rows, cols] = one
            r.dfs[1, at_rows, cols] = two
            for n in range(width // 256):
                to = pl.ds(n * 256, 256)
                res = dot(one, w1[to, :], 1, 1) + dot(two, w2[to, :], 1, 1)
                r.dn2[at_rows, to] = r.dn2[at_rows, to] + res
            return carry

        lax.fori_loop(0, rows // 512, block, 0)

    def tile_resid(j, resid, gate, attn, q, w_out, gain, dmix):
        def one(m, carry):
            here, sub = pl.ds(pl.multiple_of(j * TILE + m * 32, 32), 32), tok(m, 32)
            value = resid[sub, :]
            grad = r.dn2[here, :]
            scale = lax.rsqrt(jnp.mean(value * value, axis=-1, keepdims=True) + EPS)
            out = r.dyv[here, :].astype(F32) + norm_back(grad, value, scale)
            r.dn2[here, :] = out
            r.dlow[here, :] = out.astype(BF16)
            return carry

        lax.fori_loop(0, TILE // 32, one, 0)
        for n in range(width // 256):
            to = pl.ds(n * 256, 256)
            dmix[:, to] = dot(r.dlow[tok(j), :], w_out[to, :], 1, 1)

        def two(m, carry):
            here, sub = pl.ds(pl.multiple_of(j * TILE + m * 32, 32), 32), tok(m, 32)
            av = attn[sub, :].astype(F32)
            scale = lax.rsqrt(jnp.mean(av * av, axis=-1, keepdims=True) + EPS)
            unit = av * scale
            act, der = silu_parts(gate[sub, :].astype(F32))
            dm = dmix[sub, :]
            ds = dm * act
            r.dgate[here, :] = (dm * (unit * gain[...]) * der).astype(BF16)
            r.gacc[...] = r.gacc[...] + jnp.sum((ds * unit).reshape(4, 8, width), axis=0)
            r.dattn[here, :] = norm_back(ds * gain[...], av, scale).astype(BF16)
            return carry

        lax.fori_loop(0, TILE // 32, two, 0)

        def states(m, carry):
            s = j * (TILE // span) + m
            for p in range(pairs):
                lanes = pl.ds(p * 2 * HEAD, 2 * HEAD)
                grad = r.dattn[tok(s, span), lanes]
                per = pairs // halves
                r.sums[s * halves + p // per, p % per] = pick_heads(dot(q[tok(m, span), lanes], grad, 0, 0))
            return carry

        lax.fori_loop(0, TILE // span, states, 0)

    def tile_attn(s, q_ref, k_ref, v_ref, query, key, prefix_ref):
        causal = causal_pair(span)
        here = tok(s, span)
        for p in range(pairs):
            lanes = pl.ds(p * 2 * HEAD, 2 * HEAD)
            q, k, v, g = q_ref[:, lanes], k_ref[:, lanes], v_ref[:, lanes], r.dattn[here, lanes]
            k2, v2 = two_heads(k), two_heads(v)
            per = pairs // halves
            prefix, dstate = two_heads(prefix_ref[p]), two_heads(r.dstate[s * halves + p // per, p % per])
            scores = jnp.where(causal, dot(q, k2, 1, 1), 0.0).astype(BF16)
            dscores = jnp.where(causal, dot(g, v2, 1, 1), 0.0).astype(BF16)
            dq = dot(dscores, k2, 1, 0) + dot(g, prefix, 1, 1)
            dk = pick_heads(dot(dscores, q, 0, 0)) + dot(v, dstate, 1, 1)
            dv = pick_heads(dot(scores, g, 0, 0)) + dot(k, dstate, 1, 0)
            r.dfs[0, here, lanes] = (dq * silu_parts(query[:, lanes].astype(F32))[1]).astype(BF16)
            r.dfs[0, here, pl.ds(width + p * 2 * HEAD, 2 * HEAD)] = (
                dk * silu_parts(key[:, lanes].astype(F32))[1]).astype(BF16)
            r.dfs[1, here, lanes] = dv.astype(BF16)

    parts = [
        lambda at_rows, cols: r.dfs[0, at_rows, cols],
        lambda at_rows, cols: r.dfs[0, at_rows, pl.ds(width + cols.start, cols.size)],
        lambda at_rows, cols: r.dfs[1, at_rows, cols],
    ]
    dq_cols = lambda cols: r.dfs[0, :, cols]
    dk_cols = lambda cols: r.dfs[0, :, pl.ds(width + cols.start, cols.size)]
    dv_cols = lambda cols: r.dfs[1, :, cols]

    def load(src, dst, n):
        return pltpu.make_async_copy(src, dst, r.lsem.at[n])

    def dma(*shape):
        return pltpu.SemaphoreType.DMA(shape)

    def ring(shape, dtype):
        return pltpu.VMEM((2,) + shape, dtype)

    def steps(count, one):
        def go(j, carry):
            one(j)
            return carry

        lax.fori_loop(0, count, go, 0)

    dy_load = load(r.dy, r.dyv, 0)
    norm2_load = load(r.norm2t, r.at0, 1)
    mixed_load = load(r.mixedt, r.at1, 2)
    norm_load = load(r.normt, r.at0, 3)

    def segment0(left, w3, w1, w2, first, second, sems):
        cols = lambda ref: lambda j: ref.at[:, pl.ds(pl.multiple_of(j * 256, 256), 256)]
        s_left = Stream(lambda j: r.innert.at[:, pl.ds(pl.multiple_of(j * 32, 32), 32)], left, sems.at[0])
        tiles = [
            Stream(lambda j: r.w_third.at[pl.ds(pl.multiple_of(j * 256, 256), 256)], w3, sems.at[1]),
            Stream(cols(r.w_first), w1, sems.at[2]),
            Stream(cols(r.w_second), w2, sems.at[3]),
            Stream(cols(r.first), first, sems.at[4]),
            Stream(cols(r.second), second, sems.at[5]),
        ]
        dy_load.start()
        s_left.start(0)
        for s in tiles:
            s.start(0)
        norm2_load.start()
        r.dn2[...] = jnp.zeros_like(r.dn2)
        r.gacc[...] = jnp.zeros_like(r.gacc)
        dy_load.wait()

        def one(j):
            move(j)
            make(j, fill_tall(s_left.get(j, n_tall)[...].reshape(8 * 32, rows)))
            tile_inner(j, *(s.get(j, n_tall) for s in tiles))

        steps(n_tall, one)
        norm2_load.wait()

    pl.run_scoped(
        segment0, ring((8, 32, rows), BF16), ring((256, width), BF16), ring((width, 256), BF16),
        ring((width, 256), BF16), ring((rows, 256), BF16), ring((rows, 256), BF16), dma(6, 2))

    def segment1(resid, gate, attn, q, w_out, gain, dmix, sems, wsem):
        blk = lambda ref: lambda j: ref.at[tok(j)]
        tiles = [
            Stream(blk(ref), buf, sems.at[n])
            for n, (ref, buf) in enumerate(((r.resid, resid), (r.gate, gate), (r.attn, attn), (r.q, q)))
        ]
        w_load = pltpu.make_async_copy(r.w_out, w_out, wsem.at[0])
        g_load = pltpu.make_async_copy(r.gain, gain, wsem.at[1])
        w_load.start()
        g_load.start()
        for s in tiles:
            s.start(0)
        w_load.wait()
        g_load.wait()

        def one(j):
            t = at_wide + j
            move(t)
            scan(t)
            make_wide(t)
            rs, ga, at_, qs = (s.get(j, blocks) for s in tiles)
            tile_resid(j, rs, ga, at_, qs, w_out, gain, dmix)

        steps(blocks, one)

    pl.run_scoped(
        segment1, ring((TILE, width), F32), ring((TILE, width), BF16), ring((TILE, width), BF16),
        ring((TILE, width), BF16), pltpu.VMEM((width, width), BF16), pltpu.VMEM((1, width), F32),
        pltpu.VMEM((TILE, width), F32), dma(4, 2), dma(2))

    def gain_sum(t):
        base = at_wide + blocks
        hops = [to_core, to_y, to_x]

        def swap(n):
            return remote(r.gbuf, r.gland.at[n], r.gs.at[n], r.gr.at[n], hops[n])

        def spread(d):
            return remote(r.gbuf, r.gland.at[2 + d], r.gs.at[2 + d], r.gr.at[2 + d], to_z[d - 1])

        @pl.when(t == base)
        def _():
            total = jnp.sum(r.gacc[...], axis=0, keepdims=True)
            for n in range(8):
                r.gbuf[pl.ds(n, 1), :] = total[:, n * 128:(n + 1) * 128]
            swap(0).start()

        for n in range(3):
            @pl.when(t == base + 2 + 2 * n)
            def _(n=n):
                swap(n).wait()
                r.gbuf[...] = r.gbuf[...] + r.gland[n]
                if n < 2:
                    swap(n + 1).start()
                else:
                    for d in range(1, outer):
                        spread(d).start()

        @pl.when(t == base + 8)
        def _():
            for d in range(1, outer):
                spread(d).wait()
            for d in range(1, outer):
                r.gbuf[...] = r.gbuf[...] + r.gland[2 + d]
            pltpu.make_async_copy(r.gbuf, r.dgain, r.lsem.at[4]).start()

        pl.when(t == base + 10)(lambda: pltpu.make_async_copy(r.gbuf, r.dgain, r.lsem.at[4]).wait())

    n2 = n_wide - blocks
    n_out = blocks * (width // 256)

    def segment2(w3, inner, resid, out, sems, osem):
        per = width // 256
        cols = lambda j: pl.ds(pl.multiple_of(j % per * 256, 256), 256)
        s_w3 = Stream(lambda j: r.w_third.at[:, cols(j)], w3, sems.at[0])
        s_resid = Stream(lambda j: r.resid.at[tok(j // per), cols(j)], resid, sems.at[1])
        s_inner = Stream(lambda n: r.inner.at[tok(n)], inner, sems.at[2])

        def store(j):
            return pltpu.make_async_copy(out.at[j % 2], r.output.at[tok(j // per), cols(j)], osem.at[j % 2])

        mixed_load.start()
        for s in (s_w3, s_resid, s_inner):
            s.start(0)

        def one(j):
            t = at_wide + blocks + j
            move(t)
            scan(t)
            gain_sum(t)
            make_wide(t)

            @pl.when(j < n_out)
            def _():
                w, res = s_w3.get(j, n_out), s_resid.get(j, n_out)

                @pl.when(j % per == 0)
                def _():
                    s_inner.get(j // per, blocks)

                pl.when(j >= 2)(lambda: store(j - 2).wait())
                prod = dot(inner[j // per % 2], w[...], 1, 0)
                out[j % 2] = (res[...] + prod).astype(BF16)
                store(j).start()

        steps(n2, one)
        store(n_out - 2).wait()
        store(n_out - 1).wait()
        mixed_load.wait()

    pl.run_scoped(
        segment2, ring((ff, 256), BF16), ring((TILE, ff), BF16), ring((TILE, 256), F32),
        ring((TILE, 256), BF16), dma(3, 2), dma(2))

    def segment3(q, k, v, query, key, prefix, sems):
        blk = lambda ref: lambda j: ref.at[tok(j, span)]
        tiles = [
            Stream(blk(ref), buf, sems.at[n])
            for n, (ref, buf) in enumerate(((r.q, q), (r.k, k), (r.v, v), (r.query, query), (r.key, key)))
        ]
        tiles.append(Stream(lambda j: r.prefix.at[j], prefix, sems.at[5]))
        norm_load.start()
        for s in tiles:
            s.start(0)

        def one(j):
            t = at_square + j
            move(t)
            scan(t)
            pl.when(j < 4)(lambda: make_square(t, at_square, r.at1, lambda cols: r.dlow[:, cols]))
            pl.when(j == 4)(lambda: norm_load.wait())
            pl.when(j >= 4)(lambda: make_square(t, at_square + 4, r.at0, lambda cols: r.dgate[:, cols]))
            tile_attn(j, *(s.get(j, seqs) for s in tiles))

        steps(8, one)

    pl.run_scoped(
        segment3, *[ring((span, width), BF16)] * 5, ring((pairs, HEAD, 2 * HEAD), BF16), dma(6, 2))

    def segment4(wq, wk, wv, wg, total, xs, out, sems, xsem, osem):
        nn = width // 256
        rowsblk = lambda ref: lambda n: ref.at[pl.ds(pl.multiple_of(n * 256, 256), 256)]
        weights = [
            Stream(rowsblk(ref), buf, sems.at[n])
            for n, (ref, buf) in enumerate(
                ((r.w_query, wq), (r.w_key, wk), (r.w_value, wv), (r.w_gate, wg)))
        ]
        s_x = Stream(lambda j: r.tokens.at[tok(j)], xs, xsem)
        for s in weights:
            s.start(0)
        s_x.start(0)

        def product(j):
            n, m = j // 2, j % 2
            slot = n % 2

            @pl.when(m == 0)
            def _():
                for s in weights:
                    s.get(n, nn)

            here = tok(m, rows // 2)
            full = pl.ds(0, width)
            res = dot(r.dgate[here, :], wg[slot], 1, 1)
            for part, w in zip(parts, (wq, wk, wv)):
                res = res + dot(part(here, full), w[slot], 1, 1)
            total[here, pl.ds(pl.multiple_of(n * 256, 256), 256)] = res

        def store(j):
            return pltpu.make_async_copy(out.at[j % 2], r.dtokens.at[tok(j)], osem.at[j % 2])

        def finish_rows(j):
            xb = s_x.get(j, blocks)
            pl.when(j >= 2)(lambda: store(j - 2).wait())

            def one(m, carry):
                here, sub = pl.ds(pl.multiple_of(j * TILE + m * 32, 32), 32), tok(m, 32)
                xv = xb[sub, :].astype(F32)
                scale = lax.rsqrt(jnp.mean(xv * xv, axis=-1, keepdims=True) + EPS)
                out[j % 2, sub, :] = r.dn2[here, :] + norm_back(total[here, :], xv, scale)
                return carry

            lax.fori_loop(0, TILE // 32, one, 0)
            store(j).start()

        def one(j):
            t = at_square + 8 + j
            move(t)
            pl.when(j < 4)(lambda: make_square(t, at_square + 8, r.at0, dq_cols))
            pl.when((j >= 4) & (j < 8))(lambda: make_square(t, at_square + 12, r.at0, dk_cols))
            pl.when(j >= 8)(lambda: make_square(t, at_square + 16, r.at0, dv_cols))
            pl.when(j < 2 * nn)(lambda: product(j))
            pl.when(j >= 2 * nn)(lambda: finish_rows(j - 2 * nn))

        steps(12, one)
        store(blocks - 2).wait()
        store(blocks - 1).wait()

    pl.run_scoped(
        segment4, *[ring((256, width), BF16)] * 4, pltpu.VMEM((rows, width), F32),
        ring((TILE, width), BF16), ring((TILE, width), F32), dma(4, 2), dma(2), dma(2))

    steps(len(stages) - 1, lambda j: move(chunks + j))


def back(args, seqs, blk):
    rows, width = args["tokens"].shape
    ff = args["first"].shape[1]
    pairs = width // (2 * HEAD)
    anywhere = pl.BlockSpec(memory_space=pl.ANY)
    cut = 4

    def v(*shape, dtype=F32):
        return pltpu.VMEM(shape, dtype)

    def sem(*shape):
        return pltpu.SemaphoreType.DMA(shape)

    n_scan = seqs * 2
    chunk = (4, 2, 2, 64, 128)
    scratch = dict(
        tbuf=v(2, *chunk), core_rx=v(LAND, *chunk), acc=v(ACC, *chunk), xa=v(LAND, 4, 2, 32, 128),
        ya=v(LAND, 4, 32, 128), yb=v(LAND, 4, 2, 16, 128), xb=v(LAND, 4, 16, 128),
        xc=v(LAND, 2, 16, 128), yc=v(LAND, 16, 128), zab=v(LAND, 2, 3, 48, 128),
        zc=v(LAND, 2, 3, 2, 2, 16, 128), fin=v(FIN, 2, 64, 128),
        ssem=sem(7, LAND), rsem=sem(7, LAND), zss=sem(2, 2, 3, LAND), zrs=sem(2, 2, 3, LAND),
        osem=sem(FIN), csem=sem(FIN), crem=sem(FIN), ygs=sem(FIN), ygr=sem(FIN),
        dyv=v(rows, width, dtype=BF16), dfs=v(2, rows, ff, dtype=BF16), dn2=v(rows, width),
        dlow=v(rows, width, dtype=BF16), dgate=v(rows, width, dtype=BF16),
        dattn=v(rows, width, dtype=BF16), at0=v(8, 2, 64, rows, dtype=BF16),
        at1=v(8, 2, 64, rows, dtype=BF16), held=v(n_scan, cut, HEAD, 128), sums=v(n_scan, cut, HEAD, 128),
        other=v(n_scan, cut, HEAD, 128), dstate=v(n_scan, cut, HEAD, 128, dtype=BF16),
        sz=sem(n_scan), rz=sem(n_scan), sx=sem(n_scan), rx=sem(n_scan),
        gacc=v(8, width), gbuf=v(8, 128), gland=v(6, 8, 128), gs=sem(6), gr=sem(6), lsem=sem(5),
    )
    args = dict(args)
    args["innert"] = args["innert"].reshape(8, ff // 8, rows)
    for name in ("normt", "norm2t", "mixedt"):
        args[name] = args[name].reshape(8, 2, 64, rows)
    args["gain"] = args["gain"].reshape(1, width)
    outs = dict(
        output=((rows, width), BF16), dtokens=((rows, width), F32), tall=((ff // 8, width), F32),
        wide=((2, width // 8, ff), F32), square=((5, width // 8, width), F32), dgain=((8, 128), F32),
    )
    return pl.pallas_call(
        functools.partial(back_kernel, blk // 2, seqs),
        out_shape=[jax.ShapeDtypeStruct(*outs[name]) for name in BACK_OUT],
        in_specs=[anywhere] * len(BACK_IN),
        out_specs=[anywhere] * len(BACK_OUT),
        scratch_shapes=[scratch[name] for name in BACK_SCRATCH],
        compiler_params=pltpu.CompilerParams(
            collective_id=3, has_side_effects=True, vmem_limit_bytes=60 * MIB),
        cost_estimate=pl.CostEstimate(flops=60 * 2**30, bytes_accessed=200 * MIB, transcendentals=0),
    )(*(args[name] for name in BACK_IN))


def rms(value):
    return lax.rsqrt(jnp.mean(value * value, axis=-1, keepdims=True) + EPS)


def forward(blk, seqs, xf, weights):
    w_query, w_key, w_value, w_gate, w_out, out_gain, w_first, w_second, w_third = weights
    normed = (xf * rms(xf)).astype(BF16)
    key = project(normed, w_key)
    value = project(normed, w_value)
    k, v = silu_parts(key)[0].astype(BF16), value.astype(BF16)
    prefix = entering(local_states(k, v, seqs), blk, False)
    query = project(normed, w_query)
    gate = project(normed, w_gate)
    q = silu_parts(query)[0].astype(BF16)
    attn = attention(q, k, v, prefix, seqs)
    mixed = (attn * rms(attn) * out_gain * silu_parts(gate)[0]).astype(BF16)
    resid = xf + project(mixed, w_out)
    normed2 = (resid * rms(resid)).astype(BF16)
    first = project(normed2, w_first)
    second = project(normed2, w_second)
    inner = (first * second).astype(BF16)
    return dict(
        normed=normed, query=query, key=key, gate=gate, q=q, k=k, v=v, prefix=prefix, attn=attn,
        mixed=mixed, resid=resid, normed2=normed2, first=first, second=second, inner=inner)


def backward_plain(blk, seqs, xf, grad_top, f, weights):
    w_query, w_key, w_value, w_gate, w_out, out_gain, w_first, w_second, w_third = weights
    output = (f["resid"] + project(f["inner"], w_third)).astype(BF16)
    grad_w3 = weight_grad(f["inner"], grad_top)
    grad_inner = back_project(grad_top, w_third)
    grad_one = (grad_inner * f["second"]).astype(BF16)
    grad_two = (grad_inner * f["first"]).astype(BF16)
    grad_w1 = weight_grad(f["normed2"], grad_one)
    grad_w2 = weight_grad(f["normed2"], grad_two)
    grad_normed2 = back_project(grad_one, w_first) + back_project(grad_two, w_second)
    resid, attn = f["resid"], f["attn"]
    grad_resid = grad_top.astype(F32) + norm_back(grad_normed2, resid, rms(resid))
    grad_resid_low = grad_resid.astype(BF16)
    grad_wo = weight_grad(f["mixed"], grad_resid_low)
    grad_mixed = back_project(grad_resid_low, w_out)
    gate_act, gate_der = silu_parts(f["gate"])
    rattn = rms(attn)
    unit_attn = attn * rattn
    grad_scaled = grad_mixed * gate_act
    grad_gate_low = (grad_mixed * (unit_attn * out_gain) * gate_der).astype(BF16)
    grad_gain = jnp.sum(grad_scaled * unit_attn, axis=0)
    grad_attn = norm_back(grad_scaled * out_gain, attn, rattn).astype(BF16)
    q, k, v, prefix = f["q"], f["k"], f["v"], f["prefix"]
    dstate = entering(local_states(q, grad_attn, seqs), blk, True)
    grad_fq, grad_fk, grad_vv = attention_back(q, k, v, grad_attn, prefix, dstate, seqs)
    grad_query_low = (grad_fq * silu_parts(f["query"])[1]).astype(BF16)
    grad_key_low = (grad_fk * silu_parts(f["key"])[1]).astype(BF16)
    grad_value_low = grad_vv.astype(BF16)
    normed = f["normed"]
    grads = [weight_grad(normed, g) for g in (grad_query_low, grad_key_low, grad_value_low, grad_gate_low)]
    grads += [grad_wo, grad_gain, grad_w1, grad_w2, grad_w3]
    grad_normed = back_project(grad_query_low, w_query) + back_project(grad_key_low, w_key)
    grad_normed = (
        grad_normed + back_project(grad_value_low, w_value) + back_project(grad_gate_low, w_gate)
    )
    grad_input = grad_resid + norm_back(grad_normed, xf, rms(xf))
    summed = [
        lax.psum(lax.psum_scatter(g, "blk", scatter_dimension=0, tiled=True), "batch") for g in grads]
    return output, grad_input, summed


WEIGHTS = (
    "w_query", "w_key", "w_value", "w_gate", "w_out", "gain", "w_first", "w_second", "w_third",
)
SAVED = (
    "inner", "first", "second", "gate", "attn", "query", "key", "q", "k", "v", "prefix",
)


def backward(blk, seqs, tokens, grad_top, f, weights):
    names = WEIGHTS
    args = dict(zip(names, weights), tokens=tokens, dy=grad_top)
    for name in SAVED:
        args[name] = f[name].astype(BF16)
    args["resid"] = f["resid"]
    args["innert"] = f["inner"].T
    args["normt"], args["norm2t"], args["mixedt"] = f["normed"].T, f["normed2"].T, f["mixed"].T
    output, grad_input, tall, wide, square, dgain = back(args, seqs, blk)
    so, sg, sq, sk, sv = (square[n] for n in range(5))
    sgain = lax.dynamic_index_in_dim(dgain, lax.axis_index("blk"), 0, False)
    return output, grad_input, [sq, sk, sv, sg, so, sgain, wide[0], wide[1], tall]


def body(sizes, tokens, cotangent, *weights):
    batch, blk = sizes
    seqs, span, width = tokens.shape
    rows = seqs * span
    low = tokens.reshape(rows, width)
    xf = low.astype(F32)
    grad_top = cotangent.reshape(rows, width)
    f = forward(blk, seqs, xf, weights)
    ff = weights[-1].shape[0]
    if (batch, blk, rows, span, width, ff % 256) == (4, 8, 1024, 128, 1024, 0):
        output, grad_input, grads = backward(blk, seqs, low, grad_top, f, weights)
    else:
        output, grad_input, grads = backward_plain(blk, seqs, xf, grad_top, f, weights)
    shape = (seqs, span, width)
    return (output.reshape(shape), grad_input.reshape(shape), *grads)


def solution(mesh):
    rows = P("batch", "blk", None)
    cut = P("blk", None)
    return jax.shard_map(
        functools.partial(body, (mesh.shape["batch"], mesh.shape["blk"])),
        mesh=mesh,
        in_specs=(rows, rows) + (P(),) * 9,
        out_specs=(rows, rows) + (cut,) * 5 + (P("blk"),) + (cut,) * 3,
        check_vma=False,
    )
```

time: 846 us -> 488 us (0.58)
  local copies, waits for them, and re-layouts: 216 us -> 34.4 us
  matrix products: 168 us -> 55.6 us
  blocking collectives: 26 us -> 0 us
  other arithmetic: 31.3 us -> 5.63 us
  Pallas kernels: 395 us -> 386 us
    dot_general x16 -> x0, matrix products: 114 us -> none  [the longest x8 57.7 us: weight_grad(): return jnp.einsum('td,tf->df', left, right, preferred_element_type=F32)]
    pallas_call x2 -> x1, Pallas kernels: 126 us -> 50.6 us  [entering(): pl.pallas_call(functools.partial(scan_kernel, blk // 2, reverse), out_sha...]
    pallas_call x2 -> x1, Pallas kernels: 245 us -> 318 us  [back(): pl.pallas_call(functools.partial(back_kernel, blk // 2, seqs), out_shape=...]
    unnamed x118 -> x39, local copies, waits for them, and re-layouts: 58.7 us -> 10.3 us
    squeeze x3, local copies, waits for them, and re-layouts: 40 us -> 6.56 us  [the longest x1 3.71 us: backward(): wide[1]]
    another operation x2 -> x0, local copies, waits for them, and re-layouts: 30.3 us -> none  [wide_chunks(): g = jnp.stack([g1, g2])]
    transpose x12 -> x3, local copies, waits for them, and re-layouts: 37.3 us -> 9.24 us  [the longest x1 4.07 us: backward(): f['mixed']]
    unnamed x1 -> x0, blocking collectives: 19.9 us -> none
where the time goes in v2:
time: 488 us; the launch traced here: 483 us
  Pallas kernels  386 us (79%)
  matrix products  55.6 us (11%)
  local copies, waits for them, and re-layouts  34.4 us (7%)
  other arithmetic  5.63 us (1%)
    pallas_call x1, Pallas kernels, back(): pl.pallas_call(functools.partial(back_kernel, blk // 2, seqs), out_shape=...  318 us
    dot_general x7, matrix products, project(): return jnp.dot(left, weight, preferred_element_type=F32)  55.6 us
    pallas_call x1, Pallas kernels, entering(): pl.pallas_call(functools.partial(scan_kernel, blk // 2, reverse), out_sha...  50.6 us
    pallas_call x1, Pallas kernels, attention(): pl.pallas_call(attn_kernel, grid=(seqs,), in_specs=[rows_spec(span, width...  11 us
    unnamed x39, local copies, waits for them, and re-layouts  10.3 us

profile of v2, /device:TPU:0, one launch (start us, length us, event | category | flops | bytes accessed | tf_op | source)
XLA Modules:
  0.0 482.9 jit_solution(9259859007377314870)
XLA Ops:
  0.7 2.2 multiply_reduce_fusion.2
  4.5 4.7 fusion.2
  9.1 3.7 convolution_convert_fusion.right_ref.v_ref.refs_11_
  12.8 6.9 %shard_map.194 = f32[8,8,64,128]{3,2,1,0:T(8,128)} custom-call(bf16[1024,1024]{1,0:T(8,128)(2,1)} %get-tuple-element.27.left_ref.k_ref.refs_10_, bf16[1024,1024]{1,0:T(8,128)(2,1)} %convolution_convert_fusion.right_ref.v_ref.refs_11_), custom_call_target="tpu_custom_call" | custom-call | tf_op jit(solution)/shard_map/pallas_call | solution.py:110
  19.8 1.6 copy-done
  21.3 50.6 %shard_map.195 = bf16[16,4,64,128]{3,2,1,0:T(8,128)(2,1)S(1)} custom-call(f32[16,4,64,128]{3,2,1,0:T(8,128)S(1)} %bitcast.49), custom_call_target="tpu_custom_call" | custom-call | tf_op jit(solution)/shard_map/pallas_call | solution.py:209
  72.0 6.7 %fusion.3 = (bf16[1024,1024]{1,0:T(8,128)(2,1)}, bf16[1024,1024]{1,0:T(8,128)(2,1)}) fusion(bf16[1024,1024]{1,0:T(8,128)(2,1)S(1)} %copy-done.5, bf16[1024,1024]{1,0:T(8,128)(2,1)} %refs_19_.1), kind=kOutput, calls=%fused_computation.25 | convolution fusion | flops 2153775104 | bytes 8388608 | tf_op jit(solution)/shard_map/dot_general | solution.py:29
  78.7 11.0 %shard_map.196 = f32[1024,1024]{1,0:T(8,128)} custom-call(bf16[1024,1024]{1,0:T(8,128)(2,1)} %get-tuple-element.29.q_ref.refs_9_, bf16[1024,1024]{1,0:T(8,128)(2,1)} %get-tuple-element.27.left_ref.k_ref.refs_10_, bf16[1024,1024]{1,0:T(8,128)(2,1)} %convolution_convert_fusion.right_ref.v_ref.refs_11_, bf16[8,8,64,128]{3,2,1,0:T(8,128)(2,1)} %bitcast.50), custom_call_target="tpu_custom_call" | custom-call | tf_op jit(solution)/shard_map/pallas_call | solution.py:122
  89.7 2.7 multiply_reduce_fusion.1
  93.2 7.7 %fusion.4 = (bf16[1024,1024]{1,0:T(8,128)(2,1)}, bf16[1024,1024]{1,0:T(8,128)(2,1)S(1)}, bf16[1024,1024]{1,0:T(8,128)(2,1)}) fusion(f32[1024,1024]{1,0:T(8,128)S(1)} %copy-done.2, f32[1024]{0:T(1024)S(1)} %copy-done.17, f32[1024]{0:T(1024)S(1)} %add_rsqrt_fusion.1, bf16[1024,1024]{1,0:T(8,128)(2,1)} %copy-done.4, bf16[1024,1024]{1,0:T(8,128)(2,1)} %refs_22_.1), kind=kOutput, calls=%fused_computation.26 | convolution fusion | flops 2157969408 | bytes 14688256 | tf_op jit(solution)/shard_map/dot_general | solution.py:29
  100.8 2.5 multiply_reduce_fusion
  103.4 2.0 copy-done.8
  105.7 2.6 copy.36
  108.3 12.5 %fusion.5 = f32[1024,2816]{1,0:T(8,128)} fusion(bf16[1024,2816]{1,0:T(8,128)(2,1)} %refs_24_.1, f32[1024,1024]{1,0:T(8,128)} %copy-done.8, f32[1024]{0:T(1024)S(1)} %add_rsqrt_fusion), kind=kOutput, calls=%fused_computation.27 | convolution fusion | flops 5907677184 | bytes 21499904 | tf_op jit(solution)/shard_map/dot_general | solution.py:29
  120.8 17.9 %fusion.1 = (bf16[1024,2816]{1,0:T(8,128)(2,1)}, bf16[1024,2816]{1,0:T(8,128)(2,1)}, bf16[1024,2816]{1,0:T(8,128)(2,1)}) fusion(f32[1024,2816]{1,0:T(8,128)} %fusion.5, bf16[1024,2816]{1,0:T(8,128)(2,1)} %refs_25_.1, f32[1024,1024]{1,0:T(8,128)S(1)} %copy-done.9, f32[1024]{0:T(1024)S(1)} %add_rsqrt_fusion), kind=kOutput, calls=%fused_computation.23 | convolution fusion | flops 5919211520 | bytes 38801408 | tf_op jit(solution)/shard_map/dot_general | solution.py:29
  138.6 8.2 %copy.33 = bf16[2816,1024]{1,0:T(8,128)(2,1)} copy(bf16[2816,1024]{0,1:T(8,128)(2,1)} %bitcast.55) | data formatting | bytes 11534336 | tf_op jit(solution)/shard_map/convert_element_type | solution.py:975
  146.9 4.1 copy.37
  151.0 2.5 copy.35
  153.5 317.5 %shard_map.197 = (bf16[1024,1024]{1,0:T(8,128)(2,1)}, f32[1024,1024]{1,0:T(8,128)}, f32[352,1024]{1,0:T(8,128)}, f32[2,128,2816]{2,1,0:T(8,128)}, f32[5,128,1024]{2,1,0:T(8,128)}, /*index=5*/f32[8,128]{1,0:T(8,128)}) custom-call(bf16[1024,1024]{1,0:T(8,128)(2,1)} %bitcast.52, bf16[1024,1024]{1,0:T(8,128)(2,1)} %bitcast.63, bf16[8,352,1024]{2,1,0:T(8,128)(2,1)} %bitcast.56, ...), custom_call_target="tpu_custom_call" | custom-call | flops 64424509440 | bytes 209715200 | tf_op jit(solution)/shard_map/pallas_call | solution.py:943
  471.0 3.7 slice_bitcast_fusion
  474.7 1.5 slice_bitcast_fusion.2
  476.3 1.3 dynamic-slice_bitcast_fusion
  477.6 1.3 copy.43
  478.9 2.0 copy.44
  (40 shorter events, 4.2 us)
Async XLA Ops:
  0.6 2.3 copy-start.3
  2.9 1.6 copy-start.14
  4.5 4.7 copy-start.4
  4.5 4.7 copy-start.15
  19.8 1.6 copy-start
  21.3 50.6 %copy-start.5 = (bf16[1024,1024]{1,0:T(8,128)(2,1)S(1)}, bf16[1024,1024]{1,0:T(8,128)(2,1)}, u32[]{:S(2)}) copy-start(bf16[1024,1024]{1,0:T(8,128)(2,1)} %copy-done.4) | copy-start | bytes 6291460
  72.0 6.7 %copy-start.1 = (bf16[16,4,64,128]{3,2,1,0:T(8,128)(2,1)}, bf16[16,4,64,128]{3,2,1,0:T(8,128)(2,1)S(1)}, u32[]{:S(2)}) copy-start(bf16[16,4,64,128]{3,2,1,0:T(8,128)(2,1)S(1)} %shard_map.195) | copy-start | bytes 3145732
  89.7 3.4 copy-start.2
  89.7 3.4 copy-start.17
  93.2 7.7 %copy-start.16 = (bf16[1024,1024]{1,0:T(8,128)(2,1)S(1)}, bf16[1024,1024]{1,0:T(8,128)(2,1)}, u32[]{:S(2)}) copy-start(bf16[1024,1024]{1,0:T(8,128)(2,1)} %refs_23_.1) | copy-start | bytes 6291460
  100.8 2.5 copy-start.12
  103.3 2.0 copy-start.8
  108.3 12.5 %copy-start.9 = (f32[1024,1024]{1,0:T(8,128)S(1)}, f32[1024,1024]{1,0:T(8,128)}, u32[]{:S(2)}) copy-start(f32[1024,1024]{1,0:T(8,128)} %copy-done.8) | copy-start | bytes 12582916
  146.9 4.1 copy-start.6
  471.0 3.7 copy-start.10
  474.7 2.9 copy-start.11
  476.3 2.7 copy-start.7
  478.9 2.4 copy-start.13

commit v3 on v2

--- a/solution.py
+++ b/solution.py
@@ -258,6 +258,352 @@
     "dgate", "dattn", "at0", "at1", "held", "sums", "other", "dstate", "sz", "rz", "sx", "rx",
     "gacc", "gbuf", "gland", "gs", "gr", "lsem",
 )
+
+
+FWD_IN = (
+    "tokens", "gain", "w_query", "w_key", "w_value", "w_gate", "w_out", "w_first", "w_second",
+)
+FWD_OUT = (
+    "k", "v", "key", "normt", "q", "gate", "query", "attn", "mixedt", "resid", "norm2t", "first",
+    "second", "inner", "innert", "prefix",
+)
+FWD_SCRATCH = (
+    "xv", "gv", "wq", "wk", "wv", "wg", "wo", "w1", "w2", "nrm", "kb", "vb", "qb", "gb", "intra",
+    "keyb", "queryb", "attnb", "mixb", "residb", "n2b", "firstb", "secondb", "innerb", "tb0", "tb1",
+    "tb2", "innertb", "held", "sums", "other", "pre", "sz", "rz", "sx", "rx", "lsem", "xsem", "osem",
+)
+
+
+def forward_kernel(outer, seqs, *refs):
+    r = Named(FWD_IN + FWD_OUT + FWD_SCRATCH, refs)
+    rows, width = r.tokens.shape
+    ff = r.w_first.shape[1]
+    span, pairs = rows // seqs, width // (2 * HEAD)
+    blocks, per_block = rows // TILE, TILE // span
+    n_scan, cut = r.sums.shape[:2]
+    per_seq = pairs // cut
+
+    k = lax.axis_index("blk")
+    z, x = k // 2, k % 2
+    top = outer - 1
+    side = {"blk": z * 2 + 1 - x}
+    above, below = {"blk": jnp.minimum(z + 1, top) * 2 + x}, {"blk": jnp.maximum(z - 1, 0) * 2 + x}
+    bar = pltpu.get_barrier_semaphore()
+    pl.semaphore_signal(bar, inc=1, device_id=side, device_id_type=MESH)
+    pl.when(z < top)(lambda: pl.semaphore_signal(bar, inc=1, device_id=above, device_id_type=MESH))
+    pl.when(z > 0)(lambda: pl.semaphore_signal(bar, inc=1, device_id=below, device_id_type=MESH))
+
+    def tok(j, n=TILE):
+        return pl.ds(pl.multiple_of(j * n, n), n)
+
+    loads = [
+        pltpu.make_async_copy(src, dst, r.lsem.at[n])
+        for n, (src, dst) in enumerate((
+            (r.w_key, r.wk), (r.w_value, r.wv), (r.w_query, r.wq), (r.w_gate, r.wg), (r.gain, r.gv),
+            (r.w_out, r.wo), (r.w_first, r.w1), (r.w_second, r.w2)))
+    ]
+
+    def x_load(j):
+        return pltpu.make_async_copy(r.tokens.at[tok(j)], r.xv.at[tok(j)], r.xsem.at[j])
+
+    by_rows = dict(
+        k=lambda j: r.kb.at[tok(j)], v=lambda j: r.vb.at[tok(j)], q=lambda j: r.qb.at[tok(j)],
+        gate=lambda j: r.gb.at[tok(j)], key=lambda j: r.keyb, query=lambda j: r.queryb,
+        attn=lambda j: r.attnb, resid=lambda j: r.residb, first=lambda j: r.firstb,
+        second=lambda j: r.secondb, inner=lambda j: r.innerb)
+    by_cols = dict(normt=r.tb0, mixedt=r.tb1, norm2t=r.tb2, innert=r.innertb)
+
+    def store(name, j):
+        sem = r.osem.at[FWD_OUT.index(name)]
+        out = getattr(r, name)
+        if name in by_rows:
+            return pltpu.make_async_copy(by_rows[name](j), out.at[tok(j)], sem)
+        return pltpu.make_async_copy(by_cols[name], out.at[:, tok(j)], sem)
+
+    def free(name, j):
+        pl.when(j > 0)(lambda: store(name, j - 1).wait())
+
+    def remote(src, dst, s, t, dev):
+        return pltpu.make_async_remote_copy(
+            src_ref=src, dst_ref=dst, send_sem=s, recv_sem=t, device_id=dev, device_id_type=MESH)
+
+    def along(i):
+        return remote(r.sums.at[i], r.held.at[i], r.sz.at[i], r.rz.at[i], above)
+
+    def across(i, src):
+        return remote(src.at[i], r.other.at[i], r.sx.at[i], r.rx.at[i], side)
+
+    def pass_on(i):
+        pl.when(z > 0)(lambda: along(i).wait_recv())
+
+        @pl.when(z == 0)
+        def _():
+            r.held[i] = jnp.zeros_like(r.held[i])
+
+        r.sums[i] = r.held[i] + r.sums[i]
+        pl.when(z < top)(lambda: along(i).start())
+        pl.when(x == 0)(lambda: across(i, r.sums).start())
+        pl.when(x == 1)(lambda: across(i, r.held).start())
+
+    def finish(i):
+        across(i, r.held).wait_recv()
+        r.pre[i] = (r.held[i] + r.other[i]).astype(BF16)
+        pl.when(z < top)(lambda: along(i).wait_send())
+        across(i, r.held).wait_send()
+
+    LAG = 2
+
+    def scan(n):
+        i = n - LAG * z
+        pl.when((i >= 0) & (i < n_scan))(lambda: pass_on(i))
+        pl.when((i >= LAG) & (i < n_scan + LAG))(lambda: finish(i - LAG))
+
+    def transposed(src, dst):
+        def one(n, carry):
+            cols = pl.ds(pl.multiple_of(n * 128, 128), 128)
+            dst[cols, :] = src[:, cols].T
+            return carry
+
+        lax.fori_loop(0, dst.shape[0] // 128, one, 0)
+
+    def norm_rows(value):
+        return (value * lax.rsqrt(jnp.mean(value * value, axis=-1, keepdims=True) + EPS)).astype(BF16)
+
+    def each(count, one):
+        def go(m, carry):
+            one(m)
+            return carry
+
+        lax.fori_loop(0, count, go, 0)
+
+    def rows_of(j, m):
+        return pl.ds(pl.multiple_of(j * TILE + m * 32, 32), 32)
+
+    def col(n):
+        return pl.ds(pl.multiple_of(n * 256, 256), 256)
+
+    def tile_keys(j):
+        x_load(j).wait()
+
+        @pl.when(j == 0)
+        def _():
+            loads[0].wait()
+            loads[1].wait()
+
+        for name in ("key", "k", "v", "normt"):
+            free(name, j)
+
+        def one(m):
+            r.nrm[rows_of(j, m), :] = norm_rows(r.xv[rows_of(j, m), :].astype(F32))
+
+        each(TILE // 32, one)
+
+        def product(n):
+            key = dot(r.nrm[tok(j), :], r.wk[:, col(n)], 1, 0)
+            r.keyb[:, col(n)] = key.astype(BF16)
+            r.kb[tok(j), col(n)] = silu_parts(key)[0].astype(BF16)
+            r.vb[tok(j), col(n)] = dot(r.nrm[tok(j), :], r.wv[:, col(n)], 1, 0).astype(BF16)
+
+        each(width // 256, product)
+
+        def states(m):
+            s = j * per_block + m
+            for p in range(pairs):
+                lanes = pl.ds(p * 2 * HEAD, 2 * HEAD)
+                here = tok(s, span)
+                r.sums[s * per_seq + p // cut, p % cut] = pick_heads(dot(r.kb[here, lanes], r.vb[here, lanes], 0, 0))
+
+        each(per_block, states)
+        transposed(r.nrm.at[tok(j)], r.tb0)
+        for name in ("key", "k", "v", "normt"):
+            store(name, j).start()
+
+    def tile_query(j):
+        @pl.when(j == 0)
+        def _():
+            loads[2].wait()
+            loads[3].wait()
+
+        for name in ("query", "q", "gate"):
+            free(name, j)
+
+        def product(n):
+            query = dot(r.nrm[tok(j), :], r.wq[:, col(n)], 1, 0)
+            r.queryb[:, col(n)] = query.astype(BF16)
+            r.qb[tok(j), col(n)] = silu_parts(query)[0].astype(BF16)
+            r.gb[tok(j), col(n)] = dot(r.nrm[tok(j), :], r.wg[:, col(n)], 1, 0).astype(BF16)
+
+        each(width // 256, product)
+        for name in ("query", "q", "gate"):
+            store(name, j).start()
+
+    def tile_scores(s):
+        causal = causal_pair(span)
+        here = tok(s, span)
+        for p in range(pairs):
+            lanes = pl.ds(p * 2 * HEAD, 2 * HEAD)
+            q, k2, v2 = r.qb[here, lanes], two_heads(r.kb[here, lanes]), two_heads(r.vb[here, lanes])
+            scores = jnp.where(causal, dot(q, k2, 1, 1), 0.0).astype(BF16)
+            r.intra[here, lanes] = dot(scores, v2, 1, 0)
+
+    def tile_mixed(j):
+        pl.when(j == 0)(lambda: loads[4].wait())
+        for name in ("attn", "mixedt"):
+            free(name, j)
+
+        def inter(m):
+            s = j * per_block + m
+            here = tok(s, span)
+            for p in range(pairs):
+                lanes = pl.ds(p * 2 * HEAD, 2 * HEAD)
+                prefix = two_heads(r.pre[s * per_seq + p // cut, p % cut])
+                r.intra[here, lanes] = r.intra[here, lanes] + dot(r.qb[here, lanes], prefix, 1, 0)
+
+        each(per_block, inter)
+
+        def one(m):
+            av = r.intra[rows_of(j, m), :]
+            scale = lax.rsqrt(jnp.mean(av * av, axis=-1, keepdims=True) + EPS)
+            act = silu_parts(r.gb[rows_of(j, m), :].astype(F32))[0]
+            r.attnb[tok(m, 32), :] = av.astype(BF16)
+            r.mixb[tok(m, 32), :] = (av * scale * r.gv[...] * act).astype(BF16)
+
+        each(TILE // 32, one)
+        transposed(r.mixb, r.tb1)
+        for name in ("attn", "mixedt"):
+            store(name, j).start()
+
+    def tile_resid(j):
+        pl.when(j == 0)(lambda: loads[5].wait())
+        for name in ("resid", "norm2t"):
+            free(name, j)
+
+        def product(n):
+            r.residb[:, col(n)] = r.xv[tok(j), col(n)].astype(F32) + dot(r.mixb[...], r.wo[:, col(n)], 1, 0)
+
+        each(width // 256, product)
+
+        def one(m):
+            r.n2b[tok(m, 32), :] = norm_rows(r.residb[tok(m, 32), :])
+
+        each(TILE // 32, one)
+        transposed(r.n2b, r.tb2)
+        for name in ("resid", "norm2t"):
+            store(name, j).start()
+
+    def tile_inner(j, lo, hi):
+        def one(n):
+            n = n + lo
+            first = dot(r.n2b[...], r.w1[:, col(n)], 1, 0)
+            second = dot(r.n2b[...], r.w2[:, col(n)], 1, 0)
+            inner = (first * second).astype(BF16)
+            r.firstb[:, col(n)] = first.astype(BF16)
+            r.secondb[:, col(n)] = second.astype(BF16)
+            r.innerb[:, col(n)] = inner
+            r.innertb[col(n), :] = inner.T
+
+        each(hi - lo, one)
+
+    def tile_up(j):
+        @pl.when(j == 0)
+        def _():
+            loads[6].wait()
+            loads[7].wait()
+
+        for name in ("first", "second", "inner", "innert"):
+            free(name, j)
+        tile_inner(j, 0, ff // 512)
+
+    def tile_up2(j):
+        tile_inner(j, ff // 512, ff // 256)
+        for name in ("first", "second", "inner", "innert"):
+            store(name, j).start()
+
+    for n in range(2):
+        x_load(n).start()
+        loads[n].start()
+    for n in range(2, blocks):
+        x_load(n).start()
+    for copy in loads[2:]:
+        copy.start()
+    pl.semaphore_wait(bar, 1 + jnp.where(z < top, 1, 0) + jnp.where(z > 0, 1, 0))
+
+    per = n_scan // blocks
+    late = (tile_mixed, tile_resid, tile_up, tile_up2)
+    n_query = 1 + per_block
+
+    def slot(n, carry):
+        pl.when(n < blocks)(lambda: tile_keys(n))
+        q = n - blocks
+
+        @pl.when((q >= 0) & (q < blocks * n_query))
+        def _():
+            j, m = q // n_query, q % n_query
+            pl.when(m == 0)(lambda: tile_query(j))
+            pl.when(m > 0)(lambda: tile_scores(j * per_block + m - 1))
+
+        scan(n)
+        w = n - LAG * z - LAG - per + 1
+        j, m = w // per, w % per
+        for step, tile in enumerate(late):
+            pl.when((w >= 0) & (j < blocks) & (m == step))(functools.partial(tile, j))
+        return carry
+
+    lax.fori_loop(0, n_scan + LAG * (top + 1) + len(late), slot, 0)
+    whole = pltpu.make_async_copy(r.pre, r.prefix, r.osem.at[FWD_OUT.index("prefix")])
+    whole.start()
+    for name in FWD_OUT[:-1]:
+        store(name, blocks - 1).wait()
+    whole.wait()
+
+
+def forward_fast(blk, seqs, tokens, weights):
+    w_query, w_key, w_value, w_gate, w_out, out_gain, w_first, w_second, w_third = weights
+    rows, width = tokens.shape
+    ff = w_first.shape[1]
+    pairs = width // (2 * HEAD)
+    cut = 2
+    n_scan = seqs * pairs // cut
+
+    def v(*shape, dtype=BF16):
+        return pltpu.VMEM(shape, dtype)
+
+    def sem(*shape):
+        return pltpu.SemaphoreType.DMA(shape)
+
+    wide, tall = (rows, width), (width, ff)
+    chunks = (n_scan, cut, HEAD, 2 * HEAD)
+    scratch = dict(
+        xv=v(*wide), gv=v(1, width, dtype=F32), wq=v(width, width), wk=v(width, width), wv=v(width, width),
+        wg=v(width, width), wo=v(width, width), w1=v(*tall), w2=v(*tall), nrm=v(*wide), kb=v(*wide),
+        vb=v(*wide), qb=v(*wide), gb=v(*wide), intra=v(*wide, dtype=F32), keyb=v(TILE, width),
+        queryb=v(TILE, width), attnb=v(TILE, width), mixb=v(TILE, width), residb=v(TILE, width, dtype=F32),
+        n2b=v(TILE, width), firstb=v(TILE, ff), secondb=v(TILE, ff), innerb=v(TILE, ff),
+        tb0=v(width, TILE), tb1=v(width, TILE), tb2=v(width, TILE), innertb=v(ff, TILE),
+        held=v(*chunks, dtype=F32), sums=v(*chunks, dtype=F32), other=v(*chunks, dtype=F32), pre=v(*chunks),
+        sz=sem(n_scan), rz=sem(n_scan), sx=sem(n_scan), rx=sem(n_scan), lsem=sem(8),
+        xsem=sem(rows // TILE), osem=sem(len(FWD_OUT)),
+    )
+    shapes = dict(
+        normt=(width, rows), mixedt=(width, rows), norm2t=(width, rows), first=(rows, ff), second=(rows, ff),
+        inner=(rows, ff), innert=(ff, rows), prefix=chunks)
+    anywhere = pl.BlockSpec(memory_space=pl.ANY)
+    outs = pl.pallas_call(
+        functools.partial(forward_kernel, blk // 2, seqs),
+        out_shape=[
+            jax.ShapeDtypeStruct(shapes.get(name, wide), F32 if name == "resid" else BF16)
+            for name in FWD_OUT
+        ],
+        in_specs=[anywhere] * len(FWD_IN),
+        out_specs=[anywhere] * len(FWD_OUT),
+        scratch_shapes=[scratch[name] for name in FWD_SCRATCH],
+        compiler_params=pltpu.CompilerParams(
+            collective_id=4, has_side_effects=True, vmem_limit_bytes=60 * MIB),
+        cost_estimate=pl.CostEstimate(flops=26 * 2**30, bytes_accessed=80 * MIB, transcendentals=0),
+    )(tokens, out_gain.reshape(1, width), w_query, w_key, w_value, w_gate, w_out, w_first, w_second)
+    f = dict(zip(FWD_OUT, outs))
+    f["prefix"] = f["prefix"].reshape(seqs, pairs, HEAD, 2 * HEAD)
+    return f
 
 
 def back_kernel(outer, seqs, *refs):
@@ -1022,19 +1368,12 @@
 WEIGHTS = (
     "w_query", "w_key", "w_value", "w_gate", "w_out", "gain", "w_first", "w_second", "w_third",
 )
-SAVED = (
-    "inner", "first", "second", "gate", "attn", "query", "key", "q", "k", "v", "prefix",
-)
 
 
 def backward(blk, seqs, tokens, grad_top, f, weights):
     names = WEIGHTS
     args = dict(zip(names, weights), tokens=tokens, dy=grad_top)
-    for name in SAVED:
-        args[name] = f[name].astype(BF16)
-    args["resid"] = f["resid"]
-    args["innert"] = f["inner"].T
-    args["normt"], args["norm2t"], args["mixedt"] = f["normed"].T, f["normed2"].T, f["mixed"].T
+    args.update(f)
     output, grad_input, tall, wide, square, dgain = back(args, seqs, blk)
     so, sg, sq, sk, sv = (square[n] for n in range(5))
     sgain = lax.dynamic_index_in_dim(dgain, lax.axis_index("blk"), 0, False)
@@ -1048,11 +1387,12 @@
     low = tokens.reshape(rows, width)
     xf = low.astype(F32)
     grad_top = cotangent.reshape(rows, width)
-    f = forward(blk, seqs, xf, weights)
     ff = weights[-1].shape[0]
     if (batch, blk, rows, span, width, ff % 256) == (4, 8, 1024, 128, 1024, 0):
+        f = forward_fast(blk, seqs, low, weights)
         output, grad_input, grads = backward(blk, seqs, low, grad_top, f, weights)
     else:
+        f = forward(blk, seqs, xf, weights)
         output, grad_input, grads = backward_plain(blk, seqs, xf, grad_top, f, weights)
     shape = (seqs, span, width)
     return (output.reshape(shape), grad_input.reshape(shape), *grads)

time: 488 us -> 432 us (0.89)
  matrix products: 55.6 us -> 0 us
  Pallas kernels: 386 us -> 418 us
  local copies, waits for them, and re-layouts: 34.4 us -> 12.9 us
  other arithmetic: 5.63 us -> 0 us
    dot_general x7 -> x0, matrix products: 55.6 us -> none  [project(): return jnp.dot(left, weight, preferred_element_type=F32)]
    pallas_call x3 -> x1, Pallas kernels: 68.5 us -> 102 us  [forward_fast(): pl.pallas_call(functools.partial(forward_kernel, blk // 2, seqs), out_sha...]
    transpose x3 -> x0, local copies, waits for them, and re-layouts: 9.24 us -> none  [the longest x1 4.07 us: backward(): f['mixed']]
    convert_element_type x1 -> x0, local copies, waits for them, and re-layouts: 8.24 us -> none  [forward(): inner = (first * second).astype(BF16)]
    reduce_sum x2 -> x0, other arithmetic: 4.9 us -> none  [rms(): return lax.rsqrt(jnp.mean(value * value, axis=-1, keepdims=True) + EPS)]
    unnamed x39 -> x11, local copies, waits for them, and re-layouts: 10.3 us -> 6.45 us
where the time goes in v3:
time: 432 us; the launch traced here: 431 us
  Pallas kernels  418 us (97%)
  local copies, waits for them, and re-layouts  12.9 us (3%)
    pallas_call x1, Pallas kernels, back(): pl.pallas_call(functools.partial(back_kernel, blk // 2, seqs), out_shape=...  316 us
    pallas_call x1, Pallas kernels, forward_fast(): pl.pallas_call(functools.partial(forward_kernel, blk // 2, seqs), out_sha...  102 us

profile of v3, /device:TPU:0, one launch (start us, length us, event | category | flops | bytes accessed | tf_op | source)
XLA Modules:
  0.0 431.5 jit_solution(11310522345151119607)
XLA Ops:
  0.6 102.1 %shard_map.194 = (bf16[1024,1024]{1,0:T(8,128)(2,1)}, bf16[1024,1024]{1,0:T(8,128)(2,1)}, bf16[1024,1024]{1,0:T(8,128)(2,1)}, bf16[1024,1024]{1,0:T(8,128)(2,1)}...) custom-call(bf16[1024,1024]{1,0:T(8,128)(2,1)} %bitcast.28, ...), custom_call_target="tpu_custom_call" | custom-call | flops 27917287424 | bytes 83886080 | tf_op jit(solution)/shard_map/pallas_call | solution.py:591
  102.8 315.7 %shard_map.195 = (bf16[1024,1024]{1,0:T(8,128)(2,1)}, f32[1024,1024]{1,0:T(8,128)}, f32[352,1024]{1,0:T(8,128)}, f32[2,128,2816]{2,1,0:T(8,128)}, f32[5,128,1024]{2,1,0:T(8,128)}, /*index=5*/f32[8,128]{1,0:T(8,128)}) custom-call(bf16[1024,1024]{1,0:T(8,128)(2,1)} %bitcast.29, bf16[1024,1024]{1,0:T(8,128)(2,1)} %bitcast.30, bf16[8,352,1024]{2,1,0:T(8,128)(2,1)} %bitcast.33, ...), custom_call_target="tpu_custom_call" | custom-call | flops 64424509440 | bytes 209715200 | tf_op jit(solution)/shard_map/pallas_call | solution.py:1289
  418.5 0.0 copy-start.1
  418.5 3.7 slice_bitcast_fusion
  422.3 0.0 copy-done.1
  422.3 0.0 copy-start.2
  422.3 1.5 slice_bitcast_fusion.2
  423.8 1.2 dynamic-slice_bitcast_fusion
  425.0 0.0 copy-done.2
  425.0 0.0 copy-start
  425.0 1.3 copy.25
  426.3 1.6 copy-done
  428.0 0.0 copy-start.3
  428.0 2.0 copy.26
  430.0 0.4 copy-done.3
  430.4 1.1 copy.27
Async XLA Ops:
  418.5 3.7 copy-start.1
  422.3 2.8 copy-start.2
  425.0 2.9 copy-start
  428.0 2.4 copy-start.3

commit v4 on v3

--- a/solution.py
+++ b/solution.py
@@ -293,8 +293,11 @@
     pl.when(z < top)(lambda: pl.semaphore_signal(bar, inc=1, device_id=above, device_id_type=MESH))
     pl.when(z > 0)(lambda: pl.semaphore_signal(bar, inc=1, device_id=below, device_id_type=MESH))
 
+    def span_of(start, size, step):
+        return pl.ds(start if isinstance(start, int) else pl.multiple_of(start, step), size)
+
     def tok(j, n=TILE):
-        return pl.ds(pl.multiple_of(j * n, n), n)
+        return span_of(j * n, n, n)
 
     loads = [
         pltpu.make_async_copy(src, dst, r.lsem.at[n])
@@ -359,28 +362,22 @@
         pl.when((i >= LAG) & (i < n_scan + LAG))(lambda: finish(i - LAG))
 
     def transposed(src, dst):
-        def one(n, carry):
-            cols = pl.ds(pl.multiple_of(n * 128, 128), 128)
+        for n in range(dst.shape[0] // 128):
+            cols = pl.ds(n * 128, 128)
             dst[cols, :] = src[:, cols].T
-            return carry
-
-        lax.fori_loop(0, dst.shape[0] // 128, one, 0)
 
     def norm_rows(value):
         return (value * lax.rsqrt(jnp.mean(value * value, axis=-1, keepdims=True) + EPS)).astype(BF16)
 
     def each(count, one):
-        def go(m, carry):
+        for m in range(count):
             one(m)
-            return carry
-
-        lax.fori_loop(0, count, go, 0)
 
     def rows_of(j, m):
-        return pl.ds(pl.multiple_of(j * TILE + m * 32, 32), 32)
+        return span_of(j * TILE + m * 32, 32, 32)
 
     def col(n):
-        return pl.ds(pl.multiple_of(n * 256, 256), 256)
+        return span_of(n * 256, 256, 256)
 
     def tile_keys(j):
         x_load(j).wait()
@@ -900,8 +897,11 @@
         pl.when((i >= 0) & (i < n_scan))(lambda: pass_on(i))
         pl.when((i >= 2) & (i < n_scan + 2))(lambda: finish(i - 2))
 
+    def span_of(start, size, step):
+        return pl.ds(start if isinstance(start, int) else pl.multiple_of(start, step), size)
+
     def tok(j, n=TILE):
-        return pl.ds(pl.multiple_of(j * n, n), n)
+        return span_of(j * n, n, n)
 
     def tile_inner(j, w3, w1, w2, first, second):
         def block(m, carry):
@@ -918,7 +918,8 @@
                 r.dn2[at_rows, to] = r.dn2[at_rows, to] + res
             return carry
 
-        lax.fori_loop(0, rows // 512, block, 0)
+        for m in range(rows // 512):
+            block(m, 0)
 
     def tile_resid(j, resid, gate, attn, q, w_out, gain, dmix):
         def one(m, carry):
@@ -931,7 +932,8 @@
             r.dlow[here, :] = out.astype(BF16)
             return carry
 
-        lax.fori_loop(0, TILE // 32, one, 0)
+        for m in range(TILE // 32):
+            one(m, 0)
         for n in range(width // 256):
             to = pl.ds(n * 256, 256)
             dmix[:, to] = dot(r.dlow[tok(j), :], w_out[to, :], 1, 1)
@@ -949,7 +951,8 @@
             r.dattn[here, :] = norm_back(ds * gain[...], av, scale).astype(BF16)
             return carry
 
-        lax.fori_loop(0, TILE // 32, two, 0)
+        for m in range(TILE // 32):
+            two(m, 0)
 
         def states(m, carry):
             s = j * (TILE // span) + m
@@ -960,7 +963,8 @@
                 r.sums[s * halves + p // per, p % per] = pick_heads(dot(q[tok(m, span), lanes], grad, 0, 0))
             return carry
 
-        lax.fori_loop(0, TILE // span, states, 0)
+        for m in range(TILE // span):
+            states(m, 0)
 
     def tile_attn(s, q_ref, k_ref, v_ref, query, key, prefix_ref):
         causal = causal_pair(span)
@@ -1224,7 +1228,8 @@
                 out[j % 2, sub, :] = r.dn2[here, :] + norm_back(total[here, :], xv, scale)
                 return carry
 
-            lax.fori_loop(0, TILE // 32, one, 0)
+            for m in range(TILE // 32):
+                one(m, 0)
             store(j).start()
 
         def one(j):

time: 432 us -> 397 us (0.919)
  Pallas kernels: 418 us -> 383 us
    pallas_call x1, Pallas kernels: 102 us -> 76.3 us  [forward_fast(): pl.pallas_call(functools.partial(forward_kernel, blk // 2, seqs), out_sha...]
    pallas_call x1, Pallas kernels: 316 us -> 307 us  [back(): pl.pallas_call(functools.partial(back_kernel, blk // 2, seqs), out_shape=...]
where the time goes in v4:
time: 397 us; the launch traced here: 396 us
  Pallas kernels  383 us (96%)
  local copies, waits for them, and re-layouts  12.9 us (3%)
    pallas_call x1, Pallas kernels, back(): pl.pallas_call(functools.partial(back_kernel, blk // 2, seqs), out_shape=...  307 us
    pallas_call x1, Pallas kernels, forward_fast(): pl.pallas_call(functools.partial(forward_kernel, blk // 2, seqs), out_sha...  76.3 us

profile of v4, /device:TPU:0, one launch (start us, length us, event | category | flops | bytes accessed | tf_op | source)
XLA Modules:
  0.0 396.4 jit_solution(5728965948647222861)
XLA Ops:
  0.6 76.3 %shard_map.194 = (bf16[1024,1024]{1,0:T(8,128)(2,1)}, bf16[1024,1024]{1,0:T(8,128)(2,1)}, bf16[1024,1024]{1,0:T(8,128)(2,1)}, bf16[1024,1024]{1,0:T(8,128)(2,1)}...) custom-call(bf16[1024,1024]{1,0:T(8,128)(2,1)} %bitcast.28, ...), custom_call_target="tpu_custom_call" | custom-call | flops 27917287424 | bytes 83886080 | tf_op jit(solution)/shard_map/pallas_call | solution.py:588
  76.9 306.6 %shard_map.195 = (bf16[1024,1024]{1,0:T(8,128)(2,1)}, f32[1024,1024]{1,0:T(8,128)}, f32[352,1024]{1,0:T(8,128)}, f32[2,128,2816]{2,1,0:T(8,128)}, f32[5,128,1024]{2,1,0:T(8,128)}, /*index=5*/f32[8,128]{1,0:T(8,128)}) custom-call(bf16[1024,1024]{1,0:T(8,128)(2,1)} %bitcast.29, bf16[1024,1024]{1,0:T(8,128)(2,1)} %bitcast.30, bf16[8,352,1024]{2,1,0:T(8,128)(2,1)} %bitcast.33, ...), custom_call_target="tpu_custom_call" | custom-call | flops 64424509440 | bytes 209715200 | tf_op jit(solution)/shard_map/pallas_call | solution.py:1294
  383.5 0.0 copy-start.1
  383.5 3.7 slice_bitcast_fusion
  387.2 0.0 copy-done.1
  387.2 0.0 copy-start.2
  387.2 1.5 slice_bitcast_fusion.2
  388.7 1.2 dynamic-slice_bitcast_fusion
  390.0 0.0 copy-done.2
  390.0 0.0 copy-start
  390.0 1.3 copy.25
  391.3 1.6 copy-done
  392.9 0.0 copy-start.3
  392.9 2.0 copy.26
  394.9 0.4 copy-done.3
  395.3 1.1 copy.27
Async XLA Ops:
  383.5 3.7 copy-start.1
  387.2 2.8 copy-start.2
  390.0 2.9 copy-start
  392.9 2.4 copy-start.3

commit v5 on v4

--- a/solution.py
+++ b/solution.py
@@ -223,6 +223,16 @@
 TILE = 256
 
 
+SPARE = (2, 18)
+
+
+class Way:
+    def __init__(self, a, b, c):
+        self.a = pl.ds(0, a) if a else None
+        self.b, self.c = pl.ds(a, b), pl.ds(a + b, c)
+        self.ab, self.top_b, self.top_c = pl.ds(0, a + b), pl.ds(0, b), pl.ds(0, c)
+
+
 class Named:
     def __init__(self, names, refs):
         self.__dict__.update(zip(names, refs))
@@ -274,6 +284,9 @@
 )
 
 
+LAG, WAIT = 1, 2
+
+
 def forward_kernel(outer, seqs, *refs):
     r = Named(FWD_IN + FWD_OUT + FWD_SCRATCH, refs)
     rows, width = r.tokens.shape
@@ -354,12 +367,10 @@
         pl.when(z < top)(lambda: along(i).wait_send())
         across(i, r.held).wait_send()
 
-    LAG = 2
-
     def scan(n):
         i = n - LAG * z
         pl.when((i >= 0) & (i < n_scan))(lambda: pass_on(i))
-        pl.when((i >= LAG) & (i < n_scan + LAG))(lambda: finish(i - LAG))
+        pl.when((i >= WAIT) & (i < n_scan + WAIT))(lambda: finish(i - WAIT))
 
     def transposed(src, dst):
         for n in range(dst.shape[0] // 128):
@@ -527,26 +538,24 @@
 
     per = n_scan // blocks
     late = (tile_mixed, tile_resid, tile_up, tile_up2)
-    n_query = 1 + per_block
 
     def slot(n, carry):
         pl.when(n < blocks)(lambda: tile_keys(n))
-        q = n - blocks
-
-        @pl.when((q >= 0) & (q < blocks * n_query))
+
+        @pl.when((n >= blocks) & (n < 2 * blocks))
         def _():
-            j, m = q // n_query, q % n_query
-            pl.when(m == 0)(lambda: tile_query(j))
-            pl.when(m > 0)(lambda: tile_scores(j * per_block + m - 1))
+            tile_query(n - blocks)
+            for m in range(per_block):
+                tile_scores((n - blocks) * per_block + m)
 
         scan(n)
-        w = n - LAG * z - LAG - per + 1
+        w = n - LAG * z - WAIT - per + 1
         j, m = w // per, w % per
         for step, tile in enumerate(late):
             pl.when((w >= 0) & (j < blocks) & (m == step))(functools.partial(tile, j))
         return carry
 
-    lax.fori_loop(0, n_scan + LAG * (top + 1) + len(late), slot, 0)
+    lax.fori_loop(0, n_scan + LAG * top + WAIT + len(late), slot, 0)
     whole = pltpu.make_async_copy(r.pre, r.prefix, r.osem.at[FWD_OUT.index("prefix")])
     whole.start()
     for name in FWD_OUT[:-1]:
@@ -559,7 +568,7 @@
     rows, width = tokens.shape
     ff = w_first.shape[1]
     pairs = width // (2 * HEAD)
-    cut = 2
+    cut = 4
     n_scan = seqs * pairs // cut
 
     def v(*shape, dtype=BF16):
@@ -640,73 +649,81 @@
     def at(i, *where):
         return r.acc.at[(i % ACC,) + where]
 
-    A, B, C = pl.ds(0, 32), pl.ds(32, 16), pl.ds(48, 16)
     every = slice(None)
 
     def core_copy(i):
         return link(CORE, i, r.tbuf.at[i % 2], r.core_rx, to_core)
 
-    def xa_copy(i):
-        return link(XA, i, at(i, every, ox, every, A), r.xa, to_x)
-
-    def ya_copy(i):
-        return link(YA, i, at(i, every, x, oy, A), r.ya, to_y)
-
-    def yb_copy(i):
-        return link(YB, i, at(i, every, every, oy, B), r.yb, to_y)
-
-    def xb_copy(i):
-        return link(XB, i, at(i, every, ox, y, B), r.xb, to_x)
-
-    def xc_copy(i):
-        return link(XC, i, at(i, z, ox, every, C), r.xc, to_x)
-
-    def yc_copy(i):
-        return link(YC, i, at(i, z, x, oy, C), r.yc, to_y)
+    def xa_copy(w, i):
+        return link(XA, i, at(i, every, ox, every, w.a), r.xa, to_x)
+
+    def ya_copy(w, i):
+        return link(YA, i, at(i, every, x, oy, w.a), r.ya, to_y)
+
+    def yb_copy(w, i):
+        return link(YB, i, at(i, every, every, oy, w.b), r.yb.at[:, :, :, w.top_b], to_y)
+
+    def xb_copy(w, i):
+        return link(XB, i, at(i, every, ox, y, w.b), r.xb.at[:, :, w.top_b], to_x)
+
+    def xc_copy(w, i):
+        return link(XC, i, at(i, z, ox, every, w.c), r.xc.at[:, :, w.top_c], to_x)
+
+    def yc_copy(w, i):
+        return link(YC, i, at(i, z, x, oy, w.c), r.yc.at[:, w.top_c], to_y)
 
     def y_share(i):
         f = i % FIN
         return remote(r.fin.at[f, y], r.fin.at[f, y], r.ygs.at[f], r.ygr.at[f], to_y)
 
-    def part_ab(i, s):
-        return at(i, s, x, y, pl.ds(0, 48))
-
-    def part_c(i, s):
-        return at(i, s, every, every, C)
-
-    AB, CC = (0, part_ab, r.zab), (1, part_c, r.zc)
-
-    def hop(group, i, n, up, s):
+    def part_ab(w, i, s):
+        return at(i, s, x, y, w.ab)
+
+    def part_c(w, i, s):
+        return at(i, s, every, every, w.c)
+
+    def land_ab(w, i, d, n):
+        return r.zab.at[i % LAND, d, n - 1, w.ab]
+
+    def land_c(w, i, d, n):
+        return r.zc.at[i % LAND, d, n - 1, :, :, w.top_c]
+
+    AB, CC = (0, part_ab, land_ab), (1, part_c, land_c)
+
+    def hop(group, w, i, n, up, s):
         g, part, land = group
         d = 0 if up else 1
         sem = (g, d, n - 1, i % LAND)
-        return remote(part(i, s), land.at[i % LAND, d, n - 1], r.zss.at[sem], r.zrs.at[sem],
+        return remote(part(w, i, s), land(w, i, d, n), r.zss.at[sem], r.zrs.at[sem],
                       to_up if up else to_down)
 
-    def z_each(group, i, n, act):
-        up = hop(group, i, n, True, jnp.minimum(outer - n + z, top))
-        down = hop(group, i, n, False, jnp.maximum(n - 1 - zr, 0))
+    def z_each(group, w, i, n, act):
+        up = hop(group, w, i, n, True, jnp.minimum(outer - n + z, top))
+        down = hop(group, w, i, n, False, jnp.maximum(n - 1 - zr, 0))
         pl.when((z <= n - 1) & (z < top))(lambda: act(up))
         pl.when((zr <= n - 1) & (z > 0))(lambda: act(down))
 
-    def z_send(group, i, n):
-        z_each(group, i, n, lambda copy: copy.start())
-
-    def z_sent(group, i, n):
-        z_each(group, i, n, lambda copy: copy.wait_send())
+    def z_send(group, w, i, n):
+        z_each(group, w, i, n, lambda copy: copy.start())
+
+    def z_sent(group, w, i, n):
+        z_each(group, w, i, n, lambda copy: copy.wait_send())
 
     def add(ref, landed):
-        ref[...] = ref[...] + landed
-
-    def z_take(group, i, n):
+        ref[...] = ref[...] + landed[...]
+
+    def z_take(group, w, i, n):
         g, part, land = group
 
         def take(up, s):
-            hop(group, i, n, up, s).wait_recv()
-            add(part(i, s), land[i % LAND, 0 if up else 1, n - 1])
+            hop(group, w, i, n, up, s).wait_recv()
+            add(part(w, i, s), land(w, i, 0 if up else 1, n))
 
         pl.when((z > 0) & (z <= n))(lambda: take(True, jnp.clip(outer - n + z - 1, 0, top)))
         pl.when((z < top) & (zr <= n))(lambda: take(False, jnp.clip(n - zr, 0, top)))
+
+    BOTH = (Way(32, 16, 16), Way(0, 56, 8))
+    spare = (at_wide + SPARE[0], at_wide + SPARE[1])
 
     def places(i, act):
         f = r.fin.at[i % FIN]
@@ -733,67 +750,72 @@
                 col = pl.multiple_of(c * (width // 2) + u * 256 + yy * 128, 128)
                 act(f.at[yy], r.square.at[m, pl.ds(h * 64, 64), pl.ds(col, 128)])
 
-    def cores(i):
+    def cores(w, i):
         core_copy(i).wait_recv()
         core_copy(i).wait_send()
-        add(at(i), r.core_rx[i % LAND])
-        xa_copy(i).start()
-        yb_copy(i).start()
-        z_send(CC, i, 1)
-
-    def second(i):
-        yb_copy(i).wait_recv()
-        add(at(i, every, every, y, B), r.yb[i % LAND])
-        xb_copy(i).start()
-        xa_copy(i).wait_recv()
-        add(at(i, every, x, every, A), r.xa[i % LAND])
-        ya_copy(i).start()
-        z_take(CC, i, 1)
-        z_send(CC, i, 2)
-        xa_copy(i).wait_send()
-        yb_copy(i).wait_send()
-        z_sent(CC, i, 1)
-
-    def third(i):
-        xb_copy(i).wait_recv()
-        add(at(i, every, x, y, B), r.xb[i % LAND])
-        ya_copy(i).wait_recv()
-        add(at(i, every, x, y, A), r.ya[i % LAND])
-        z_send(AB, i, 1)
-        z_take(CC, i, 2)
-        z_send(CC, i, 3)
-        xb_copy(i).wait_send()
-        ya_copy(i).wait_send()
-        z_sent(CC, i, 2)
-
-    def fourth(i):
-        z_take(AB, i, 1)
-        z_send(AB, i, 2)
-        z_take(CC, i, 3)
-        xc_copy(i).start()
-        z_sent(AB, i, 1)
-        z_sent(CC, i, 3)
-
-    def fifth(i):
-        z_take(AB, i, 2)
-        z_send(AB, i, 3)
-        xc_copy(i).wait_recv()
-        add(at(i, z, x, every, C), r.xc[i % LAND])
-        yc_copy(i).start()
-        z_sent(AB, i, 2)
-        xc_copy(i).wait_send()
-
-    def sixth(i):
-        yc_copy(i).wait_recv()
-        z_take(AB, i, 3)
+        add(at(i), r.core_rx.at[i % LAND])
+        if w.a is not None:
+            xa_copy(w, i).start()
+        yb_copy(w, i).start()
+        z_send(CC, w, i, 1)
+
+    def second(w, i):
+        yb_copy(w, i).wait_recv()
+        add(at(i, every, every, y, w.b), r.yb.at[i % LAND, :, :, w.top_b])
+        xb_copy(w, i).start()
+        if w.a is not None:
+            xa_copy(w, i).wait_recv()
+            add(at(i, every, x, every, w.a), r.xa.at[i % LAND])
+            ya_copy(w, i).start()
+        z_take(CC, w, i, 1)
+        z_send(CC, w, i, 2)
+        if w.a is not None:
+            xa_copy(w, i).wait_send()
+        yb_copy(w, i).wait_send()
+        z_sent(CC, w, i, 1)
+
+    def third(w, i):
+        xb_copy(w, i).wait_recv()
+        add(at(i, every, x, y, w.b), r.xb.at[i % LAND, :, w.top_b])
+        if w.a is not None:
+            ya_copy(w, i).wait_recv()
+            add(at(i, every, x, y, w.a), r.ya.at[i % LAND])
+        z_send(AB, w, i, 1)
+        z_take(CC, w, i, 2)
+        z_send(CC, w, i, 3)
+        xb_copy(w, i).wait_send()
+        if w.a is not None:
+            ya_copy(w, i).wait_send()
+        z_sent(CC, w, i, 2)
+
+    def fourth(w, i):
+        z_take(AB, w, i, 1)
+        z_send(AB, w, i, 2)
+        z_take(CC, w, i, 3)
+        xc_copy(w, i).start()
+        z_sent(AB, w, i, 1)
+        z_sent(CC, w, i, 3)
+
+    def fifth(w, i):
+        z_take(AB, w, i, 2)
+        z_send(AB, w, i, 3)
+        xc_copy(w, i).wait_recv()
+        add(at(i, z, x, every, w.c), r.xc.at[i % LAND, :, w.top_c])
+        yc_copy(w, i).start()
+        z_sent(AB, w, i, 2)
+        xc_copy(w, i).wait_send()
+
+    def sixth(w, i):
+        yc_copy(w, i).wait_recv()
+        z_take(AB, w, i, 3)
         f = i % FIN
-        r.fin[f, y, pl.ds(0, 48)] = r.acc[i % ACC, z, x, y, pl.ds(0, 48)]
-        r.fin[f, y, C] = r.acc[i % ACC, z, x, y, C] + r.yc[i % LAND]
+        r.fin[f, y, w.ab] = r.acc[i % ACC, z, x, y, w.ab]
+        r.fin[f, y, w.c] = r.acc[i % ACC, z, x, y, w.c] + r.yc[i % LAND, w.top_c]
         y_share(i).start()
-        z_sent(AB, i, 3)
-        yc_copy(i).wait_send()
-
-    def seventh(i):
+        z_sent(AB, w, i, 3)
+        yc_copy(w, i).wait_send()
+
+    def seventh(w, i):
         y_share(i).wait_recv()
         y_share(i).wait_send()
         f = i % FIN
@@ -804,7 +826,7 @@
 
         places(i, go)
 
-    def last(i):
+    def last(w, i):
         f = i % FIN
         whole = r.fin.at[f]
         copy = remote(whole, whole, r.csem.at[f], r.crem.at[f], to_core)
@@ -814,11 +836,22 @@
 
     stages = (None, cores, second, third, fourth, fifth, sixth, seventh, last)
 
-    def move(t):
-        for n, stage in enumerate(stages):
-            if stage is not None:
-                i = t - n
-                pl.when((i >= 0) & (i < chunks))(functools.partial(stage, i))
+    def advance(t, some, ways):
+        for n in some:
+            i = t - n
+            live = (i >= 0) & (i < chunks)
+            if n >= 7 or len(ways) == 1:
+                pl.when(live)(functools.partial(stages[n], ways[0], i))
+            else:
+                spared = (i >= spare[0]) & (i < spare[1])
+                pl.when(live & ~spared)(functools.partial(stages[n], ways[0], i))
+                pl.when(spared)(functools.partial(stages[n], ways[1], i))
+
+    def send_first(t, ways=BOTH):
+        advance(t, (1,), ways)
+
+    def move(t, ways=BOTH):
+        advance(t, range(2, len(stages)), ways)
 
     def make(t, fill):
         fill(1 - c, r.tbuf.at[t % 2])
@@ -866,7 +899,7 @@
     zz, xx = zr, ox
     n_scan = r.sums.shape[0]
     halves = n_scan // seqs
-    scan_at = at_wide + 1
+    scan_at = at_wide
 
     def along(i):
         return remote(r.sums.at[i], r.held.at[i], r.sz.at[i], r.rz.at[i], to_down)
@@ -1035,9 +1068,10 @@
         dy_load.wait()
 
         def one(j):
-            move(j)
+            send_first(j, BOTH[:1])
             make(j, fill_tall(s_left.get(j, n_tall)[...].reshape(8 * 32, rows)))
             tile_inner(j, *(s.get(j, n_tall) for s in tiles))
+            move(j, BOTH[:1])
 
         steps(n_tall, one)
         norm2_load.wait()
@@ -1063,11 +1097,12 @@
 
         def one(j):
             t = at_wide + j
-            move(t)
-            scan(t)
+            send_first(t)
             make_wide(t)
             rs, ga, at_, qs = (s.get(j, blocks) for s in tiles)
             tile_resid(j, rs, ga, at_, qs, w_out, gain, dmix)
+            move(t)
+            scan(t)
 
         steps(blocks, one)
 
@@ -1133,9 +1168,7 @@
 
         def one(j):
             t = at_wide + blocks + j
-            move(t)
-            scan(t)
-            gain_sum(t)
+            send_first(t)
             make_wide(t)
 
             @pl.when(j < n_out)
@@ -1150,6 +1183,10 @@
                 prod = dot(inner[j // per % 2], w[...], 1, 0)
                 out[j % 2] = (res[...] + prod).astype(BF16)
                 store(j).start()
+
+            move(t)
+            scan(t)
+            gain_sum(t)
 
         steps(n2, one)
         store(n_out - 2).wait()
@@ -1173,12 +1210,12 @@
 
         def one(j):
             t = at_square + j
-            move(t)
-            scan(t)
+            send_first(t)
             pl.when(j < 4)(lambda: make_square(t, at_square, r.at1, lambda cols: r.dlow[:, cols]))
             pl.when(j == 4)(lambda: norm_load.wait())
             pl.when(j >= 4)(lambda: make_square(t, at_square + 4, r.at0, lambda cols: r.dgate[:, cols]))
             tile_attn(j, *(s.get(j, seqs) for s in tiles))
+            move(t)
 
         steps(8, one)
 
@@ -1234,12 +1271,13 @@
 
         def one(j):
             t = at_square + 8 + j
-            move(t)
+            send_first(t, BOTH[:1])
             pl.when(j < 4)(lambda: make_square(t, at_square + 8, r.at0, dq_cols))
             pl.when((j >= 4) & (j < 8))(lambda: make_square(t, at_square + 12, r.at0, dk_cols))
             pl.when(j >= 8)(lambda: make_square(t, at_square + 16, r.at0, dv_cols))
             pl.when(j < 2 * nn)(lambda: product(j))
             pl.when(j >= 2 * nn)(lambda: finish_rows(j - 2 * nn))
+            move(t, BOTH[:1])
 
         steps(12, one)
         store(blocks - 2).wait()
@@ -1249,7 +1287,11 @@
         segment4, *[ring((256, width), BF16)] * 4, pltpu.VMEM((rows, width), F32),
         ring((TILE, width), BF16), ring((TILE, width), F32), dma(4, 2), dma(2), dma(2))
 
-    steps(len(stages) - 1, lambda j: move(chunks + j))
+    def rest(j):
+        send_first(chunks + j, BOTH[:1])
+        move(chunks + j, BOTH[:1])
+
+    steps(len(stages) - 1, rest)
 
 
 def back(args, seqs, blk):
@@ -1269,8 +1311,8 @@
     chunk = (4, 2, 2, 64, 128)
     scratch = dict(
         tbuf=v(2, *chunk), core_rx=v(LAND, *chunk), acc=v(ACC, *chunk), xa=v(LAND, 4, 2, 32, 128),
-        ya=v(LAND, 4, 32, 128), yb=v(LAND, 4, 2, 16, 128), xb=v(LAND, 4, 16, 128),
-        xc=v(LAND, 2, 16, 128), yc=v(LAND, 16, 128), zab=v(LAND, 2, 3, 48, 128),
+        ya=v(LAND, 4, 32, 128), yb=v(LAND, 4, 2, 56, 128), xb=v(LAND, 4, 56, 128),
+        xc=v(LAND, 2, 16, 128), yc=v(LAND, 16, 128), zab=v(LAND, 2, 3, 56, 128),
         zc=v(LAND, 2, 3, 2, 2, 16, 128), fin=v(FIN, 2, 64, 128),
         ssem=sem(7, LAND), rsem=sem(7, LAND), zss=sem(2, 2, 3, LAND), zrs=sem(2, 2, 3, LAND),
         osem=sem(FIN), csem=sem(FIN), crem=sem(FIN), ygs=sem(FIN), ygr=sem(FIN),

time: 397 us -> 365 us (0.919)
  Pallas kernels: 383 us -> 351 us
    pallas_call x1, Pallas kernels: 307 us -> 288 us  [back(): pl.pallas_call(functools.partial(back_kernel, blk // 2, seqs), out_shape=...]
    pallas_call x1, Pallas kernels: 76.3 us -> 63.6 us  [forward_fast(): pl.pallas_call(functools.partial(forward_kernel, blk // 2, seqs), out_sha...]
where the time goes in v5:
time: 365 us
  Pallas kernels  351 us (96%)
  local copies, waits for them, and re-layouts  12.9 us (4%)
    pallas_call x1, Pallas kernels, back(): pl.pallas_call(functools.partial(back_kernel, blk // 2, seqs), out_shape=...  288 us
    pallas_call x1, Pallas kernels, forward_fast(): pl.pallas_call(functools.partial(forward_kernel, blk // 2, seqs), out_sha...  63.6 us

profile of v5, /device:TPU:0, one launch (start us, length us, event | category | flops | bytes accessed | tf_op | source)
XLA Modules:
  0.0 364.8 jit_solution(8541845210846185085)
XLA Ops:
  0.6 63.6 %shard_map.194 = (bf16[1024,1024]{1,0:T(8,128)(2,1)}, bf16[1024,1024]{1,0:T(8,128)(2,1)}, bf16[1024,1024]{1,0:T(8,128)(2,1)}, bf16[1024,1024]{1,0:T(8,128)(2,1)}...) custom-call(bf16[1024,1024]{1,0:T(8,128)(2,1)} %bitcast.28, ...), custom_call_target="tpu_custom_call" | custom-call | flops 27917287424 | bytes 83886080 | tf_op jit(solution)/shard_map/pallas_call | solution.py:597
  64.3 287.6 %shard_map.195 = (bf16[1024,1024]{1,0:T(8,128)(2,1)}, f32[1024,1024]{1,0:T(8,128)}, f32[352,1024]{1,0:T(8,128)}, f32[2,128,2816]{2,1,0:T(8,128)}, f32[5,128,1024]{2,1,0:T(8,128)}, /*index=5*/f32[8,128]{1,0:T(8,128)}) custom-call(bf16[1024,1024]{1,0:T(8,128)(2,1)} %bitcast.29, bf16[1024,1024]{1,0:T(8,128)(2,1)} %bitcast.30, bf16[8,352,1024]{2,1,0:T(8,128)(2,1)} %bitcast.33, ...), custom_call_target="tpu_custom_call" | custom-call | flops 64424509440 | bytes 209715200 | tf_op jit(solution)/shard_map/pallas_call | solution.py:1336
  351.9 0.0 copy-start.1
  351.9 3.7 %slice_bitcast_fusion = (f32[128,2816]{1,0:T(8,128)}, f32[128,2816]{1,0:T(8,128)}) fusion(f32[2,128,2816]{2,1,0:T(8,128)} %get-tuple-element.53), kind=kLoop, calls=%fused_computation | loop fusion | bytes 5767168 | tf_op jit(solution)/shard_map/squeeze | solution.py:1427
  355.6 0.0 copy-done.1
  355.6 0.0 copy-start.2
  355.6 1.5 slice_bitcast_fusion.2
  357.1 1.2 dynamic-slice_bitcast_fusion
  358.3 0.0 copy-done.2
  358.3 0.0 copy-start
  358.3 1.3 copy.25
  359.7 1.6 copy-done
  361.3 0.0 copy-start.3
  361.3 2.0 copy.26
  363.3 0.4 copy-done.3
  363.7 1.1 copy.27
Async XLA Ops:
  351.9 3.7 %copy-start.1 = (f32[5,128,1024]{2,1,0:T(8,128)S(1)}, f32[5,128,1024]{2,1,0:T(8,128)}, u32[]{:S(2)}) copy-start(f32[5,128,1024]{2,1,0:T(8,128)} %get-tuple-element.51) | copy-start | bytes 7864324
  355.6 2.8 copy-start.2
  358.3 2.9 copy-start
  361.3 2.4 copy-start.3

commit v6 on v5

--- a/solution.py
+++ b/solution.py
@@ -284,7 +284,7 @@
 )
 
 
-LAG, WAIT = 1, 2
+LAG, WAIT, GROUP = 1, 3, 2
 
 
 def forward_kernel(outer, seqs, *refs):
@@ -368,9 +368,17 @@
         across(i, r.held).wait_send()
 
     def scan(n):
-        i = n - LAG * z
-        pl.when((i >= 0) & (i < n_scan))(lambda: pass_on(i))
-        pl.when((i >= WAIT) & (i < n_scan + WAIT))(lambda: finish(i - WAIT))
+        i = (n - LAG * z) * GROUP
+
+        @pl.when((i >= 0) & (i < n_scan))
+        def _():
+            for g in range(GROUP):
+                pass_on(i + g)
+
+        @pl.when((i >= WAIT * GROUP) & (i < n_scan + WAIT * GROUP))
+        def _():
+            for g in range(GROUP):
+                finish(i - WAIT * GROUP + g)
 
     def transposed(src, dst):
         for n in range(dst.shape[0] // 128):
@@ -454,32 +462,28 @@
             scores = jnp.where(causal, dot(q, k2, 1, 1), 0.0).astype(BF16)
             r.intra[here, lanes] = dot(scores, v2, 1, 0)
 
-    def tile_mixed(j):
-        pl.when(j == 0)(lambda: loads[4].wait())
-        for name in ("attn", "mixedt"):
-            free(name, j)
-
-        def inter(m):
-            s = j * per_block + m
-            here = tok(s, span)
-            for p in range(pairs):
-                lanes = pl.ds(p * 2 * HEAD, 2 * HEAD)
-                prefix = two_heads(r.pre[s * per_seq + p // cut, p % cut])
-                r.intra[here, lanes] = r.intra[here, lanes] + dot(r.qb[here, lanes], prefix, 1, 0)
-
-        each(per_block, inter)
-
-        def one(m):
-            av = r.intra[rows_of(j, m), :]
+    def tile_mixed(j, m):
+        if m == 0:
+            pl.when(j == 0)(lambda: loads[4].wait())
+            for name in ("attn", "mixedt"):
+                free(name, j)
+        s = j * per_block + m
+        here = tok(s, span)
+        for p in range(pairs):
+            lanes = pl.ds(p * 2 * HEAD, 2 * HEAD)
+            prefix = two_heads(r.pre[s * per_seq + p // cut, p % cut])
+            r.intra[here, lanes] = r.intra[here, lanes] + dot(r.qb[here, lanes], prefix, 1, 0)
+        for n in range(m * span // 32, (m + 1) * span // 32):
+            av = r.intra[rows_of(j, n), :]
             scale = lax.rsqrt(jnp.mean(av * av, axis=-1, keepdims=True) + EPS)
-            act = silu_parts(r.gb[rows_of(j, m), :].astype(F32))[0]
-            r.attnb[tok(m, 32), :] = av.astype(BF16)
-            r.mixb[tok(m, 32), :] = (av * scale * r.gv[...] * act).astype(BF16)
-
-        each(TILE // 32, one)
-        transposed(r.mixb, r.tb1)
-        for name in ("attn", "mixedt"):
-            store(name, j).start()
+            act = silu_parts(r.gb[rows_of(j, n), :].astype(F32))[0]
+            r.attnb[tok(n, 32), :] = av.astype(BF16)
+            r.mixb[tok(n, 32), :] = (av * scale * r.gv[...] * act).astype(BF16)
+        for n in range(width // 128):
+            r.tb1[pl.ds(n * 128, 128), tok(m, span)] = r.mixb[tok(m, span), pl.ds(n * 128, 128)].T
+        if m == per_block - 1:
+            for name in ("attn", "mixedt"):
+                store(name, j).start()
 
     def tile_resid(j):
         pl.when(j == 0)(lambda: loads[5].wait())
@@ -512,20 +516,30 @@
 
         each(hi - lo, one)
 
-    def tile_up(j):
-        @pl.when(j == 0)
-        def _():
-            loads[6].wait()
-            loads[7].wait()
-
-        for name in ("first", "second", "inner", "innert"):
-            free(name, j)
-        tile_inner(j, 0, ff // 512)
-
-    def tile_up2(j):
-        tile_inner(j, ff // 512, ff // 256)
-        for name in ("first", "second", "inner", "innert"):
-            store(name, j).start()
+    half = ff // 512 * 256
+    halves = (pl.ds(0, half), pl.ds(half, ff - half))
+
+    def up_stores(j, h):
+        cols = halves[h]
+        sem = lambda name: r.osem.at[FWD_OUT.index(name)]
+        copies = [
+            pltpu.make_async_copy(by_rows[name](j).at[:, cols], getattr(r, name).at[tok(j), cols], sem(name))
+            for name in ("first", "second", "inner")]
+        return copies + [
+            pltpu.make_async_copy(r.innertb.at[cols], r.innert.at[cols, tok(j)], sem("innert"))]
+
+    def tile_up(j, h):
+        if h == 0:
+            @pl.when(j == 0)
+            def _():
+                loads[6].wait()
+                loads[7].wait()
+
+            for name in ("first", "second", "inner", "innert"):
+                free(name, j)
+        tile_inner(j, (0, half // 256)[h], (half // 256, ff // 256)[h])
+        for copy in up_stores(j, h):
+            copy.start()
 
     for n in range(2):
         x_load(n).start()
@@ -536,8 +550,7 @@
         copy.start()
     pl.semaphore_wait(bar, 1 + jnp.where(z < top, 1, 0) + jnp.where(z > 0, 1, 0))
 
-    per = n_scan // blocks
-    late = (tile_mixed, tile_resid, tile_up, tile_up2)
+    per = n_scan // blocks // GROUP
 
     def slot(n, carry):
         pl.when(n < blocks)(lambda: tile_keys(n))
@@ -549,13 +562,21 @@
                 tile_scores((n - blocks) * per_block + m)
 
         scan(n)
-        w = n - LAG * z - WAIT - per + 1
+        w = n - LAG * z - WAIT - per // 2 + 1
         j, m = w // per, w % per
-        for step, tile in enumerate(late):
-            pl.when((w >= 0) & (j < blocks) & (m == step))(functools.partial(tile, j))
+        live = (w >= 0) & (j < blocks)
+        pl.when((w >= per) & (j <= blocks) & (m == 0))(lambda: tile_up(j - 1, 1))
+        pl.when(live & (m == 0))(lambda: tile_mixed(j, 0))
+
+        @pl.when(live & (m == 2))
+        def _():
+            tile_mixed(j, 1)
+            tile_resid(j)
+
+        pl.when(live & (m == 3))(lambda: tile_up(j, 0))
         return carry
 
-    lax.fori_loop(0, n_scan + LAG * top + WAIT + len(late), slot, 0)
+    lax.fori_loop(0, n_scan // GROUP + LAG * top + WAIT + 3, slot, 0)
     whole = pltpu.make_async_copy(r.pre, r.prefix, r.osem.at[FWD_OUT.index("prefix")])
     whole.start()
     for name in FWD_OUT[:-1]:
@@ -568,7 +589,7 @@
     rows, width = tokens.shape
     ff = w_first.shape[1]
     pairs = width // (2 * HEAD)
-    cut = 4
+    cut = 2
     n_scan = seqs * pairs // cut
 
     def v(*shape, dtype=BF16):
@@ -637,7 +658,6 @@
     bar = pltpu.get_barrier_semaphore()
     for d in peers:
         pl.semaphore_signal(bar, inc=1, device_id=d, device_id_type=MESH)
-    pl.semaphore_wait(bar, len(peers))
 
     def remote(src, dst, s, t, dev):
         return pltpu.make_async_remote_copy(
@@ -834,6 +854,7 @@
         copy.wait_recv()
         pltpu.make_async_copy(whole, whole, r.osem.at[f]).wait()
 
+    ORDER = range(2, 9)
     stages = (None, cores, second, third, fourth, fifth, sixth, seventh, last)
 
     def advance(t, some, ways):
@@ -851,7 +872,7 @@
         advance(t, (1,), ways)
 
     def move(t, ways=BOTH):
-        advance(t, range(2, len(stages)), ways)
+        advance(t, ORDER, ways)
 
     def make(t, fill):
         fill(1 - c, r.tbuf.at[t % 2])
@@ -1066,6 +1087,7 @@
         r.dn2[...] = jnp.zeros_like(r.dn2)
         r.gacc[...] = jnp.zeros_like(r.gacc)
         dy_load.wait()
+        pl.semaphore_wait(bar, len(peers))
 
         def one(j):
             send_first(j, BOTH[:1])
@@ -1417,14 +1439,57 @@
 )
 
 
+def laid_out(output, grad_input, tall, wide, square, dgain):
+    arrays = (output, grad_input, tall, wide, square, dgain)
+    squares, wides = square.shape[0], wide.shape[0]
+    shapes = [square.shape[1:]] * squares + [wide.shape[1:]] * wides + [(1, dgain.shape[1])]
+    types = [F32] * len(shapes) + [output.dtype, grad_input.dtype, F32]
+    shapes += [output.shape, grad_input.shape, tall.shape]
+    cuts = [2] * squares + [4] * wides + [1, 4, 8, 4]
+
+    def kernel(output, grad_input, tall, wide, square, dgain, *rest):
+        outs, bufs = rest[:len(shapes)], rest[len(shapes):2 * len(shapes)]
+        sem_in, sem_out = rest[2 * len(shapes):]
+        k = lax.axis_index("blk")
+        ins = [square.at[n] for n in range(squares)] + [wide.at[n] for n in range(wides)]
+        ins += [dgain.at[pl.ds(k, 1)], output, grad_input, tall]
+        loads, stores = [], []
+        for src, buf, dst, cut in zip(ins, bufs, outs, cuts):
+            step = dst.shape[0] // cut
+            for n in range(cut):
+                part = pl.ds(n * step, step)
+                m = len(loads)
+                loads.append(pltpu.make_async_copy(src.at[part], buf.at[part], sem_in.at[m]))
+                stores.append(pltpu.make_async_copy(buf.at[part], dst.at[part], sem_out.at[m]))
+        for copy in loads:
+            copy.start()
+        for load, store in zip(loads, stores):
+            load.wait()
+            store.start()
+        for copy in stores:
+            copy.wait()
+
+    anywhere = pl.BlockSpec(memory_space=pl.ANY)
+    outs = pl.pallas_call(
+        kernel,
+        out_shape=[jax.ShapeDtypeStruct(*of) for of in zip(shapes, types)],
+        in_specs=[anywhere] * len(arrays),
+        out_specs=[anywhere] * len(shapes),
+        scratch_shapes=[pltpu.VMEM(*of) for of in zip(shapes, types)]
+        + [pltpu.SemaphoreType.DMA((sum(cuts),))] * 2,
+        compiler_params=pltpu.CompilerParams(vmem_limit_bytes=60 * MIB),
+    )(*arrays)
+    return outs[:squares], outs[squares:squares + wides], *outs[squares + wides:]
+
+
 def backward(blk, seqs, tokens, grad_top, f, weights):
     names = WEIGHTS
     args = dict(zip(names, weights), tokens=tokens, dy=grad_top)
     args.update(f)
     output, grad_input, tall, wide, square, dgain = back(args, seqs, blk)
-    so, sg, sq, sk, sv = (square[n] for n in range(5))
-    sgain = lax.dynamic_index_in_dim(dgain, lax.axis_index("blk"), 0, False)
-    return output, grad_input, [sq, sk, sv, sg, so, sgain, wide[0], wide[1], tall]
+    (so, sg, sq, sk, sv), (s1, s2), sgain, output, grad_input, tall = laid_out(
+        output, grad_input, tall, wide, square, dgain)
+    return output, grad_input, [sq, sk, sv, sg, so, sgain.reshape(-1), s1, s2, tall]
 
 
 def body(sizes, tokens, cotangent, *weights):

time: 365 us -> 359 us (0.984)
  local copies, waits for them, and re-layouts: 12.9 us -> 0 us
  Pallas kernels: 351 us -> 358 us
    pallas_call x0 -> x1, Pallas kernels: none -> 10.2 us  [laid_out(): pl.pallas_call(kernel, out_shape=[jax.ShapeDtypeStruct(*of) for of in zip...]
    squeeze x3 -> x0, local copies, waits for them, and re-layouts: 6.47 us -> none  [the longest x1 3.71 us: backward(): wide[1]]
    unnamed x11 -> x0, local copies, waits for them, and re-layouts: 6.45 us -> none
where the time goes in v6:
time: 359 us
  Pallas kernels  358 us (100%)
    pallas_call x1, Pallas kernels, back(): pl.pallas_call(functools.partial(back_kernel, blk // 2, seqs), out_shape=...  285 us
    pallas_call x1, Pallas kernels, forward_fast(): pl.pallas_call(functools.partial(forward_kernel, blk // 2, seqs), out_sha...  62.9 us
    pallas_call x1, Pallas kernels, laid_out(): pl.pallas_call(kernel, out_shape=[jax.ShapeDtypeStruct(*of) for of in zip...  10.2 us

profile of v6, /device:TPU:0, one launch (start us, length us, event | category | flops | bytes accessed | tf_op | source)
XLA Modules:
  0.0 359.2 jit_solution(11348499922661615051)
XLA Ops:
  0.6 62.9 %shard_map.194 = (bf16[1024,1024]{1,0:T(8,128)(2,1)}, bf16[1024,1024]{1,0:T(8,128)(2,1)}, bf16[1024,1024]{1,0:T(8,128)(2,1)}, bf16[1024,1024]{1,0:T(8,128)(2,1)}...) custom-call(bf16[1024,1024]{1,0:T(8,128)(2,1)} %bitcast.12, ...), custom_call_target="tpu_custom_call" | custom-call | flops 27917287424 | bytes 83886080 | tf_op jit(solution)/shard_map/pallas_call | solution.py:618
  63.6 285.3 %shard_map.195 = (bf16[1024,1024]{1,0:T(8,128)(2,1)}, f32[1024,1024]{1,0:T(8,128)}, f32[352,1024]{1,0:T(8,128)}, f32[2,128,2816]{2,1,0:T(8,128)}, f32[5,128,1024]{2,1,0:T(8,128)}, /*index=5*/f32[8,128]{1,0:T(8,128)}) custom-call(bf16[1024,1024]{1,0:T(8,128)(2,1)} %bitcast.13, bf16[1024,1024]{1,0:T(8,128)(2,1)} %bitcast.14, bf16[8,352,1024]{2,1,0:T(8,128)(2,1)} %bitcast.19, ...), custom_call_target="tpu_custom_call" | custom-call | flops 64424509440 | bytes 209715200 | tf_op jit(solution)/shard_map/pallas_call | solution.py:1358
  348.8 10.2 %shard_map.196 = (f32[128,1024]{1,0:T(8,128)}, f32[128,1024]{1,0:T(8,128)}, f32[128,1024]{1,0:T(8,128)}, f32[128,1024]{1,0:T(8,128)}, f32[128,1024]{1,0:T(8,128)...) custom-call(bf16[1024,1024]{1,0:T(8,128)(2,1)} %get-tuple-element.60, ...), custom_call_target="tpu_custom_call" | custom-call | tf_op jit(solution)/shard_map/pallas_call | solution.py:1473

commit v7 on v6

--- a/solution.py
+++ b/solution.py
@@ -223,14 +223,16 @@
 TILE = 256
 
 
-SPARE = (2, 18)
+SPARE = (2, 19)
+QUICK = 2
 
 
 class Way:
     def __init__(self, a, b, c):
         self.a = pl.ds(0, a) if a else None
         self.b, self.c = pl.ds(a, b), pl.ds(a + b, c)
-        self.ab, self.top_b, self.top_c = pl.ds(0, a + b), pl.ds(0, b), pl.ds(0, c)
+        self.ab, self.top_a = pl.ds(0, a + b), pl.ds(0, max(a, 8))
+        self.top_b, self.top_c = pl.ds(0, b), pl.ds(0, c)
 
 
 class Named:
@@ -254,41 +256,11 @@
         return self.buf.at[j % 2]
 
 
-BACK_IN = (
-    "tokens", "dy", "innert", "inner", "first", "second", "resid", "gate", "attn", "q", "k", "v",
-    "query", "key", "prefix", "normt", "norm2t", "mixedt", "gain", "w_query", "w_key", "w_value",
-    "w_gate", "w_out", "w_first", "w_second", "w_third",
-)
-BACK_OUT = (
-    "output", "dtokens", "tall", "wide", "square", "dgain",
-)
-BACK_SCRATCH = (
-    "tbuf", "core_rx", "acc", "xa", "ya", "yb", "xb", "xc", "yc", "zab", "zc", "fin", "ssem",
-    "rsem", "zss", "zrs", "osem", "csem", "crem", "ygs", "ygr", "dyv", "dfs", "dn2", "dlow",
-    "dgate", "dattn", "at0", "at1", "held", "sums", "other", "dstate", "sz", "rz", "sx", "rx",
-    "gacc", "gbuf", "gland", "gs", "gr", "lsem",
-)
-
-
-FWD_IN = (
-    "tokens", "gain", "w_query", "w_key", "w_value", "w_gate", "w_out", "w_first", "w_second",
-)
-FWD_OUT = (
-    "k", "v", "key", "normt", "q", "gate", "query", "attn", "mixedt", "resid", "norm2t", "first",
-    "second", "inner", "innert", "prefix",
-)
-FWD_SCRATCH = (
-    "xv", "gv", "wq", "wk", "wv", "wg", "wo", "w1", "w2", "nrm", "kb", "vb", "qb", "gb", "intra",
-    "keyb", "queryb", "attnb", "mixb", "residb", "n2b", "firstb", "secondb", "innerb", "tb0", "tb1",
-    "tb2", "innertb", "held", "sums", "other", "pre", "sz", "rz", "sx", "rx", "lsem", "xsem", "osem",
-)
-
-
-LAG, WAIT, GROUP = 1, 3, 2
-
-
-def forward_kernel(outer, seqs, *refs):
-    r = Named(FWD_IN + FWD_OUT + FWD_SCRATCH, refs)
+LAG, WAIT, OFFER = 1, 8, (0, 1, 4, 8)
+
+
+def forward_kernel(outer, seqs, names, results, *refs):
+    r = Named(names, refs)
     rows, width = r.tokens.shape
     ff = r.w_first.shape[1]
     span, pairs = rows // seqs, width // (2 * HEAD)
@@ -330,7 +302,7 @@
     by_cols = dict(normt=r.tb0, mixedt=r.tb1, norm2t=r.tb2, innert=r.innertb)
 
     def store(name, j):
-        sem = r.osem.at[FWD_OUT.index(name)]
+        sem = r.osem.at[results.index(name)]
         out = getattr(r, name)
         if name in by_rows:
             return pltpu.make_async_copy(by_rows[name](j), out.at[tok(j)], sem)
@@ -349,36 +321,68 @@
     def across(i, src):
         return remote(src.at[i], r.other.at[i], r.sx.at[i], r.rx.at[i], side)
 
+    def owned(i):
+        return i % 2 == x
+
     def pass_on(i):
+        across(i, r.other).wait_recv()
         pl.when(z > 0)(lambda: along(i).wait_recv())
 
         @pl.when(z == 0)
         def _():
             r.held[i] = jnp.zeros_like(r.held[i])
 
-        r.sums[i] = r.held[i] + r.sums[i]
+        @pl.when(x == 0)
+        def _():
+            mine = r.held[i] + r.sums[i]
+            r.pre[i] = r.held[i].astype(BF16)
+            r.sums[i] = mine + r.other[i]
+            r.other[i] = mine
+            across(i, r.other).start()
+
+        @pl.when(x == 1)
+        def _():
+            mine = r.held[i] + r.other[i]
+            r.pre[i] = mine.astype(BF16)
+            r.sums[i] = mine + r.sums[i]
+            across(i, r.held).start()
+
         pl.when(z < top)(lambda: along(i).start())
-        pl.when(x == 0)(lambda: across(i, r.sums).start())
-        pl.when(x == 1)(lambda: across(i, r.held).start())
 
     def finish(i):
-        across(i, r.held).wait_recv()
-        r.pre[i] = (r.held[i] + r.other[i]).astype(BF16)
-        pl.when(z < top)(lambda: along(i).wait_send())
-        across(i, r.held).wait_send()
+        @pl.when(owned(i))
+        def _():
+            pl.when(z < top)(lambda: along(i).wait_send())
+
+        @pl.when(~owned(i))
+        def _():
+            across(i, r.sums).wait_recv()
+            r.pre[i] = r.other[i].astype(BF16)
+
+        across(i, r.sums).wait_send()
 
     def scan(n):
-        i = (n - LAG * z) * GROUP
+        per_tile = n_scan // blocks
+        for j in range(blocks):
+            @pl.when(n == OFFER[j])
+            def _(j=j):
+                for g in range(per_tile):
+                    i = j * per_tile + g
+                    pl.when(~owned(i))(lambda: across(i, r.sums).start())
+
+        i = (n - 1 - LAG * z) * 2
 
         @pl.when((i >= 0) & (i < n_scan))
         def _():
-            for g in range(GROUP):
-                pass_on(i + g)
-
-        @pl.when((i >= WAIT * GROUP) & (i < n_scan + WAIT * GROUP))
-        def _():
-            for g in range(GROUP):
-                finish(i - WAIT * GROUP + g)
+            for g in range(2):
+                pl.when(owned(i + g))(lambda: pass_on(i + g))
+
+        q = (n - WAIT) * 2
+
+        @pl.when((q >= 0) & (q < n_scan))
+        def _():
+            for g in range(2):
+                finish(q + g)
 
     def transposed(src, dst):
         for n in range(dst.shape[0] // 128):
@@ -405,6 +409,10 @@
         def _():
             loads[0].wait()
             loads[1].wait()
+            for n in range(1, blocks):
+                x_load(n).start()
+            for copy in loads[2:]:
+                copy.start()
 
         for name in ("key", "k", "v", "normt"):
             free(name, j)
@@ -521,7 +529,7 @@
 
     def up_stores(j, h):
         cols = halves[h]
-        sem = lambda name: r.osem.at[FWD_OUT.index(name)]
+        sem = lambda name: r.osem.at[results.index(name)]
         copies = [
             pltpu.make_async_copy(by_rows[name](j).at[:, cols], getattr(r, name).at[tok(j), cols], sem(name))
             for name in ("first", "second", "inner")]
@@ -541,19 +549,18 @@
         for copy in up_stores(j, h):
             copy.start()
 
-    for n in range(2):
-        x_load(n).start()
-        loads[n].start()
-    for n in range(2, blocks):
-        x_load(n).start()
-    for copy in loads[2:]:
-        copy.start()
-    pl.semaphore_wait(bar, 1 + jnp.where(z < top, 1, 0) + jnp.where(z > 0, 1, 0))
-
-    per = n_scan // blocks // GROUP
+    x_load(0).start()
+    loads[0].start()
+    loads[1].start()
+
+    per = n_scan // blocks // 2
 
     def slot(n, carry):
         pl.when(n < blocks)(lambda: tile_keys(n))
+
+        @pl.when(n == 0)
+        def _():
+            pl.semaphore_wait(bar, 1 + jnp.where(z < top, 1, 0) + jnp.where(z > 0, 1, 0))
 
         @pl.when((n >= blocks) & (n < 2 * blocks))
         def _():
@@ -562,7 +569,7 @@
                 tile_scores((n - blocks) * per_block + m)
 
         scan(n)
-        w = n - LAG * z - WAIT - per // 2 + 1
+        w = n - WAIT - per // 2 + 1
         j, m = w // per, w % per
         live = (w >= 0) & (j < blocks)
         pl.when((w >= per) & (j <= blocks) & (m == 0))(lambda: tile_up(j - 1, 1))
@@ -576,10 +583,10 @@
         pl.when(live & (m == 3))(lambda: tile_up(j, 0))
         return carry
 
-    lax.fori_loop(0, n_scan // GROUP + LAG * top + WAIT + 3, slot, 0)
-    whole = pltpu.make_async_copy(r.pre, r.prefix, r.osem.at[FWD_OUT.index("prefix")])
+    lax.fori_loop(0, n_scan // 2 + WAIT + 2, slot, 0)
+    whole = pltpu.make_async_copy(r.pre, r.prefix, r.osem.at[results.index("prefix")])
     whole.start()
-    for name in FWD_OUT[:-1]:
+    for name in results[:-1]:
         store(name, blocks - 1).wait()
     whole.wait()
 
@@ -609,32 +616,37 @@
         tb0=v(width, TILE), tb1=v(width, TILE), tb2=v(width, TILE), innertb=v(ff, TILE),
         held=v(*chunks, dtype=F32), sums=v(*chunks, dtype=F32), other=v(*chunks, dtype=F32), pre=v(*chunks),
         sz=sem(n_scan), rz=sem(n_scan), sx=sem(n_scan), rx=sem(n_scan), lsem=sem(8),
-        xsem=sem(rows // TILE), osem=sem(len(FWD_OUT)),
+        xsem=sem(rows // TILE), osem=sem(16),
     )
-    shapes = dict(
-        normt=(width, rows), mixedt=(width, rows), norm2t=(width, rows), first=(rows, ff), second=(rows, ff),
-        inner=(rows, ff), innert=(ff, rows), prefix=chunks)
+    turned = (width, rows)
+    outs = dict(
+        k=wide, v=wide, key=wide, normt=turned, q=wide, gate=wide, query=wide, attn=wide, mixedt=turned,
+        resid=wide, norm2t=turned, first=(rows, ff), second=(rows, ff), inner=(rows, ff),
+        innert=(ff, rows), prefix=chunks)
+    ins = dict(
+        tokens=tokens, gain=out_gain.reshape(1, width), w_query=w_query, w_key=w_key, w_value=w_value,
+        w_gate=w_gate, w_out=w_out, w_first=w_first, w_second=w_second)
+    results = tuple(outs)
     anywhere = pl.BlockSpec(memory_space=pl.ANY)
-    outs = pl.pallas_call(
-        functools.partial(forward_kernel, blk // 2, seqs),
+    made = pl.pallas_call(
+        functools.partial(forward_kernel, blk // 2, seqs, (*ins, *outs, *scratch), results),
         out_shape=[
-            jax.ShapeDtypeStruct(shapes.get(name, wide), F32 if name == "resid" else BF16)
-            for name in FWD_OUT
+            jax.ShapeDtypeStruct(shape, F32 if name == "resid" else BF16) for name, shape in outs.items()
         ],
-        in_specs=[anywhere] * len(FWD_IN),
-        out_specs=[anywhere] * len(FWD_OUT),
-        scratch_shapes=[scratch[name] for name in FWD_SCRATCH],
+        in_specs=[anywhere] * len(ins),
+        out_specs=[anywhere] * len(outs),
+        scratch_shapes=list(scratch.values()),
         compiler_params=pltpu.CompilerParams(
             collective_id=4, has_side_effects=True, vmem_limit_bytes=60 * MIB),
         cost_estimate=pl.CostEstimate(flops=26 * 2**30, bytes_accessed=80 * MIB, transcendentals=0),
-    )(tokens, out_gain.reshape(1, width), w_query, w_key, w_value, w_gate, w_out, w_first, w_second)
-    f = dict(zip(FWD_OUT, outs))
+    )(*ins.values())
+    f = dict(zip(results, made))
     f["prefix"] = f["prefix"].reshape(seqs, pairs, HEAD, 2 * HEAD)
     return f
 
 
-def back_kernel(outer, seqs, *refs):
-    r = Named(BACK_IN + BACK_OUT + BACK_SCRATCH, refs)
+def back_kernel(outer, seqs, names, *refs):
+    r = Named(names, refs)
     rows, width = r.tokens.shape
     ff = r.first.shape[1]
     span, pairs = rows // seqs, width // (2 * HEAD)
@@ -675,10 +687,10 @@
         return link(CORE, i, r.tbuf.at[i % 2], r.core_rx, to_core)
 
     def xa_copy(w, i):
-        return link(XA, i, at(i, every, ox, every, w.a), r.xa, to_x)
+        return link(XA, i, at(i, every, ox, every, w.a), r.xa.at[:, :, :, w.top_a], to_x)
 
     def ya_copy(w, i):
-        return link(YA, i, at(i, every, x, oy, w.a), r.ya, to_y)
+        return link(YA, i, at(i, every, x, oy, w.a), r.ya.at[:, :, w.top_a], to_y)
 
     def yb_copy(w, i):
         return link(YB, i, at(i, every, every, oy, w.b), r.yb.at[:, :, :, w.top_b], to_y)
@@ -742,7 +754,7 @@
         pl.when((z > 0) & (z <= n))(lambda: take(True, jnp.clip(outer - n + z - 1, 0, top)))
         pl.when((z < top) & (zr <= n))(lambda: take(False, jnp.clip(n - zr, 0, top)))
 
-    BOTH = (Way(32, 16, 16), Way(0, 56, 8))
+    BOTH = (Way(32, 16, 16), Way(0, 48, 16))
     spare = (at_wide + SPARE[0], at_wide + SPARE[1])
 
     def places(i, act):
@@ -785,7 +797,7 @@
         xb_copy(w, i).start()
         if w.a is not None:
             xa_copy(w, i).wait_recv()
-            add(at(i, every, x, every, w.a), r.xa.at[i % LAND])
+            add(at(i, every, x, every, w.a), r.xa.at[i % LAND, :, :, w.top_a])
             ya_copy(w, i).start()
         z_take(CC, w, i, 1)
         z_send(CC, w, i, 2)
@@ -799,7 +811,7 @@
         add(at(i, every, x, y, w.b), r.xb.at[i % LAND, :, w.top_b])
         if w.a is not None:
             ya_copy(w, i).wait_recv()
-            add(at(i, every, x, y, w.a), r.ya.at[i % LAND])
+            add(at(i, every, x, y, w.a), r.ya.at[i % LAND, :, w.top_a])
         z_send(AB, w, i, 1)
         z_take(CC, w, i, 2)
         z_send(CC, w, i, 3)
@@ -860,13 +872,97 @@
     def advance(t, some, ways):
         for n in some:
             i = t - n
-            live = (i >= 0) & (i < chunks)
-            if n >= 7 or len(ways) == 1:
-                pl.when(live)(functools.partial(stages[n], ways[0], i))
-            else:
+            live = (i >= 0) & (i < chunks - QUICK)
+            if n >= 7:
+                pl.when(live)(functools.partial(stages[n], None, i))
+                continue
+            if len(ways) == 2:
                 spared = (i >= spare[0]) & (i < spare[1])
-                pl.when(live & ~spared)(functools.partial(stages[n], ways[0], i))
                 pl.when(spared)(functools.partial(stages[n], ways[1], i))
+                live = live & ~spared
+            pl.when(live)(functools.partial(stages[n], ways[0], i))
+
+    def z_straight(group, i, act):
+        w = BOTH[0]
+        g, part, _ = group
+        land = (r.qab, r.qc)[g].at[i % 2]
+        for d in range(1, outer):
+            sem = (g, d - 1, i % 2)
+            act(remote(part(w, i, (z + d) % outer), land.at[d - 1], r.qss.at[sem], r.qrs.at[sem],
+                       to_z[d - 1]))
+
+    def z_arrived(group, i):
+        w = BOTH[0]
+        g, part, _ = group
+        land = (r.qab, r.qc)[g].at[i % 2]
+        z_straight(group, i, lambda copy: copy.wait_recv())
+        total = land[0]
+        for d in range(1, outer - 1):
+            total = total + land[d]
+        ref = part(w, i, z)
+        ref[...] = ref[...] + total
+        z_straight(group, i, lambda copy: copy.wait_send())
+
+    def quick_xc(i):
+        w, m = BOTH[0], i % 2
+        return remote(at(i, z, ox, every, w.c), r.qxc.at[m], r.qks.at[0, m], r.qkr.at[0, m], to_x)
+
+    def quick_yc(i):
+        w, m = BOTH[0], i % 2
+        return remote(at(i, z, x, oy, w.c), r.qyc.at[m], r.qks.at[1, m], r.qkr.at[1, m], to_y)
+
+    def quick_cores(i):
+        w = BOTH[0]
+        core_copy(i).wait_recv()
+        core_copy(i).wait_send()
+        add(at(i), r.core_rx.at[i % LAND])
+        xa_copy(w, i).start()
+        yb_copy(w, i).start()
+        z_straight(CC, i, lambda copy: copy.start())
+
+    def quick_second(i):
+        w = BOTH[0]
+        yb_copy(w, i).wait_recv()
+        add(at(i, every, every, y, w.b), r.yb.at[i % LAND, :, :, w.top_b])
+        xb_copy(w, i).start()
+        z_arrived(CC, i)
+        quick_xc(i).start()
+        xa_copy(w, i).wait_recv()
+        add(at(i, every, x, every, w.a), r.xa.at[i % LAND, :, :, w.top_a])
+        ya_copy(w, i).start()
+        xa_copy(w, i).wait_send()
+        yb_copy(w, i).wait_send()
+
+    def quick_third(i):
+        w = BOTH[0]
+        quick_xc(i).wait_recv()
+        add(at(i, z, x, every, w.c), r.qxc.at[i % 2])
+        quick_yc(i).start()
+        xb_copy(w, i).wait_recv()
+        add(at(i, every, x, y, w.b), r.xb.at[i % LAND, :, w.top_b])
+        ya_copy(w, i).wait_recv()
+        add(at(i, every, x, y, w.a), r.ya.at[i % LAND, :, w.top_a])
+        z_straight(AB, i, lambda copy: copy.start())
+        for copy in (xb_copy(w, i), ya_copy(w, i), quick_xc(i)):
+            copy.wait_send()
+
+    def quick_fourth(i):
+        w = BOTH[0]
+        quick_yc(i).wait_recv()
+        z_arrived(AB, i)
+        f = i % FIN
+        r.fin[f, y, w.ab] = r.acc[i % ACC, z, x, y, w.ab]
+        r.fin[f, y, w.c] = r.acc[i % ACC, z, x, y, w.c] + r.qyc[i % 2]
+        y_share(i).start()
+        quick_yc(i).wait_send()
+
+    quick = (None, quick_cores, quick_second, quick_third, quick_fourth,
+             functools.partial(seventh, None), functools.partial(last, None))
+
+    def finish_chunks(t, some):
+        for n in some:
+            i = t - n
+            pl.when((i >= chunks - QUICK) & (i < chunks))(functools.partial(quick[n], i))
 
     def send_first(t, ways=BOTH):
         advance(t, (1,), ways)
@@ -928,28 +1024,52 @@
     def across(i, src):
         return remote(src.at[i], r.other.at[i], r.sx.at[i], r.rx.at[i], to_x)
 
+    def owned(i):
+        return i % 2 == xx
+
     def pass_on(i):
+        across(i, r.other).wait_recv()
         pl.when(zz > 0)(lambda: along(i).wait_recv())
 
         @pl.when(zz == 0)
         def _():
             r.held[i] = jnp.zeros_like(r.held[i])
 
-        r.sums[i] = r.held[i] + r.sums[i]
+        @pl.when(xx == 0)
+        def _():
+            mine = r.held[i] + r.sums[i]
+            r.dstate[i] = r.held[i].astype(BF16)
+            r.sums[i] = mine + r.other[i]
+            r.other[i] = mine
+            across(i, r.other).start()
+
+        @pl.when(xx == 1)
+        def _():
+            mine = r.held[i] + r.other[i]
+            r.dstate[i] = mine.astype(BF16)
+            r.sums[i] = mine + r.sums[i]
+            across(i, r.held).start()
+
         pl.when(zz < top)(lambda: along(i).start())
-        pl.when(xx == 0)(lambda: across(i, r.sums).start())
-        pl.when(xx == 1)(lambda: across(i, r.held).start())
 
     def finish(i):
-        across(i, r.held).wait_recv()
-        r.dstate[i] = (r.held[i] + r.other[i]).astype(BF16)
-        pl.when(zz < top)(lambda: along(i).wait_send())
-        across(i, r.held).wait_send()
+        @pl.when(owned(i))
+        def _():
+            pl.when(zz < top)(lambda: along(i).wait_send())
+
+        @pl.when(~owned(i))
+        def _():
+            across(i, r.sums).wait_recv()
+            r.dstate[i] = r.other[i].astype(BF16)
+
+        across(i, r.sums).wait_send()
 
     def scan(t):
-        i = t - scan_at - zz
-        pl.when((i >= 0) & (i < n_scan))(lambda: pass_on(i))
-        pl.when((i >= 2) & (i < n_scan + 2))(lambda: finish(i - 2))
+        i = t - scan_at
+        pl.when((i >= 0) & (i < n_scan) & ~owned(i))(lambda: across(i, r.sums).start())
+        j = i - 1 - zz
+        pl.when((j >= 0) & (j < n_scan) & owned(j))(lambda: pass_on(j))
+        pl.when((j >= 2) & (j < n_scan + 2))(lambda: finish(j - 2))
 
     def span_of(start, size, step):
         return pl.ds(start if isinstance(start, int) else pl.multiple_of(start, step), size)
@@ -1079,14 +1199,14 @@
             Stream(cols(r.first), first, sems.at[4]),
             Stream(cols(r.second), second, sems.at[5]),
         ]
+        s_left.start(0)
         dy_load.start()
-        s_left.start(0)
+        r.dn2[...] = jnp.zeros_like(r.dn2)
+        r.gacc[...] = jnp.zeros_like(r.gacc)
+        dy_load.wait()
         for s in tiles:
             s.start(0)
         norm2_load.start()
-        r.dn2[...] = jnp.zeros_like(r.dn2)
-        r.gacc[...] = jnp.zeros_like(r.gacc)
-        dy_load.wait()
         pl.semaphore_wait(bar, len(peers))
 
         def one(j):
@@ -1294,6 +1414,7 @@
         def one(j):
             t = at_square + 8 + j
             send_first(t, BOTH[:1])
+            finish_chunks(t, (1,))
             pl.when(j < 4)(lambda: make_square(t, at_square + 8, r.at0, dq_cols))
             pl.when((j >= 4) & (j < 8))(lambda: make_square(t, at_square + 12, r.at0, dk_cols))
             pl.when(j >= 8)(lambda: make_square(t, at_square + 16, r.at0, dv_cols))
@@ -1310,10 +1431,12 @@
         ring((TILE, width), BF16), ring((TILE, width), F32), dma(4, 2), dma(2), dma(2))
 
     def rest(j):
-        send_first(chunks + j, BOTH[:1])
-        move(chunks + j, BOTH[:1])
-
-    steps(len(stages) - 1, rest)
+        t = chunks + j
+        finish_chunks(t, (1,))
+        finish_chunks(t, range(2, len(quick)))
+        move(t, BOTH[:1])
+
+    steps(len(quick) - 1, rest)
 
 
 def back(args, seqs, blk):
@@ -1345,6 +1468,8 @@
         other=v(n_scan, cut, HEAD, 128), dstate=v(n_scan, cut, HEAD, 128, dtype=BF16),
         sz=sem(n_scan), rz=sem(n_scan), sx=sem(n_scan), rx=sem(n_scan),
         gacc=v(8, width), gbuf=v(8, 128), gland=v(6, 8, 128), gs=sem(6), gr=sem(6), lsem=sem(5),
+        qab=v(2, 3, 48, 128), qc=v(2, 3, 2, 2, 16, 128), qss=sem(2, 3, 2), qrs=sem(2, 3, 2),
+        qxc=v(2, 2, 16, 128), qyc=v(2, 16, 128), qks=sem(2, 2), qkr=sem(2, 2),
     )
     args = dict(args)
     args["innert"] = args["innert"].reshape(8, ff // 8, rows)
@@ -1356,15 +1481,15 @@
         wide=((2, width // 8, ff), F32), square=((5, width // 8, width), F32), dgain=((8, 128), F32),
     )
     return pl.pallas_call(
-        functools.partial(back_kernel, blk // 2, seqs),
-        out_shape=[jax.ShapeDtypeStruct(*outs[name]) for name in BACK_OUT],
-        in_specs=[anywhere] * len(BACK_IN),
-        out_specs=[anywhere] * len(BACK_OUT),
-        scratch_shapes=[scratch[name] for name in BACK_SCRATCH],
+        functools.partial(back_kernel, blk // 2, seqs, (*args, *outs, *scratch)),
+        out_shape=[jax.ShapeDtypeStruct(*of) for of in outs.values()],
+        in_specs=[anywhere] * len(args),
+        out_specs=[anywhere] * len(outs),
+        scratch_shapes=list(scratch.values()),
         compiler_params=pltpu.CompilerParams(
             collective_id=3, has_side_effects=True, vmem_limit_bytes=60 * MIB),
         cost_estimate=pl.CostEstimate(flops=60 * 2**30, bytes_accessed=200 * MIB, transcendentals=0),
-    )(*(args[name] for name in BACK_IN))
+    )(*args.values())
 
 
 def rms(value):
@@ -1434,18 +1559,13 @@
     return output, grad_input, summed
 
 
-WEIGHTS = (
-    "w_query", "w_key", "w_value", "w_gate", "w_out", "gain", "w_first", "w_second", "w_third",
-)
-
-
 def laid_out(output, grad_input, tall, wide, square, dgain):
     arrays = (output, grad_input, tall, wide, square, dgain)
     squares, wides = square.shape[0], wide.shape[0]
     shapes = [square.shape[1:]] * squares + [wide.shape[1:]] * wides + [(1, dgain.shape[1])]
     types = [F32] * len(shapes) + [output.dtype, grad_input.dtype, F32]
     shapes += [output.shape, grad_input.shape, tall.shape]
-    cuts = [2] * squares + [4] * wides + [1, 4, 8, 4]
+    cuts = [1] * squares + [2] * wides + [1, 2, 4, 2]
 
     def kernel(output, grad_input, tall, wide, square, dgain, *rest):
         outs, bufs = rest[:len(shapes)], rest[len(shapes):2 * len(shapes)]
@@ -1483,8 +1603,10 @@
 
 
 def backward(blk, seqs, tokens, grad_top, f, weights):
-    names = WEIGHTS
-    args = dict(zip(names, weights), tokens=tokens, dy=grad_top)
+    w_query, w_key, w_value, w_gate, w_out, gain, w_first, w_second, w_third = weights
+    args = dict(
+        tokens=tokens, dy=grad_top, gain=gain, w_query=w_query, w_key=w_key, w_value=w_value,
+        w_gate=w_gate, w_out=w_out, w_first=w_first, w_second=w_second, w_third=w_third)
     args.update(f)
     output, grad_input, tall, wide, square, dgain = back(args, seqs, blk)
     (so, sg, sq, sk, sv), (s1, s2), sgain, output, grad_input, tall = laid_out(

time: 359 us -> 338 us (0.942)
  Pallas kernels: 358 us -> 337 us
    pallas_call x2, Pallas kernels: 348 us -> 327 us  [the longest x1 265 us: back(): pl.pallas_call(functools.partial(back_kernel, blk // 2, seqs, (*args, *ou...]
where the time goes in v7:
time: 338 us
  Pallas kernels  337 us (100%)
    pallas_call x1, Pallas kernels, back(): pl.pallas_call(functools.partial(back_kernel, blk // 2, seqs, (*args, *ou...  265 us
    pallas_call x1, Pallas kernels, forward_fast(): pl.pallas_call(functools.partial(forward_kernel, blk // 2, seqs, (*ins, *...  62.8 us
    pallas_call x1, Pallas kernels, laid_out(): pl.pallas_call(kernel, out_shape=[jax.ShapeDtypeStruct(*of) for of in zip...  9.56 us

profile of v7, /device:TPU:0, one launch (start us, length us, event | category | flops | bytes accessed | tf_op | source)
XLA Modules:
  0.0 337.7 jit_solution(4597679833771890485)
XLA Ops:
  0.6 62.8 %shard_map.194 = (bf16[1024,1024]{1,0:T(8,128)(2,1)}, bf16[1024,1024]{1,0:T(8,128)(2,1)}, bf16[1024,1024]{1,0:T(8,128)(2,1)}, bf16[1024,1024]{1,0:T(8,128)(2,1)}...) custom-call(bf16[1024,1024]{1,0:T(8,128)(2,1)} %bitcast.12, ...), custom_call_target="tpu_custom_call" | custom-call | flops 27917287424 | bytes 83886080 | tf_op jit(solution)/shard_map/pallas_call | solution.py:631
  63.4 264.5 %shard_map.195 = (bf16[1024,1024]{1,0:T(8,128)(2,1)}, f32[1024,1024]{1,0:T(8,128)}, f32[352,1024]{1,0:T(8,128)}, f32[2,128,2816]{2,1,0:T(8,128)}, f32[5,128,1024]{2,1,0:T(8,128)}, /*index=5*/f32[8,128]{1,0:T(8,128)}) custom-call(bf16[1024,1024]{1,0:T(8,128)(2,1)} %bitcast.13, bf16[1024,1024]{1,0:T(8,128)(2,1)} %bitcast.14, f32[1,1024]{1,0:T(1,128)} %bitcast.17, ...), custom_call_target="tpu_custom_call" | custom-call | flops 64424509440 | bytes 209715200 | tf_op jit(solution)/shard_map/pallas_call | solution.py:1483
  327.9 9.6 %shard_map.196 = (f32[128,1024]{1,0:T(8,128)}, f32[128,1024]{1,0:T(8,128)}, f32[128,1024]{1,0:T(8,128)}, f32[128,1024]{1,0:T(8,128)}, f32[128,1024]{1,0:T(8,128)...) custom-call(bf16[1024,1024]{1,0:T(8,128)(2,1)} %get-tuple-element.60, ...), custom_call_target="tpu_custom_call" | custom-call | tf_op jit(solution)/shard_map/pallas_call | solution.py:1593

commit v8 on v7

--- a/solution.py
+++ b/solution.py
@@ -414,7 +414,7 @@
             for copy in loads[2:]:
                 copy.start()
 
-        for name in ("key", "k", "v", "normt"):
+        for name in ("key", "k", "v"):
             free(name, j)
 
         def one(m):
@@ -438,8 +438,7 @@
                 r.sums[s * per_seq + p // cut, p % cut] = pick_heads(dot(r.kb[here, lanes], r.vb[here, lanes], 0, 0))
 
         each(per_block, states)
-        transposed(r.nrm.at[tok(j)], r.tb0)
-        for name in ("key", "k", "v", "normt"):
+        for name in ("key", "k", "v"):
             store(name, j).start()
 
     def tile_query(j):
@@ -448,7 +447,7 @@
             loads[2].wait()
             loads[3].wait()
 
-        for name in ("query", "q", "gate"):
+        for name in ("query", "q", "gate", "normt"):
             free(name, j)
 
         def product(n):
@@ -458,7 +457,8 @@
             r.gb[tok(j), col(n)] = dot(r.nrm[tok(j), :], r.wg[:, col(n)], 1, 0).astype(BF16)
 
         each(width // 256, product)
-        for name in ("query", "q", "gate"):
+        transposed(r.nrm.at[tok(j)], r.tb0)
+        for name in ("query", "q", "gate", "normt"):
             store(name, j).start()
 
     def tile_scores(s):
@@ -1234,13 +1234,17 @@
         g_load.start()
         for s in tiles:
             s.start(0)
-        w_load.wait()
-        g_load.wait()
 
         def one(j):
             t = at_wide + j
             send_first(t)
             make_wide(t)
+
+            @pl.when(j == 0)
+            def _():
+                w_load.wait()
+                g_load.wait()
+
             rs, ga, at_, qs = (s.get(j, blocks) for s in tiles)
             tile_resid(j, rs, ga, at_, qs, w_out, gain, dmix)
             move(t)
@@ -1363,6 +1367,12 @@
 
     pl.run_scoped(
         segment3, *[ring((span, width), BF16)] * 5, ring((pairs, HEAD, 2 * HEAD), BF16), dma(6, 2))
+
+    def rest(j):
+        t = chunks + j
+        finish_chunks(t, (1,))
+        finish_chunks(t, range(2, len(quick)))
+        move(t, BOTH[:1])
 
     def segment4(wq, wk, wv, wg, total, xs, out, sems, xsem, osem):
         nn = width // 256
@@ -1423,20 +1433,13 @@
             move(t, BOTH[:1])
 
         steps(12, one)
+        steps(len(quick) - 1, rest)
         store(blocks - 2).wait()
         store(blocks - 1).wait()
 
     pl.run_scoped(
         segment4, *[ring((256, width), BF16)] * 4, pltpu.VMEM((rows, width), F32),
         ring((TILE, width), BF16), ring((TILE, width), F32), dma(4, 2), dma(2), dma(2))
-
-    def rest(j):
-        t = chunks + j
-        finish_chunks(t, (1,))
-        finish_chunks(t, range(2, len(quick)))
-        move(t, BOTH[:1])
-
-    steps(len(quick) - 1, rest)
 
 
 def back(args, seqs, blk):

time: 338 us -> 337 us (level)
  no operation moved by 1% of the time
where the time goes in v8:
time: 337 us
  Pallas kernels  336 us (100%)
    pallas_call x1, Pallas kernels, back(): pl.pallas_call(functools.partial(back_kernel, blk // 2, seqs, (*args, *ou...  264 us
    pallas_call x1, Pallas kernels, forward_fast(): pl.pallas_call(functools.partial(forward_kernel, blk // 2, seqs, (*ins, *...  62.7 us
    pallas_call x1, Pallas kernels, laid_out(): pl.pallas_call(kernel, out_shape=[jax.ShapeDtypeStruct(*of) for of in zip...  9.56 us

profile of v8, /device:TPU:0, one launch (start us, length us, event | category | flops | bytes accessed | tf_op | source)
XLA Modules:
  0.0 336.9 jit_solution(7950117398961284034)
XLA Ops:
  0.6 62.7 %shard_map.194 = (bf16[1024,1024]{1,0:T(8,128)(2,1)}, bf16[1024,1024]{1,0:T(8,128)(2,1)}, bf16[1024,1024]{1,0:T(8,128)(2,1)}, bf16[1024,1024]{1,0:T(8,128)(2,1)}...) custom-call(bf16[1024,1024]{1,0:T(8,128)(2,1)} %bitcast.12, ...), custom_call_target="tpu_custom_call" | custom-call | flops 27917287424 | bytes 83886080 | tf_op jit(solution)/shard_map/pallas_call | solution.py:631
  63.4 263.7 %shard_map.195 = (bf16[1024,1024]{1,0:T(8,128)(2,1)}, f32[1024,1024]{1,0:T(8,128)}, f32[352,1024]{1,0:T(8,128)}, f32[2,128,2816]{2,1,0:T(8,128)}, f32[5,128,1024]{2,1,0:T(8,128)}, /*index=5*/f32[8,128]{1,0:T(8,128)}) custom-call(bf16[1024,1024]{1,0:T(8,128)(2,1)} %bitcast.13, bf16[1024,1024]{1,0:T(8,128)(2,1)} %bitcast.14, f32[1,1024]{1,0:T(1,128)} %bitcast.17, ...), custom_call_target="tpu_custom_call" | custom-call | flops 64424509440 | bytes 209715200 | tf_op jit(solution)/shard_map/pallas_call | solution.py:1486
  327.1 9.6 %shard_map.196 = (f32[128,1024]{1,0:T(8,128)}, f32[128,1024]{1,0:T(8,128)}, f32[128,1024]{1,0:T(8,128)}, f32[128,1024]{1,0:T(8,128)}, f32[128,1024]{1,0:T(8,128)...) custom-call(bf16[1024,1024]{1,0:T(8,128)(2,1)} %get-tuple-element.60, ...), custom_call_target="tpu_custom_call" | custom-call | tf_op jit(solution)/shard_map/pallas_call | solution.py:1596

commit v9 on v8

--- a/solution.py
+++ b/solution.py
@@ -1247,8 +1247,8 @@
 
             rs, ga, at_, qs = (s.get(j, blocks) for s in tiles)
             tile_resid(j, rs, ga, at_, qs, w_out, gain, dmix)
+            scan(t)
             move(t)
-            scan(t)
 
         steps(blocks, one)
 
@@ -1330,8 +1330,8 @@
                 out[j % 2] = (res[...] + prod).astype(BF16)
                 store(j).start()
 
+            scan(t)
             move(t)
-            scan(t)
             gain_sum(t)
 
         steps(n2, one)

time: 337 us -> 342 us (1.015)
  Pallas kernels: 336 us -> 341 us
    pallas_call x1, Pallas kernels: 264 us -> 268 us  [back(): pl.pallas_call(functools.partial(back_kernel, blk // 2, seqs, (*args, *ou...]
where the time goes in v9:
time: 342 us; the launch traced here: 341 us
  Pallas kernels  341 us (100%)
    pallas_call x1, Pallas kernels, back(): pl.pallas_call(functools.partial(back_kernel, blk // 2, seqs, (*args, *ou...  268 us
    pallas_call x1, Pallas kernels, forward_fast(): pl.pallas_call(functools.partial(forward_kernel, blk // 2, seqs, (*ins, *...  62.7 us
    pallas_call x1, Pallas kernels, laid_out(): pl.pallas_call(kernel, out_shape=[jax.ShapeDtypeStruct(*of) for of in zip...  9.56 us

profile of v9, /device:TPU:0, one launch (start us, length us, event | category | flops | bytes accessed | tf_op | source)
XLA Modules:
  0.0 341.4 jit_solution(10057686694319332197)
XLA Ops:
  0.6 62.7 %shard_map.194 = (bf16[1024,1024]{1,0:T(8,128)(2,1)}, bf16[1024,1024]{1,0:T(8,128)(2,1)}, bf16[1024,1024]{1,0:T(8,128)(2,1)}, bf16[1024,1024]{1,0:T(8,128)(2,1)}...) custom-call(bf16[1024,1024]{1,0:T(8,128)(2,1)} %bitcast.12, ...), custom_call_target="tpu_custom_call" | custom-call | flops 27917287424 | bytes 83886080 | tf_op jit(solution)/shard_map/pallas_call | solution.py:631
  63.4 268.2 %shard_map.195 = (bf16[1024,1024]{1,0:T(8,128)(2,1)}, f32[1024,1024]{1,0:T(8,128)}, f32[352,1024]{1,0:T(8,128)}, f32[2,128,2816]{2,1,0:T(8,128)}, f32[5,128,1024]{2,1,0:T(8,128)}, /*index=5*/f32[8,128]{1,0:T(8,128)}) custom-call(bf16[1024,1024]{1,0:T(8,128)(2,1)} %bitcast.13, bf16[1024,1024]{1,0:T(8,128)(2,1)} %bitcast.14, f32[1,1024]{1,0:T(1,128)} %bitcast.17, ...), custom_call_target="tpu_custom_call" | custom-call | flops 64424509440 | bytes 209715200 | tf_op jit(solution)/shard_map/pallas_call | solution.py:1486
  331.6 9.6 %shard_map.196 = (f32[128,1024]{1,0:T(8,128)}, f32[128,1024]{1,0:T(8,128)}, f32[128,1024]{1,0:T(8,128)}, f32[128,1024]{1,0:T(8,128)}, f32[128,1024]{1,0:T(8,128)...) custom-call(bf16[1024,1024]{1,0:T(8,128)(2,1)} %get-tuple-element.60, ...), custom_call_target="tpu_custom_call" | custom-call | tf_op jit(solution)/shard_map/pallas_call | solution.py:1596
